TPU v7x, 512 devices: a whole 4x4x16 slice. The times are simulated.
512 devices in a mesh: box: 128 (over z, x, core), rhs: 4 (over y).
Axes of the slice: x: 4, y: 4, z: 16, core: 2. Of those that a mesh axis runs over, the one named last changes fastest.
Arguments:
- charges: bfloat16 [64, 1572864], P(None, ('box', 'rhs')), may hold values from -6 to 6
- points: float32 [3, 1572864], P(None, ('box', 'rhs')), may hold values from 1 to 1.2
- leaf_basis: bfloat16 [64, 1572864], P(None, ('box', 'rhs')), may hold values from -0.5 to 0.5
- leaf_parent: int32 [512, 24], P(('box', 'rhs')), may hold values from 0 to 5, never falling along the last dimension, each value on 1 to 8 neighbouring positions
- leaf_up: bfloat16 [12288, 64, 64], P(('box', 'rhs')), may hold values from -0.375 to 0.375
- leaf_down: bfloat16 [12288, 64, 64], P(('box', 'rhs')), may hold values from -0.75 to 0.75
- box_up: bfloat16 [3072, 64, 64], P(('box', 'rhs')), may hold values from -0.3125 to 0.3125
- box_down: bfloat16 [3072, 64, 64], P(('box', 'rhs')), may hold values from -0.75 to 0.75
- top_up: bfloat16 [8, 2, 64, 64], replicated, may hold values from -0.5 to 0.5
- top_down: bfloat16 [8, 2, 64, 64], replicated, may hold values from -0.75 to 0.75
- top_coupling: bfloat16 [8, 2, 64, 64], replicated, may hold values from -0.5 to 0.5
- leaf_sources: int32 [12288, 16], P(('box', 'rhs')), may hold values from 0 to 12287, as said below
- leaf_classes: int32 [12288, 16], P(('box', 'rhs')), may hold values from 0 to 31
- leaf_coupling: bfloat16 [32, 64, 64], replicated, may hold values from -0.1875 to 0.1875
- box_sources: int32 [3072, 8], P(('box', 'rhs')), may hold values from 0 to 3071, as said below
- box_classes: int32 [3072, 8], P(('box', 'rhs')), may hold values from 0 to 31
- box_coupling: bfloat16 [32, 64, 64], replicated, may hold values from -0.25 to 0.25
- near_leaves: int32 [12288, 27], P(('box', 'rhs')), may hold values from 0 to 12287, as said below
- near_count: int32 [12288], P(('box', 'rhs')), may hold values from 1 to 27
Outputs:
- potentials: float32 [64, 1572864], P(None, ('box', 'rhs'))
Inputs may be any that keep to these rules, and one draw needn't show every extreme that they name: `leaf_parent`: within each row the entries never fall, and each of the 6 boxes is named by 1 to 8 leaves. `leaf_sources`: the 16 entries of a leaf are different leaves, never the leaf itself and never one of its near_leaves entries, of its own group or an adjacent group. `box_sources`: the 8 entries of a box are different level-one boxes, never the box itself, of its own group or an adjacent group. `near_leaves`: slot 0 of leaf t holds t; the other slots hold different leaves of the same or an adjacent group.
All inputs are finite; a program needn't handle non-finite values.
Results may differ from a plain program's by a relative error of at most 0.0065.
Values may be sent and summed in bfloat16 or wider, within the bound.
No kernel may reach another device: no remote copies, remote signals or barrier semaphores. Data moves between devices by JAX's collectives and lax.ppermute only.
A program may use at most 128 MiB of HBM per device.

v0:
```python
import math

import jax
import jax.numpy as jnp
from jax import lax
from jax.sharding import PartitionSpec as P

M = 128
NEAR = 27


delta_squared = 0.0001


def with_halo(cells, sides, width):
    for axis, dim in sides:
        count = lax.axis_size(axis)
        ends = count - 1
        head = lax.slice_in_dim(cells, 0, width, axis=dim)
        tail = lax.slice_in_dim(cells, cells.shape[dim] - width, cells.shape[dim], axis=dim)
        cells = jnp.concatenate(
            [
                lax.ppermute(tail, axis, [(i, (i + 1) % count) for i in range(ends)]),
                cells,
                lax.ppermute(head, axis, [((i + 1) % count, i) for i in range(ends)]),
            ],
            axis=dim,
        )
    return cells


def swapped(block, axis, bit):
    count = lax.axis_size(axis)
    route = []
    for low in range(count):
        high = low | 1 << bit
        if high != low and high < count:
            route += [(low, high), (high, low)]
    return lax.ppermute(block, axis, route)


def apply_matrix(vector, matrix):
    return jnp.dot(vector, matrix.astype(jnp.float32), precision=lax.Precision.HIGHEST)


def couple_level(table_ext, sources, classes, coupling, offset):
    summed = jnp.zeros((table_ext.shape[0], sources.shape[0], table_ext.shape[2]), jnp.float32)
    for column in range(sources.shape[1]):
        picked = jnp.take(table_ext, sources[:, column] - offset, axis=1)
        blocks = jnp.take(coupling, classes[:, column], axis=0)
        summed = summed + jnp.einsum(
            "rnk,nkj->rnj", picked, blocks, preferred_element_type=jnp.float32
        )
    return summed


def local(
    charges,
    points,
    leaf_basis,
    leaf_parent,
    leaf_up,
    leaf_down,
    box_up,
    box_down,
    top_up,
    top_down,
    top_coupling,
    leaf_sources,
    leaf_classes,
    leaf_coupling,
    box_sources,
    box_classes,
    box_coupling,
    near_leaves,
    near_count,
):
    row_count = charges.shape[0]
    point_count = charges.shape[1]
    leaf_count = near_count.shape[0]
    leaf_size = point_count // leaf_count
    rank_size = leaf_basis.shape[0]
    box_count = leaf_count // 4
    device = lax.axis_index(("box", "rhs"))
    charge_ext = with_halo(charges, ((("box", "rhs"), 1),), point_count)
    point_ext = with_halo(points, ((("box", "rhs"), 1),), point_count)
    grouped = charges.reshape(row_count, leaf_count, leaf_size)
    basis_grid = leaf_basis.reshape(rank_size, leaf_count, leaf_size)
    leaf_coef = jnp.einsum(
        "rlm,klm->rlk", grouped, basis_grid, preferred_element_type=jnp.float32
    ).astype(jnp.bfloat16)
    lifted = jnp.einsum("rlk,lkj->rlj", leaf_coef, leaf_up, preferred_element_type=jnp.float32)
    parents = leaf_parent[0]
    member = (parents[None, :] == jnp.arange(box_count, dtype=jnp.int32)[:, None]).astype(
        jnp.float32
    )
    box_coef = jnp.einsum("rlj,pl->rpj", lifted, member, precision=lax.Precision.HIGHEST).astype(
        jnp.bfloat16
    )
    ascent = jnp.einsum("rpk,pkj->rj", box_coef, box_up, preferred_element_type=jnp.float32)
    leaf_flat = leaf_coef.reshape(row_count, leaf_count * rank_size)
    box_flat = box_coef.reshape(row_count, box_count * rank_size)
    leaf_ext = with_halo(leaf_flat, ((("box", "rhs"), 1),), leaf_count * rank_size)
    box_ext = with_halo(box_flat, ((("box", "rhs"), 1),), box_count * rank_size)
    tier_count = lax.axis_size(("box", "rhs")).bit_length() - 1
    top_level = tier_count - 2
    fields = []
    ascents = []
    others = []
    climbing = ascent
    for height in range(top_level + 1):
        partner = swapped(climbing, ("box", "rhs"), height)
        ascents.append(climbing)
        others.append(partner)
        if height < top_level:
            parity = device >> height & 1
            left_half = jnp.where(parity == 0, climbing, partner)
            right_half = jnp.where(parity == 0, partner, climbing)
            climbing = apply_matrix(left_half, top_up[height, 0]) + apply_matrix(
                right_half, top_up[height, 1]
            )
    for height in range(top_level + 1):
        cousin, cousin_far = swapped((ascents[height], others[height]), ("box", "rhs"), height + 1)
        fields.append(
            apply_matrix(cousin, top_coupling[height, 0])
            + apply_matrix(cousin_far, top_coupling[height, 1])
        )
    descent = fields[top_level]
    for height in reversed(range(top_level)):
        parity = device >> height & 1
        descent = fields[height] + apply_matrix(descent, top_down[height, parity])
    group_local = descent.astype(jnp.bfloat16)
    leaf_grid = leaf_ext.reshape(row_count, 3 * leaf_count, rank_size)
    box_grid = box_ext.reshape(row_count, 3 * box_count, rank_size)
    leaf_field = couple_level(
        leaf_grid, leaf_sources, leaf_classes, leaf_coupling, (device - 1) * leaf_count
    )
    box_field = couple_level(
        box_grid, box_sources, box_classes, box_coupling, (device - 1) * box_count
    )
    box_local = (
        box_field
        + jnp.einsum("rj,pjk->rpk", group_local, box_down, preferred_element_type=jnp.float32)
    ).astype(jnp.bfloat16)
    parent_rows = jnp.take(box_local, parents, axis=1)
    leaf_local = (
        leaf_field
        + jnp.einsum("rlj,ljk->rlk", parent_rows, leaf_down, preferred_element_type=jnp.float32)
    ).astype(jnp.bfloat16)
    far_part = jnp.einsum(
        "rlk,klm->rlm", leaf_local, basis_grid, preferred_element_type=jnp.float32
    )
    point_grid = point_ext.reshape(3, 3 * leaf_count, leaf_size)
    own_points = points.reshape(3, leaf_count, leaf_size)
    charge_grid = charge_ext.reshape(row_count, 3 * leaf_count, leaf_size)
    near_scale = 0.5 / math.sqrt(NEAR * M)
    first_leaf = (device - 1) * leaf_count

    def slot_step(slot_index, summed):
        column = lax.dynamic_index_in_dim(near_leaves, slot_index, 1, keepdims=False) - first_leaf
        source_points = jnp.take(point_grid, column, axis=1)
        squared = jnp.zeros((leaf_count, leaf_size, leaf_size), jnp.float32)
        for axis_index in range(3):
            offset = own_points[axis_index][:, :, None] - source_points[axis_index][:, None, :]
            squared = squared + offset * offset
        kernel = jnp.where(
            slot_index < near_count[:, None, None],
            near_scale * lax.rsqrt(squared + delta_squared),
            0.0,
        ).astype(jnp.bfloat16)
        source_charges = jnp.take(charge_grid, column, axis=1)
        return summed + jnp.einsum(
            "lim,rlm->rli", kernel, source_charges, preferred_element_type=jnp.float32
        )

    slot_limit = jnp.max(near_count)
    near_part = lax.fori_loop(
        0, slot_limit, slot_step, jnp.zeros((row_count, leaf_count, leaf_size), jnp.float32)
    )
    return (near_part + far_part).reshape(row_count, point_count)


def solution(mesh):
    return jax.shard_map(
        local,
        mesh=mesh,
        in_specs=(
            P(None, ("box", "rhs")),
            P(None, ("box", "rhs")),
            P(None, ("box", "rhs")),
            P(("box", "rhs"), None),
            P(("box", "rhs"), None, None),
            P(("box", "rhs"), None, None),
            P(("box", "rhs"), None, None),
            P(("box", "rhs"), None, None),
            P(),
            P(),
            P(),
            P(("box", "rhs"), None),
            P(("box", "rhs"), None),
            P(),
            P(("box", "rhs"), None),
            P(("box", "rhs"), None),
            P(),
            P(("box", "rhs"), None),
            P(("box", "rhs")),
        ),
        out_specs=P(None, ("box", "rhs")),
        check_vma=False,
    )
```

profile of v0, /device:TPU:71, one launch (start us, length us, event | category | flops | bytes accessed | tf_op | source)
XLA Modules:
  0.0 493.8 jit_solution(15587638095973166769)
XLA Ops:
  0.0 5.3 %collective-permute-start.1 = (bf16[64,3072]{1,0:T(8,128)(2,1)}, bf16[64,3072]{1,0:T(8,128)(2,1)}, u32[]{:S(2)}, u32[]{:S(2)}) collective-permute-start(bf16[64,3072]{1,0:T(8,128)(2,1)} %param.29), channel_id=1, source_target_pairs={{1,0},{2,1},{3,2},{4,3},{5,4},{6,5},{7,6},{8,7},{9,8},{10,9},{11,1... | collective-permute-start | bytes 1179656 | tf_op jit(solution)/shard_map/ppermute | solution.py:25
  7.3 4.9 collective-permute-start.3
  62.0 11.5 %collective-permute-start.8 = (f32[64,64]{1,0:T(8,128)S(1)}, f32[64,64]{1,0:T(8,128)S(1)}, u32[]{:S(2)}, u32[]{:S(2)}) collective-permute-start(f32[64,64]{1,0:T(8,128)S(1)} %convolution_bitcast_fusion.4), channel_id=1, source_target_pairs={{0,2},{2,0},{1,3},{3,1},{4,6},{6,4},{5,7},{7,5},{8,10},{10,8},{9,1... | collective-permute-start | bytes 49160 | tf_op jit(solution)/shard_map/ppermute | solution.py:39
  100.3 8.2 %collective-permute-start.5 = (bf16[64,1536]{0,1:T(8,128)(2,1)S(1)}, bf16[64,1536]{0,1:T(8,128)(2,1)}, u32[]{:S(2)}, u32[]{:S(2)}) collective-permute-start(bf16[64,1536]{0,1:T(8,128)(2,1)S(1)} %bitcast.431), channel_id=1, source_target_pairs={{1,0},{2,1},{3,2},{4,3},{5,4},{6,5},{7,6},{8,7},{9,8},{10,9},{11,1... | collective-permute-start | bytes 589832 | tf_op jit(solution)/shard_map/ppermute | solution.py:25
  127.4 5.0 %collective-permute-start.21 = (f32[64,64]{1,0:T(8,128)S(1)}, f32[64,64]{1,0:T(8,128)S(1)}, u32[]{:S(2)}, u32[]{:S(2)}) collective-permute-start(f32[64,64]{1,0:T(8,128)S(1)} %convolution_add_fusion.29), channel_id=1, source_target_pairs={{0,16},{16,0},{1,17},{17,1},{2,18},{18,2},{3,19},{19,3},{4,20},{20... | collective-permute-start | bytes 49160 | tf_op jit(solution)/shard_map/ppermute | solution.py:39
  132.4 7.8 %collective-permute-start.20 = (f32[64,64]{1,0:T(8,128)S(1)}, f32[64,64]{1,0:T(8,128)S(1)}, u32[]{:S(2)}, u32[]{:S(2)}) collective-permute-start(f32[64,64]{1,0:T(8,128)S(1)} %convolution_add_fusion.29), channel_id=1, source_target_pairs={{0,32},{32,0},{1,33},{33,1},{2,34},{34,2},{3,35},{35,3},{4,36},{36... | collective-permute-start | bytes 49160 | tf_op jit(solution)/shard_map/ppermute | solution.py:39
  153.7 8.8 %collective-permute-start.26 = (f32[64,64]{1,0:T(8,128)S(1)}, f32[64,64]{1,0:T(8,128)S(1)}, u32[]{:S(2)}, u32[]{:S(2)}) collective-permute-start(f32[64,64]{1,0:T(8,128)S(1)} %convolution_add_fusion.25), channel_id=1, source_target_pairs={{0,128},{128,0},{1,129},{129,1},{2,130},{130,2},{3,131},{131,3},{4... | collective-permute-start | bytes 49160 | tf_op jit(solution)/shard_map/ppermute | solution.py:39
  165.2 5.8 %collective-permute-start.29 = (f32[64,64]{1,0:T(8,128)S(1)}, f32[64,64]{1,0:T(8,128)S(1)}, u32[]{:S(2)}, u32[]{:S(2)}) collective-permute-start(f32[64,64]{1,0:T(8,128)S(1)} %convolution_add_fusion.23), channel_id=1, source_target_pairs={{0,256},{256,0},{1,257},{257,1},{2,258},{258,2},{3,259},{259,3},{4... | collective-permute-start | bytes 49160 | tf_op jit(solution)/shard_map/ppermute | solution.py:39
  171.1 7.3 %collective-permute-start.30 = (f32[64,64]{1,0:T(8,128)S(1)}, f32[64,64]{1,0:T(8,128)S(1)}, u32[]{:S(2)}, u32[]{:S(2)}) collective-permute-start(f32[64,64]{1,0:T(8,128)S(1)} %convolution_add_fusion.23), channel_id=1, source_target_pairs={{0,128},{128,0},{1,129},{129,1},{2,130},{130,2},{3,131},{131,3},{4... | collective-permute-start | bytes 49160 | tf_op jit(solution)/shard_map/ppermute | solution.py:39
  181.2 6.6 %collective-permute-start.31 = (f32[64,64]{1,0:T(8,128)S(1)}, f32[64,64]{1,0:T(8,128)S(1)}, u32[]{:S(2)}, u32[]{:S(2)}) collective-permute-start(f32[64,64]{1,0:T(8,128)S(1)} %collective-permute-done.30), channel_id=1, source_target_pairs={{0,256},{256,0},{1,257},{257,1},{2,258},{258,2},{3,259},{259,3},{4... | collective-permute-start | bytes 49160 | tf_op jit(solution)/shard_map/ppermute | solution.py:39
  188.7 6.0 %collective-permute-done.31 = f32[64,64]{1,0:T(8,128)S(1)} collective-permute-done((f32[64,64]{1,0:T(8,128)S(1)}, f32[64,64]{1,0:T(8,128)S(1)}, u32[]{:S(2)}, u32[]{:S(2)}) %collective-permute-start.31) | collective-permute-done | bytes 16416 | tf_op jit(solution)/shard_map/ppermute | solution.py:39
  194.7 7.3 %collective-permute-start.28 = (f32[64,64]{1,0:T(8,128)S(1)}, f32[64,64]{1,0:T(8,128)S(1)}, u32[]{:S(2)}, u32[]{:S(2)}) collective-permute-start(f32[64,64]{1,0:T(8,128)S(1)} %collective-permute-done.27), channel_id=1, source_target_pairs={{0,128},{128,0},{1,129},{129,1},{2,130},{130,2},{3,131},{131,3},{4... | collective-permute-start | bytes 49160 | tf_op jit(solution)/shard_map/ppermute | solution.py:39
  225.7 13.7 %collective-permute-start.13 = (f32[64,64]{1,0:T(8,128)S(1)}, f32[64,64]{1,0:T(8,128)S(1)}, u32[]{:S(2)}, u32[]{:S(2)}) collective-permute-start(f32[64,64]{1,0:T(8,128)S(1)} %copy-done.42), channel_id=1, source_target_pairs={{0,4},{4,0},{1,5},{5,1},{2,6},{6,2},{3,7},{7,3},{8,12},{12,8},{9,1... | collective-permute-start | bytes 49160 | tf_op jit(solution)/shard_map/ppermute | solution.py:39
  295.6 195.2 %while.10 = (s32[]{:T(128)}, f32[64,24,128]{2,0,1:T(8,128)}, s32[]{:T(128)}, s32[24,27]{0,1:T(8,128)}, s32[]{:T(128)}, /*index=5*/bf16[64,72,128]{2,0,1:T(8,128)...) while((s32[]{:T(128)}, f32[64,24,128]{2,0,1:T(8,128)}, ...), condition=%wide.region_2.3_spmd, body=%wide.region_1.2_spmd.sunk | while | flops 55453892 | bytes 3126115 | solution.py:177
  298.5 4.4 fusion.421
  305.7 4.4 fusion.421
  320.1 4.4 fusion.421
  348.9 4.4 fusion.421
  356.1 4.4 fusion.421
  363.3 4.4 fusion.421
  377.7 4.4 fusion.421
  384.9 4.4 fusion.421
  392.1 4.4 fusion.421
  399.3 4.4 fusion.421
  406.5 4.4 fusion.421
  413.7 4.4 fusion.421
  420.9 4.4 fusion.421
  428.1 4.4 fusion.421
  442.5 4.4 fusion.421
  449.7 4.4 fusion.421
  456.9 4.4 fusion.421
  485.7 4.4 fusion.421
  (659 shorter events, 293.5 us)
Async XLA Ops:
  0.0 293.2 %collective-permute-start.1 = (bf16[64,3072]{1,0:T(8,128)(2,1)}, bf16[64,3072]{1,0:T(8,128)(2,1)}, u32[]{:S(2)}, u32[]{:S(2)}) collective-permute-start(bf16[64,3072]{1,0:T(8,128)(2,1)} %param.29), channel_id=1, source_target_pairs={{1,0},{2,1},{3,2},{4,3},{5,4},{6,5},{7,6},{8,7},{9,8},{10,9},{11,1... | collective-permute-start | bytes 1179656 | tf_op jit(solution)/shard_map/ppermute | solution.py:25
  5.4 287.8 %collective-permute-start = (bf16[64,3072]{1,0:T(8,128)(2,1)}, bf16[64,3072]{1,0:T(8,128)(2,1)}, u32[]{:S(2)}, u32[]{:S(2)}) collective-permute-start(bf16[64,3072]{1,0:T(8,128)(2,1)} %param.29), channel_id=1, source_target_pairs={{0,1},{1,2},{2,3},{3,4},{4,5},{5,6},{6,7},{7,8},{8,9},{9,10},{10,1... | collective-permute-start | bytes 1179656 | tf_op jit(solution)/shard_map/ppermute | solution.py:23
  7.3 82.9 %collective-permute-start.3 = (f32[3,3072]{1,0:T(4,128)}, f32[3,3072]{1,0:T(4,128)S(1)}, u32[]{:S(2)}, u32[]{:S(2)}) collective-permute-start(f32[3,3072]{1,0:T(4,128)} %param.30), channel_id=1, source_target_pairs={{1,0},{2,1},{3,2},{4,3},{5,4},{6,5},{7,6},{8,7},{9,8},{10,9},{11,1... | collective-permute-start | bytes 110600 | tf_op jit(solution)/shard_map/ppermute | solution.py:25
  12.2 80.0 %collective-permute-start.2 = (f32[3,3072]{1,0:T(4,128)}, f32[3,3072]{1,0:T(4,128)S(1)}, u32[]{:S(2)}, u32[]{:S(2)}) collective-permute-start(f32[3,3072]{1,0:T(4,128)} %param.30), channel_id=1, source_target_pairs={{0,1},{1,2},{2,3},{3,4},{4,5},{5,6},{6,7},{7,8},{8,9},{9,10},{10,1... | collective-permute-start | bytes 110600 | tf_op jit(solution)/shard_map/ppermute | solution.py:23
  17.0 45.1 %collective-permute-start.9 = (f32[64,64]{1,0:T(8,128)S(1)}, f32[64,64]{1,0:T(8,128)S(1)}, u32[]{:S(2)}, u32[]{:S(2)}) collective-permute-start(f32[64,64]{1,0:T(8,128)S(1)} %convolution_bitcast_fusion.4), channel_id=1, source_target_pairs={{0,1},{1,0},{2,3},{3,2},{4,5},{5,4},{6,7},{7,6},{8,9},{9,8},{10,11... | collective-permute-start | bytes 49160 | tf_op jit(solution)/shard_map/ppermute | solution.py:39
  62.0 13.2 %collective-permute-start.8 = (f32[64,64]{1,0:T(8,128)S(1)}, f32[64,64]{1,0:T(8,128)S(1)}, u32[]{:S(2)}, u32[]{:S(2)}) collective-permute-start(f32[64,64]{1,0:T(8,128)S(1)} %convolution_bitcast_fusion.4), channel_id=1, source_target_pairs={{0,2},{2,0},{1,3},{3,1},{4,6},{6,4},{5,7},{7,5},{8,10},{10,8},{9,1... | collective-permute-start | bytes 49160 | tf_op jit(solution)/shard_map/ppermute | solution.py:39
  75.2 6.2 %collective-permute-start.12 = (f32[64,64]{1,0:T(8,128)S(1)}, f32[64,64]{1,0:T(8,128)S(1)}, u32[]{:S(2)}, u32[]{:S(2)}) collective-permute-start(f32[64,64]{1,0:T(8,128)S(1)} %convolution_add_fusion.35), channel_id=1, source_target_pairs={{0,2},{2,0},{1,3},{3,1},{4,6},{6,4},{5,7},{7,5},{8,10},{10,8},{9,1... | collective-permute-start | bytes 49160 | tf_op jit(solution)/shard_map/ppermute | solution.py:39
  81.4 3.7 collective-permute-start.11
  85.1 25.0 %collective-permute-start.7 = (bf16[64,384]{1,0:T(8,128)(2,1)S(1)}, bf16[64,384]{1,0:T(8,128)(2,1)S(1)}, u32[]{:S(2)}, u32[]{:S(2)}) collective-permute-start(bf16[64,384]{1,0:T(8,128)(2,1)S(1)} %reshape.156), channel_id=1, source_target_pairs={{1,0},{2,1},{3,2},{4,3},{5,4},{6,5},{7,6},{8,7},{9,8},{10,9},{11,1... | collective-permute-start | bytes 147464 | tf_op jit(solution)/shard_map/ppermute | solution.py:25
  90.2 21.9 %collective-permute-start.6 = (bf16[64,384]{1,0:T(8,128)(2,1)S(1)}, bf16[64,384]{1,0:T(8,128)(2,1)S(1)}, u32[]{:S(2)}, u32[]{:S(2)}) collective-permute-start(bf16[64,384]{1,0:T(8,128)(2,1)S(1)} %reshape.156), channel_id=1, source_target_pairs={{0,1},{1,2},{2,3},{3,4},{4,5},{5,6},{6,7},{7,8},{8,9},{9,10},{10,1... | collective-permute-start | bytes 147464 | tf_op jit(solution)/shard_map/ppermute | solution.py:23
  92.1 3.6 collective-permute-start.15
  95.7 4.6 collective-permute-start.14
  100.3 150.0 %collective-permute-start.5 = (bf16[64,1536]{0,1:T(8,128)(2,1)S(1)}, bf16[64,1536]{0,1:T(8,128)(2,1)}, u32[]{:S(2)}, u32[]{:S(2)}) collective-permute-start(bf16[64,1536]{0,1:T(8,128)(2,1)S(1)} %bitcast.431), channel_id=1, source_target_pairs={{1,0},{2,1},{3,2},{4,3},{5,4},{6,5},{7,6},{8,7},{9,8},{10,9},{11,1... | collective-permute-start | bytes 589832 | tf_op jit(solution)/shard_map/ppermute | solution.py:25
  110.0 15.5 %collective-permute-start.18 = (f32[64,64]{1,0:T(8,128)S(1)}, f32[64,64]{1,0:T(8,128)}, u32[]{:S(2)}, u32[]{:S(2)}) collective-permute-start(f32[64,64]{1,0:T(8,128)S(1)} %convolution_add_fusion.31), channel_id=1, source_target_pairs={{0,8},{8,0},{1,9},{9,1},{2,10},{10,2},{3,11},{11,3},{4,12},{12,4},... | collective-permute-start | bytes 49160 | tf_op jit(solution)/shard_map/ppermute | solution.py:39
  112.1 20.3 %collective-permute-start.17 = (f32[64,64]{1,0:T(8,128)S(1)}, f32[64,64]{1,0:T(8,128)}, u32[]{:S(2)}, u32[]{:S(2)}) collective-permute-start(f32[64,64]{1,0:T(8,128)S(1)} %convolution_add_fusion.31), channel_id=1, source_target_pairs={{0,16},{16,0},{1,17},{17,1},{2,18},{18,2},{3,19},{19,3},{4,20},{20... | collective-permute-start | bytes 49160 | tf_op jit(solution)/shard_map/ppermute | solution.py:39
  127.4 13.7 %collective-permute-start.21 = (f32[64,64]{1,0:T(8,128)S(1)}, f32[64,64]{1,0:T(8,128)S(1)}, u32[]{:S(2)}, u32[]{:S(2)}) collective-permute-start(f32[64,64]{1,0:T(8,128)S(1)} %convolution_add_fusion.29), channel_id=1, source_target_pairs={{0,16},{16,0},{1,17},{17,1},{2,18},{18,2},{3,19},{19,3},{4,20},{20... | collective-permute-start | bytes 49160 | tf_op jit(solution)/shard_map/ppermute | solution.py:39
  132.4 12.4 %collective-permute-start.20 = (f32[64,64]{1,0:T(8,128)S(1)}, f32[64,64]{1,0:T(8,128)S(1)}, u32[]{:S(2)}, u32[]{:S(2)}) collective-permute-start(f32[64,64]{1,0:T(8,128)S(1)} %convolution_add_fusion.29), channel_id=1, source_target_pairs={{0,32},{32,0},{1,33},{33,1},{2,34},{34,2},{3,35},{35,3},{4,36},{36... | collective-permute-start | bytes 49160 | tf_op jit(solution)/shard_map/ppermute | solution.py:39
  142.9 4.7 collective-permute-start.24
  144.8 8.9 %collective-permute-start.23 = (f32[64,64]{1,0:T(8,128)S(1)}, f32[64,64]{1,0:T(8,128)S(1)}, u32[]{:S(2)}, u32[]{:S(2)}) collective-permute-start(f32[64,64]{1,0:T(8,128)S(1)} %convolution_add_fusion.27), channel_id=1, source_target_pairs={{0,64},{64,0},{1,65},{65,1},{2,66},{66,2},{3,67},{67,3},{4,68},{68... | collective-permute-start | bytes 49160 | tf_op jit(solution)/shard_map/ppermute | solution.py:39
  149.4 14.0 %collective-permute-start.27 = (f32[64,64]{1,0:T(8,128)S(1)}, f32[64,64]{1,0:T(8,128)S(1)}, u32[]{:S(2)}, u32[]{:S(2)}) collective-permute-start(f32[64,64]{1,0:T(8,128)S(1)} %convolution_add_fusion.25), channel_id=1, source_target_pairs={{0,64},{64,0},{1,65},{65,1},{2,66},{66,2},{3,67},{67,3},{4,68},{68... | collective-permute-start | bytes 49160 | tf_op jit(solution)/shard_map/ppermute | solution.py:39
  153.7 17.4 %collective-permute-start.26 = (f32[64,64]{1,0:T(8,128)S(1)}, f32[64,64]{1,0:T(8,128)S(1)}, u32[]{:S(2)}, u32[]{:S(2)}) collective-permute-start(f32[64,64]{1,0:T(8,128)S(1)} %convolution_add_fusion.25), channel_id=1, source_target_pairs={{0,128},{128,0},{1,129},{129,1},{2,130},{130,2},{3,131},{131,3},{4... | collective-permute-start | bytes 49160 | tf_op jit(solution)/shard_map/ppermute | solution.py:39
  165.2 14.0 %collective-permute-start.29 = (f32[64,64]{1,0:T(8,128)S(1)}, f32[64,64]{1,0:T(8,128)S(1)}, u32[]{:S(2)}, u32[]{:S(2)}) collective-permute-start(f32[64,64]{1,0:T(8,128)S(1)} %convolution_add_fusion.23), channel_id=1, source_target_pairs={{0,256},{256,0},{1,257},{257,1},{2,258},{258,2},{3,259},{259,3},{4... | collective-permute-start | bytes 49160 | tf_op jit(solution)/shard_map/ppermute | solution.py:39
  171.1 10.1 %collective-permute-start.30 = (f32[64,64]{1,0:T(8,128)S(1)}, f32[64,64]{1,0:T(8,128)S(1)}, u32[]{:S(2)}, u32[]{:S(2)}) collective-permute-start(f32[64,64]{1,0:T(8,128)S(1)} %convolution_add_fusion.23), channel_id=1, source_target_pairs={{0,128},{128,0},{1,129},{129,1},{2,130},{130,2},{3,131},{131,3},{4... | collective-permute-start | bytes 49160 | tf_op jit(solution)/shard_map/ppermute | solution.py:39
  179.2 71.1 %collective-permute-start.4 = (bf16[64,1536]{0,1:T(8,128)(2,1)S(1)}, bf16[64,1536]{0,1:T(8,128)(2,1)S(1)}, u32[]{:S(2)}, u32[]{:S(2)}) collective-permute-start(bf16[64,1536]{0,1:T(8,128)(2,1)S(1)} %bitcast.432), channel_id=1, source_target_pairs={{0,1},{1,2},{2,3},{3,4},{4,5},{5,6},{6,7},{7,8},{8,9},{9,10},{10,1... | collective-permute-start | bytes 589832 | tf_op jit(solution)/shard_map/ppermute | solution.py:23
  181.2 13.5 %collective-permute-start.31 = (f32[64,64]{1,0:T(8,128)S(1)}, f32[64,64]{1,0:T(8,128)S(1)}, u32[]{:S(2)}, u32[]{:S(2)}) collective-permute-start(f32[64,64]{1,0:T(8,128)S(1)} %collective-permute-done.30), channel_id=1, source_target_pairs={{0,256},{256,0},{1,257},{257,1},{2,258},{258,2},{3,259},{259,3},{4... | collective-permute-start | bytes 49160 | tf_op jit(solution)/shard_map/ppermute | solution.py:39
  194.7 9.0 %collective-permute-start.28 = (f32[64,64]{1,0:T(8,128)S(1)}, f32[64,64]{1,0:T(8,128)S(1)}, u32[]{:S(2)}, u32[]{:S(2)}) collective-permute-start(f32[64,64]{1,0:T(8,128)S(1)} %collective-permute-done.27), channel_id=1, source_target_pairs={{0,128},{128,0},{1,129},{129,1},{2,130},{130,2},{3,131},{131,3},{4... | collective-permute-start | bytes 49160 | tf_op jit(solution)/shard_map/ppermute | solution.py:39
  203.7 5.7 %collective-permute-start.25 = (f32[64,64]{1,0:T(8,128)S(1)}, f32[64,64]{1,0:T(8,128)S(1)}, u32[]{:S(2)}, u32[]{:S(2)}) collective-permute-start(f32[64,64]{1,0:T(8,128)S(1)} %collective-permute-done.24), channel_id=1, source_target_pairs={{0,64},{64,0},{1,65},{65,1},{2,66},{66,2},{3,67},{67,3},{4,68},{68... | collective-permute-start | bytes 49160 | tf_op jit(solution)/shard_map/ppermute | solution.py:39
  209.4 5.3 %collective-permute-start.22 = (f32[64,64]{1,0:T(8,128)S(1)}, f32[64,64]{1,0:T(8,128)S(1)}, u32[]{:S(2)}, u32[]{:S(2)}) collective-permute-start(f32[64,64]{1,0:T(8,128)S(1)} %collective-permute-done.21), channel_id=1, source_target_pairs={{0,32},{32,0},{1,33},{33,1},{2,34},{34,2},{3,35},{35,3},{4,36},{36... | collective-permute-start | bytes 49160 | tf_op jit(solution)/shard_map/ppermute | solution.py:39
  214.7 6.4 %collective-permute-start.19 = (f32[64,64]{1,0:T(8,128)}, f32[64,64]{1,0:T(8,128)S(1)}, u32[]{:S(2)}, u32[]{:S(2)}) collective-permute-start(f32[64,64]{1,0:T(8,128)} %collective-permute-done.18), channel_id=1, source_target_pairs={{0,16},{16,0},{1,17},{17,1},{2,18},{18,2},{3,19},{19,3},{4,20},{20... | collective-permute-start | bytes 49160 | tf_op jit(solution)/shard_map/ppermute | solution.py:39
  221.1 4.6 collective-permute-start.16
  225.7 15.5 %collective-permute-start.13 = (f32[64,64]{1,0:T(8,128)S(1)}, f32[64,64]{1,0:T(8,128)S(1)}, u32[]{:S(2)}, u32[]{:S(2)}) collective-permute-start(f32[64,64]{1,0:T(8,128)S(1)} %copy-done.42), channel_id=1, source_target_pairs={{0,4},{4,0},{1,5},{5,1},{2,6},{6,2},{3,7},{7,3},{8,12},{12,8},{9,1... | collective-permute-start | bytes 49160 | tf_op jit(solution)/shard_map/ppermute | solution.py:39
  241.2 6.2 %collective-permute-start.10 = (f32[64,64]{1,0:T(8,128)S(1)}, f32[64,64]{1,0:T(8,128)S(1)}, u32[]{:S(2)}, u32[]{:S(2)}) collective-permute-start(f32[64,64]{1,0:T(8,128)S(1)} %collective-permute-done.9), channel_id=1, source_target_pairs={{0,2},{2,0},{1,3},{3,1},{4,6},{6,4},{5,7},{7,5},{8,10},{10,8},{9,1... | collective-permute-start | bytes 49160 | tf_op jit(solution)/shard_map/ppermute | solution.py:39
  (99 other events, 1546.1 us)
where the time goes:
time: 500 us; the launch traced here: 494 us
  matrix products  171 us (34%)
  starting transfers between devices  141 us (28%)
  local copies, waits for them, and re-layouts  107 us (21%)
  other arithmetic  37.1 us (7%)
  loops' own time  21.1 us (4%)
  waiting for transfers between devices  14.9 us (3%)
    dot_general x27, matrix products, slot_step(): jnp.einsum('lim,rlm->rli', kernel, source_charges, preferred_element_type...  119 us
    ppermute x24, starting transfers between devices, swapped(): return lax.ppermute(block, axis, route)  111 us
    dot_general x37, matrix products, apply_matrix(): jnp.dot(vector, matrix.astype(jnp.float32), precision=lax.Precision.HIGHEST)  34 us
    gather x24, local copies, waits for them, and re-layouts, couple_level(): blocks = jnp.take(coupling, classes[:, column], axis=0)  29.2 us
    gather x24, local copies, waits for them, and re-layouts, couple_level(): picked = jnp.take(table_ext, sources[:, column] - offset, axis=1)  28.4 us
    ppermute x4, starting transfers between devices, with_halo(): lax.ppermute(head, axis, [((i + 1) % count, i) for i in range(ends)])  22 us
    another operation x1, loops' own time, local(): lax.fori_loop(0, slot_limit, slot_step, jnp.zeros((row_count, leaf_count,...  21.1 us
    reduce_and x27, other arithmetic, slot_step(): source_charges = jnp.take(charge_grid, column, axis=1)  18.8 us
  transfers between devices with their start and end apart: 32, of which 8 were waited for; matrix products, arithmetic and copies ran while one was open for 25% of the time, Pallas kernels for 0%

commit v1 on v0

v1 whole, which is shorter than its diff:
```python
import math

import jax
import jax.numpy as jnp
import numpy as np
from jax import lax
from jax.experimental import pallas as pl
from jax.experimental.pallas import tpu as pltpu
from jax.sharding import PartitionSpec as P

BF = jnp.bfloat16
F32 = jnp.float32
AXES = ("box", "rhs")

R = 64
K = 64
M = 128
LD = 24
BX = 6
ADM = 16
ADMB = 8
NEAR = 27
FR = 16
ROWS = R + FR
FX = 32
UNROLL = 8
LOW = 32
SLOTS = LD * (NEAR + 1) + 2 * UNROLL

DELTA2 = 0.0001
INV_SCALE = 2.0 * math.sqrt(NEAR * M)
CENTRE = 1.1

PARTS = ((0, 0), (0, 1), (0, 2), (1, 0), (1, 1), (1, 2), (2, 0), (2, 1))

VMEM = pl.BlockSpec(memory_space=pltpu.VMEM)
SMEM = pl.BlockSpec(memory_space=pltpu.SMEM)
ANY = pl.BlockSpec(memory_space=pl.ANY)


def params():
    return pltpu.CompilerParams(vmem_limit_bytes=40 * 1024 * 1024)


def sds(shape, dtype):
    return jax.ShapeDtypeStruct(shape, dtype)


def dot(a, b):
    return jnp.dot(a, b, preferred_element_type=F32)


def dot_nt(a, b):
    return lax.dot_general(a, b, (((1,), (1,)), ((), ())), preferred_element_type=F32)


def dot2(x, m):
    hi = x.astype(BF)
    lo = (x - hi.astype(F32)).astype(BF)
    return dot(hi, m) + dot(lo, m)


def expansion():
    out = np.zeros((8 * FR, 8, M), np.float32)
    for leaf in range(8):
        e = 0
        for a, _ in PARTS:
            for c in range(3):
                out[FR * leaf + 3 * a + c, leaf, e] = 1.0
                e += 1
        for c in range(3):
            out[FR * leaf + 9 + c, leaf, e] = 1.0
            e += 1
        for c in range(3):
            out[FR * leaf + 12, leaf, e] = 1.0
            e += 1
    return out.reshape(8 * FR, 8 * M)


def split3(x):
    hi = x.astype(BF).astype(F32)
    rest = x - hi
    mid = rest.astype(BF).astype(F32)
    return hi, mid, rest - mid


def pack_body(charges, points, sent, target, feat, wide):
    p = (points[...] - CENTRE) * INV_SCALE
    parts = split3(p)
    norm = p[0:1] * p[0:1] + p[1:2] * p[1:2] + p[2:3] * p[2:3]
    source_norm = split3(norm)
    target_norm = split3(norm + DELTA2 * INV_SCALE * INV_SCALE)
    feat[...] = jnp.zeros(feat.shape, F32)
    wide[...] = jnp.zeros(wide.shape, F32)
    one = jnp.ones(norm.shape, F32)
    for a in range(3):
        feat[3 * a : 3 * a + 3, :] = parts[a]
        feat[9 + a : 10 + a, :] = source_norm[a]
    feat[12:13, :] = one
    for n, (_, b) in enumerate(PARTS):
        wide[3 * n : 3 * n + 3, :] = -2.0 * parts[b]
    base = 3 * len(PARTS)
    for a in range(3):
        wide[base + a : base + a + 1, :] = one
        wide[base + 3 + a : base + 4 + a, :] = target_norm[a]
    for leaf in range(LD):
        cols = pl.ds(leaf * M, M)
        sent[leaf, 0:R, :] = charges[:, cols]
        target[leaf, :, :] = wide[:, cols].astype(BF)
    for o in range(LD // 8):
        rows = jnp.concatenate([feat[:, pl.ds((8 * o + i) * M, M)] for i in range(8)], axis=0)
        turned = rows.T.astype(BF)
        for i in range(8):
            sent[8 * o + i, R:ROWS, :] = turned[FR * i : FR * (i + 1), :]


def pack(charges, points):
    return pl.pallas_call(
        pack_body,
        in_specs=[VMEM, VMEM],
        out_specs=[VMEM, VMEM],
        out_shape=[sds((LD, ROWS, M), BF), sds((LD, FX, M), BF)],
        scratch_shapes=[pltpu.VMEM((FR, LD * M), F32), pltpu.VMEM((FX, LD * M), F32)],
        compiler_params=params(),
        name="pack_points",
    )(charges, points)


def up_body(charges, basis, leaf_up, box_up, parents, code, coef, ascent, own, halo, sizes, acc):
    acc[...] = jnp.zeros(acc.shape, F32)
    po = jnp.int32(0)
    ph = jnp.int32(0)
    for leaf in range(LD):
        cols = pl.ds(leaf * M, M)
        c = dot_nt(charges[:, cols], basis[:, cols])
        if leaf % 2 == 0:
            even = c
        else:
            coef[leaf // 2] = jnp.concatenate([even, c], axis=1).astype(BF)
        acc[parents[leaf]] += dot(c.astype(BF), leaf_up[leaf])
        for s in range(NEAR):
            x = code[leaf, s]
            own[po] = x
            halo[ph] = x
            po = po + ((x >> 16) & 1)
            ph = ph + (x >> 17)
        own[po] = leaf << 8 | LD
        halo[ph] = leaf << 8 | (2 * LD)
        po = (po + 1) & -2
        ph = (ph + 1) & -2
    for n in range(2 * UNROLL):
        own[po + n] = LD << 8 | LD
        halo[ph + n] = LD << 8 | (2 * LD)
    sizes[0] = (po // 2 + UNROLL - 1) // UNROLL
    sizes[1] = (ph // 2 + UNROLL - 1) // UNROLL
    total = jnp.zeros((R, K), F32)
    for box in range(BX):
        b = acc[box]
        if box % 2 == 0:
            even = b
        else:
            coef[(LD + box) // 2] = jnp.concatenate([even, b], axis=1).astype(BF)
        total = total + dot(b.astype(BF), box_up[box])
    ascent[...] = jnp.concatenate([total[: R // 2], total[R // 2 :]], axis=1).astype(BF)


def climb(charges, basis, leaf_up, box_up, parents, code):
    return pl.pallas_call(
        up_body,
        in_specs=[VMEM, VMEM, VMEM, VMEM, SMEM, SMEM],
        out_specs=[VMEM, VMEM, SMEM, SMEM, SMEM],
        out_shape=[
            sds(((LD + BX) // 2, R, 2 * K), BF),
            sds((R // 2, 2 * K), BF),
            sds((SLOTS,), jnp.int32),
            sds((SLOTS,), jnp.int32),
            sds((2,), jnp.int32),
        ],
        scratch_shapes=[pltpu.VMEM((BX, R, K), F32)],
        compiler_params=params(),
        name="leaf_to_group",
    )(charges, basis, leaf_up, box_up, parents, code)


def near_body(which, blocks, *refs):
    sizes, slots, target, expand = refs[:4]
    sources = refs[4 : 4 + blocks]
    rest = refs[4 + blocks :]
    if which == 1:
        start_from, _, out, table, feats, acc, sems = rest
    else:
        out, table, feats, acc, sems = rest
    count = blocks * LD
    copies = [
        pltpu.make_async_copy(src, table.at[pl.ds(n * LD, LD)], sems.at[n])
        for n, src in enumerate(sources)
    ]
    for copy in copies:
        copy.start()
    if which == 1:
        acc[0:LD] = start_from[...]
        acc[LD] = jnp.zeros((R, M), F32)
    else:
        acc[...] = jnp.zeros(acc.shape, F32)
    table[count] = jnp.zeros((ROWS, M), BF)
    for copy in copies:
        copy.wait()
    for o in range(count // 8):
        rows = jnp.concatenate([table[8 * o + i, R:ROWS, :] for i in range(8)], axis=0)
        spread = dot(rows, expand[...]).astype(BF)
        for i in range(8):
            feats[8 * o + i] = spread[:, M * i : M * (i + 1)]
    lane = lax.broadcasted_iota(jnp.int32, (M, M), 1)
    ones = 3 * len(PARTS) + 3
    feats[count] = jnp.where((lane >= ones) & (lane < ones + 3), 1.0, 0.0).astype(BF)
    pad = jnp.zeros((M - FX, M), BF)

    def step(it, _):
        for u in range(UNROLL):
            at = (it * UNROLL + u) * 2
            first, second = slots[at], slots[at + 1]
            s0, s1 = first & 255, second & 255
            t = (first >> 8) & 255
            rows = jnp.concatenate([feats[s0], feats[s1]], axis=0)
            square = dot(rows, jnp.concatenate([target[jnp.minimum(t, LD - 1)], pad], axis=0))
            kernel = lax.rsqrt(square).astype(BF)
            weights = jnp.concatenate([table[s0, 0:R, :], table[s1, 0:R, :]], axis=1)
            acc[t] += dot(weights, kernel)
        return 0

    lax.fori_loop(0, sizes[which], step, 0)
    out[...] = acc[0:LD]


def near(which, sizes, slots, target, expand, sources, extra):
    blocks = len(sources)
    pairs = 400 if which else 200
    return pl.pallas_call(
        lambda *refs: near_body(which, blocks, *refs),
        in_specs=[SMEM, SMEM, VMEM, VMEM] + [ANY] * blocks + ([VMEM, ANY] if which else []),
        out_specs=VMEM,
        out_shape=sds((LD, R, M), F32),
        scratch_shapes=[
            pltpu.VMEM((blocks * LD + 1, ROWS, M), BF),
            pltpu.VMEM((blocks * LD + 1, M, M), BF),
            pltpu.VMEM((LD + 1, R, M), F32),
            pltpu.SemaphoreType.DMA((blocks,)),
        ],
        compiler_params=params(),
        cost_estimate=pl.CostEstimate(
            flops=pairs * 2 * 256 * 128 * 320, bytes_accessed=2 << 20, transcendentals=pairs << 15
        ),
        name="near_halo" if which else "near_own",
    )(sizes, slots, target, expand, *sources, *extra)


def level_up(nodes, matrices):
    count = nodes.shape[0] // 2
    pairs = nodes.reshape(count, 2, R // 2, 2 * K)
    left = pairs[:, 0].reshape(count * (R // 2), 2 * K)
    right = pairs[:, 1].reshape(count * (R // 2), 2 * K)
    if nodes.dtype == BF:
        out = dot(left, matrices[0]) + dot(right, matrices[1])
    else:
        out = dot2(left, matrices[0]) + dot2(right, matrices[1])
    return out.reshape(count, R // 2, 2 * K)


def block_fields(nodes, up, coupling, held, place, fields):
    out = []
    for h in range(4):
        count = LOW >> h
        held[0:count] = nodes.astype(F32)
        q = place >> h
        out.append(dot2(held[q ^ 2], coupling[h, 0]) + dot2(held[q ^ 3], coupling[h, 1]))
        if h < 3 or fields is None:
            nodes = level_up(nodes, (up[h, 0], up[h, 1]))
    return out, nodes


def low_body(place, nodes, up, coupling, down, _, top, field, held):
    me = place[0]
    fields, nodes = block_fields(nodes[...], up, coupling, held, me & (LOW - 1), None)
    top[...] = nodes.astype(BF)
    total = fields[3]
    for h in (2, 1, 0):
        total = fields[h] + dot2(total, down[h, (me >> h) & 1])
    field[...] = total


def low_tree(place, nodes, mats, order):
    return pl.pallas_call(
        low_body,
        in_specs=[SMEM, VMEM, VMEM, VMEM, VMEM, ANY],
        out_specs=[VMEM, VMEM],
        out_shape=[sds((2, R // 2, 2 * K), BF), sds((R // 2, 2 * K), F32)],
        scratch_shapes=[pltpu.VMEM((LOW, R // 2, 2 * K), F32)],
        compiler_params=params(),
        name="coarse_low",
    )(place, nodes, *mats, order)


def couple_body(codes, box_codes, matrices, box_matrices, left, mine, right, _, leaf_field, box_field, table, low, high, sems):
    pairs = (LD + BX) // 2
    copies = [
        pltpu.make_async_copy(src, table.at[pl.ds(n * pairs, pairs)], sems.at[n])
        for n, src in enumerate((left, mine, right))
    ]
    for copy in copies:
        copy.start()
    for copy in copies:
        copy.wait()
    first = lax.broadcasted_iota(jnp.int32, (R, 2 * K), 1) < K
    for n in range(3):
        for i in range(pairs):
            x = table[n * pairs + i].astype(F32)
            y = pltpu.roll(x, K, 1)
            at = 2 * (n * pairs + i)
            low[at] = jnp.where(first, x, 0.0).astype(BF)
            low[at + 1] = jnp.where(first, y, 0.0).astype(BF)
            high[at] = jnp.where(first, 0.0, y).astype(BF)
            high[at + 1] = jnp.where(first, 0.0, x).astype(BF)

    def gather(codes, row, mats, width):
        total = jnp.zeros((R, K), F32)
        for g in range(width // 4):
            c = [codes[row, 4 * g + i] for i in range(4)]
            s = [x & 255 for x in c]
            vec = jnp.concatenate([low[s[0]] + high[s[1]], low[s[2]] + high[s[3]]], axis=1)
            mat = jnp.concatenate([mats[x >> 8] for x in c], axis=0)
            total = total + dot(vec, mat)
        return total

    def step(it, _):
        for u in range(6):
            row = it * 6 + u
            leaf_field[row] = gather(codes, row, matrices, ADM)
        return 0

    lax.fori_loop(0, LD // 6, step, 0)
    for box in range(BX):
        box_field[box] = gather(box_codes, box, box_matrices, ADMB)


def couple(codes, box_codes, matrices, box_matrices, coefs, order):
    pairs = (LD + BX) // 2
    return pl.pallas_call(
        couple_body,
        in_specs=[SMEM, SMEM, VMEM, VMEM, ANY, ANY, ANY, ANY],
        out_specs=[VMEM, VMEM],
        out_shape=[sds((LD, R, K), F32), sds((BX, R, K), F32)],
        scratch_shapes=[
            pltpu.VMEM((3 * pairs, R, 2 * K), BF),
            pltpu.VMEM((6 * pairs, R, 2 * K), BF),
            pltpu.VMEM((6 * pairs, R, 2 * K), BF),
            pltpu.SemaphoreType.DMA((3,)),
        ],
        compiler_params=params(),
        cost_estimate=pl.CostEstimate(flops=1 << 30, bytes_accessed=1 << 20, transcendentals=0),
        name="couple_levels",
    )(codes, box_codes, matrices, box_matrices, *coefs, order)


def final_body(place, nodes, up, coupling, down, low_down, low_field, parents, leaf_field, box_field, box_down, leaf_down, basis, near_part, out, held, boxes):
    me = place[0]
    block = nodes[...].reshape(LOW, R // 2, 2 * K)
    fields, _ = block_fields(block, up, coupling, held, (me >> 4) & (LOW - 1), True)
    total = fields[3]
    for h in (2, 1, 0):
        total = fields[h] + dot2(total, down[h, (me >> (h + 4)) & 1])
    for h in (3, 2, 1, 0):
        total = dot2(total, low_down[h, (me >> h) & 1])
    total = total + low_field[...]
    group = jnp.concatenate([total[:, :K], total[:, K:]], axis=0).astype(BF)
    for box in range(BX):
        boxes[box] = (box_field[box] + dot(group, box_down[box])).astype(BF)
    for leaf in range(LD):
        cols = pl.ds(leaf * M, M)
        field = leaf_field[leaf] + dot(boxes[parents[leaf]], leaf_down[leaf])
        out[:, cols] = near_part[leaf] + dot(field.astype(BF), basis[:, cols])


def finish(place, nodes, high_mats, low_down, low_field, parents, fields, box_down, leaf_down, basis, near_part):
    return pl.pallas_call(
        final_body,
        in_specs=[SMEM] + [VMEM] * 6 + [SMEM] + [VMEM] * 6,
        out_specs=VMEM,
        out_shape=sds((R, LD * M), F32),
        scratch_shapes=[pltpu.VMEM((LOW, R // 2, 2 * K), F32), pltpu.VMEM((BX, R, K), BF)],
        compiler_params=params(),
        name="group_to_points",
    )(place, nodes, *high_mats, low_down, low_field, parents, *fields, box_down, leaf_down, basis, near_part)


def doubled(m):
    edge = ((0, 0),) * (m.ndim - 2)
    return jnp.pad(m, edge + ((0, K), (0, K))) + jnp.pad(m, edge + ((K, 0), (K, 0)))


def exchange(x):
    count = lax.axis_size(AXES)
    left = lax.ppermute(x, AXES, [(i, i + 1) for i in range(count - 1)])
    right = lax.ppermute(x, AXES, [(i + 1, i) for i in range(count - 1)])
    return left, right


def local(
    charges,
    points,
    leaf_basis,
    leaf_parent,
    leaf_up,
    leaf_down,
    box_up,
    box_down,
    top_up,
    top_down,
    top_coupling,
    leaf_sources,
    leaf_classes,
    leaf_coupling,
    box_sources,
    box_classes,
    box_coupling,
    near_leaves,
    near_count,
):
    count = lax.axis_size(AXES)
    device = lax.axis_index(AXES)
    place = device.astype(jnp.int32).reshape(1)
    parents = leaf_parent[0]
    pairs = (LD + BX) // 2

    sent, target = pack(charges, points)
    sent_left, sent_right = exchange(sent)

    rel = near_leaves - device * LD
    mine = (rel >= 0) & (rel < LD)
    used = jnp.arange(NEAR, dtype=jnp.int32)[None, :] < near_count[:, None]
    row = jnp.where(rel < 0, rel + LD, rel)
    leaf_ids = jnp.arange(LD, dtype=jnp.int32)[:, None]
    flags = jnp.where(used, jnp.where(mine, 1, 2), 0)
    code = row | leaf_ids << 8 | flags << 16

    coef, ascent, own, halo, sizes = climb(charges, leaf_basis, leaf_up, box_up, parents, code)

    blocks = count // LOW
    low_groups = [[b * LOW + i for i in range(LOW)] for b in range(blocks)]
    high_groups = [[b * LOW + i for b in range(blocks)] for i in range(LOW)]
    low_nodes = lax.all_gather(ascent, AXES, axis_index_groups=low_groups)
    coef_left, coef_right = exchange(coef)

    expand = jnp.asarray(expansion(), BF)
    near_own = near(0, sizes, own, target, expand, (sent,), ())

    low_mats = [doubled(m[0:4]) for m in (top_up, top_coupling, top_down)]
    high_mats = [doubled(m[4:8]) for m in (top_up, top_coupling, top_down)]
    top, low_field = low_tree(place, low_nodes, low_mats, near_own)
    high_nodes = lax.all_gather(top, AXES, axis_index_groups=high_groups)

    near_all = near(1, sizes, halo, target, expand, (sent_left, sent_right), (near_own, low_field))

    def table_row(sources, classes, width, start):
        rel = sources - (device - 1) * width
        block = (rel >= width).astype(jnp.int32) + (rel >= 2 * width).astype(jnp.int32)
        return rel + block * (2 * pairs - width) + start | classes << 8

    codes = table_row(leaf_sources, leaf_classes, LD, 0)
    box_codes = table_row(box_sources, box_classes, BX, LD)
    fields = couple(
        codes, box_codes, leaf_coupling, box_coupling, (coef_left, coef, coef_right), low_field
    )
    return finish(
        place, high_nodes, high_mats, low_mats[2], low_field, parents, fields, box_down, leaf_down, leaf_basis, near_all
    )


def solution(mesh):
    split = P(AXES)
    return jax.shard_map(
        local,
        mesh=mesh,
        in_specs=(
            P(None, AXES),
            P(None, AXES),
            P(None, AXES),
            split,
            split,
            split,
            split,
            split,
            P(),
            P(),
            P(),
            split,
            split,
            P(),
            split,
            split,
            P(),
            split,
            split,
        ),
        out_specs=P(None, AXES),
        check_vma=False,
    )
```

time: 500 us -> 184 us (0.37)
  the two profiles are of different devices: /device:TPU:71 before, /device:TPU:32 now
where the time goes in v1:
time: 184 us; the launch traced here: 183 us
  blocking collectives  80.3 us (44%)
  Pallas kernels  72.3 us (39%)
  starting transfers between devices  19.7 us (11%)
  local copies, waits for them, and re-layouts  9.19 us (5%)
    pallas_call x2, Pallas kernels, near(): pl.pallas_call(lambda *refs: near_body(which, blocks, *refs), in_specs=[S...  54.5 us
    all_gather x1, blocking collectives, local(): low_nodes = lax.all_gather(ascent, AXES, axis_index_groups=low_groups)  41.2 us
    all_gather x1, blocking collectives, local(): high_nodes = lax.all_gather(top, AXES, axis_index_groups=high_groups)  39 us
    ppermute x2, starting transfers between devices, exchange(): right = lax.ppermute(x, AXES, [(i + 1, i) for i in range(count - 1)])  14.2 us
    unnamed x52, local copies, waits for them, and re-layouts  8.48 us
    pallas_call x1, Pallas kernels, climb(): pl.pallas_call(up_body, in_specs=[VMEM, VMEM, VMEM, VMEM, SMEM, SMEM], ou...  6.49 us
    ppermute x2, starting transfers between devices, exchange(): left = lax.ppermute(x, AXES, [(i, i + 1) for i in range(count - 1)])  5.53 us
    pallas_call x1, Pallas kernels, couple(): pl.pallas_call(couple_body, in_specs=[SMEM, SMEM, VMEM, VMEM, ANY, ANY, A...  4.68 us
  transfers between devices with their start and end apart: 4, of which 0 were waited for; matrix products, arithmetic and copies ran while one was open for 1% of the time, Pallas kernels for 17%

profile of v1, /device:TPU:32, one launch (start us, length us, event | category | flops | bytes accessed | tf_op | source)
XLA Modules:
  0.0 183.1 jit_solution(10099626911061416979)
XLA Ops:
  0.0 1.0 copy-done
  1.0 0.8 copy-done.8
  1.8 1.1 pack_points.1
  2.9 3.5 %collective-permute-start.2 = (bf16[24,80,128]{2,1,0:T(8,128)(2,1)}, bf16[24,80,128]{2,1,0:T(8,128)(2,1)}, u32[]{:S(2)}, u32[]{:S(2)}) collective-permute-start(bf16[24,80,128]{2,1,0:T(8,128)(2,1)} %get-tuple-element.20.refs_4_), channel_id=1, source_target_pairs={{0,1},{1,2},{2,3},{3,4},{4,5},{5,6},{6,7},{7,8},{8,9},{9,10},{10,1... | collective-permute-start | bytes 1474568 | tf_op jit(solution)/shard_map/ppermute | solution.py:402
  6.4 6.3 %collective-permute-start.3 = (bf16[24,80,128]{2,1,0:T(8,128)(2,1)}, bf16[24,80,128]{2,1,0:T(8,128)(2,1)}, u32[]{:S(2)}, u32[]{:S(2)}) collective-permute-start(bf16[24,80,128]{2,1,0:T(8,128)(2,1)} %get-tuple-element.20.refs_4_), channel_id=1, source_target_pairs={{1,0},{2,1},{3,2},{4,3},{5,4},{6,5},{7,6},{8,7},{9,8},{10,9},{11,1... | collective-permute-start | bytes 1474568 | tf_op jit(solution)/shard_map/ppermute | solution.py:403
  12.7 0.8 fusion.1.code
  13.5 1.0 copy-done.2
  14.5 1.0 copy-done.4
  15.5 0.7 copy-done.9
  16.2 6.5 %leaf_to_group.1 = (bf16[15,64,128]{2,1,0:T(8,128)(2,1)}, bf16[32,128]{1,0:T(8,128)(2,1)S(1)}, s32[688]{0:T(1024)S(1)}, s32[688]{0:T(1024)S(1)}, s32[2]{0:T(128)S(1)}) custom-call(bf16[64,3072]{1,0:T(8,128)(2,1)S(1)} %copy-done.1, bf16[64,3072]{1,0:T(8,128)(2,1)S(1)} %copy-done.2, bf16[24,64,64]{2,1,0:T(8,128)(2,1)S(1)} %copy-done.4, ...), custom_call_target="tpu_custom_call" | custom-call | tf_op jit(solution)/shard_map/leaf_to_group/pallas_call | solution.py:168
  22.7 2.1 %collective-permute-start = (bf16[15,64,128]{2,1,0:T(8,128)(2,1)}, bf16[15,64,128]{2,1,0:T(8,128)(2,1)}, u32[]{:S(2)}, u32[]{:S(2)}) collective-permute-start(bf16[15,64,128]{2,1,0:T(8,128)(2,1)} %get-tuple-element.23.mine), channel_id=1, source_target_pairs={{0,1},{1,2},{2,3},{3,4},{4,5},{5,6},{6,7},{7,8},{8,9},{9,10},{10,1... | collective-permute-start | bytes 737288 | tf_op jit(solution)/shard_map/ppermute | solution.py:402
  24.7 7.9 %collective-permute-start.1 = (bf16[15,64,128]{2,1,0:T(8,128)(2,1)}, bf16[15,64,128]{2,1,0:T(8,128)(2,1)}, u32[]{:S(2)}, u32[]{:S(2)}) collective-permute-start(bf16[15,64,128]{2,1,0:T(8,128)(2,1)} %get-tuple-element.23.mine), channel_id=1, source_target_pairs={{1,0},{2,1},{3,2},{4,3},{5,4},{6,5},{7,6},{8,7},{9,8},{10,9},{11,1... | collective-permute-start | bytes 737288 | tf_op jit(solution)/shard_map/ppermute | solution.py:403
  32.6 41.2 %all-gather = bf16[1024,128]{1,0:T(8,128)(2,1)S(1)} all-gather(bf16[32,128]{1,0:T(8,128)(2,1)S(1)} %get-tuple-element.16), channel_id=2, replica_groups={{0,1,2,3,4,5,6,7,8,9,10,11,12,13,14,15,16,17,18,19,20,21,22,23,24,25,26..., dimensions={0}, use_global_device_ids=true | all-gather | bytes 270336 | tf_op jit(solution)/shard_map/all_gather | solution.py:450
  73.9 0.9 copy-done.19
  74.8 0.7 fusion.4
  75.5 0.3 copy-done.20
  75.8 0.1 pad_add_fusion.3.down.low_down
  75.9 0.2 pad_add_fusion.4
  76.1 0.2 pad_add_fusion
  76.3 0.5 copy-done.23
  76.8 0.3 copy-done.15
  77.1 18.7 %near_own.1._.refs_6_ = f32[24,64,128]{2,1,0:T(8,128)S(1)} custom-call(s32[2]{0:T(128)S(1)} %get-tuple-element.17.refs_0_, s32[688]{0:T(1024)S(1)} %get-tuple-element.18.refs_1_, bf16[24,32,128]{2,1,0:T(8,128)(2,1)S(1)} %get-tuple-element.19.refs_2_, bf16[128,1024]{1,0:T(8,128)(2,1)S(1)} %copy-done.15, bf16[24,80,128]{2,1,0:T(8,128)(2,1)} %get-tuple-element.20.refs_4_), custom_call_target="tpu_custom_call" | custom-call | flops 4194304000 | bytes 2097152 | tf_op jit(solution)/shard_map/near_own/pallas_call | solution.py:238
  95.8 1.5 coarse_low.1
  97.3 39.0 %all-gather.1 = bf16[32,32,128]{2,1,0:T(8,128)(2,1)S(1)} all-gather(bf16[2,32,128]{2,1,0:T(8,128)(2,1)S(1)} %get-tuple-element.21), channel_id=3, replica_groups={{0,32,64,96,128,160,192,224,256,288,320,352,384,416,448,480},{1,33,65,9..., dimensions={0}, use_global_device_ids=true | all-gather | bytes 278528 | tf_op jit(solution)/shard_map/all_gather | solution.py:459
  136.3 0.1 pad_add_fusion.2.up
  136.5 0.6 copy-done.21
  137.1 0.6 copy-done.22
  137.7 0.1 copy.27
  137.9 4.7 %couple_levels.1 = (f32[24,64,64]{2,1,0:T(8,128)S(1)}, f32[6,64,64]{2,1,0:T(8,128)S(1)}) custom-call(s32[24,16]{1,0:T(8,128)S(1)} %shift-left_or_fusion.codes, s32[6,8]{1,0:T(8,128)S(1)} %shift-left_or_fusion.1.box_codes, bf16[32,64,64]{2,1,0:T(8,128)(2,1)S(1)} %copy-done.11, bf16[32,64,64]{2,1,0:T(8,128)(2,1)S(1)} %copy-done.12, ...), custom_call_target="tpu_custom_call" | custom-call | flops 1073741824 | bytes 1048576 | tf_op jit(solution)/shard_map/couple_levels/pallas_call | solution.py:347
  142.6 35.8 %near_halo.1.near_part = f32[24,64,128]{2,1,0:T(8,128)S(1)} custom-call(s32[2]{0:T(128)S(1)} %get-tuple-element.17.refs_0_, s32[688]{0:T(1024)S(1)} %get-tuple-element.26.refs_1_, bf16[24,32,128]{2,1,0:T(8,128)(2,1)S(1)} %copy-done.14, bf16[128,1024]{1,0:T(8,128)(2,1)S(1)} %copy-done.16, bf16[24,80,128]{2,1,0:T(8,128)(2,1)} %collective-permute-done.2.refs_4_, ...), custom_call_target="tpu_custom_call" | custom-call | flops 8388608000 | bytes 2097152 | tf_op jit(solution)/shard_map/near_halo/pallas_call | solution.py:238
  178.5 0.6 copy-done.10
  179.1 4.1 %group_to_points.1 = f32[64,3072]{1,0:T(8,128)} custom-call(s32[1]{0:T(128)} %bitcast.place, bf16[16,2,32,128]{3,2,1,0:T(8,128)(2,1)S(1)} %bitcast.5, bf16[4,2,128,128]{3,2,1,0:T(8,128)(2,1)S(1)} %pad_add_fusion.2.up, bf16[4,2,128,128]{3,2,1,0:T(8,128)(2,1)S(1)} %get-tuple-element.36.coupling, bf16[4,2,128,128]{3,2,1,0:T(8,128)(2,1)S(1)} %get-tuple-element.35.down, ...), custom_call_target="tpu_custom_call" | custom-call | tf_op jit(solution)/shard_map/group_to_points/pallas_call | solution.py:384
  (48 shorter events, 0.3 us)
Async XLA Ops:
  0.0 1.0 copy-start
  1.0 0.8 copy-start.8
  1.8 11.7 %copy-start.1 = (bf16[64,3072]{1,0:T(8,128)(2,1)S(1)}, bf16[64,3072]{1,0:T(8,128)(2,1)}, u32[]{:S(2)}) copy-start(bf16[64,3072]{1,0:T(8,128)(2,1)} %charges.3) | copy-start | bytes 1179652
  1.8 11.7 %copy-start.6 = (bf16[6,64,64]{2,1,0:T(8,128)(2,1)S(1)}, bf16[6,64,64]{2,1,0:T(8,128)(2,1)}, u32[]{:S(2)}) copy-start(bf16[6,64,64]{2,1,0:T(8,128)(2,1)} %box_up.1) | copy-start | bytes 147460
  2.9 73.9 %copy-start.13 = (bf16[24,32,128]{2,1,0:T(8,128)(2,1)}, bf16[24,32,128]{2,1,0:T(8,128)(2,1)S(1)}, u32[]{:S(2)}) copy-start(bf16[24,32,128]{2,1,0:T(8,128)(2,1)S(1)} %get-tuple-element.19.refs_2_) | copy-start | bytes 589828
  2.9 139.6 %collective-permute-start.2 = (bf16[24,80,128]{2,1,0:T(8,128)(2,1)}, bf16[24,80,128]{2,1,0:T(8,128)(2,1)}, u32[]{:S(2)}, u32[]{:S(2)}) collective-permute-start(bf16[24,80,128]{2,1,0:T(8,128)(2,1)} %get-tuple-element.20.refs_4_), channel_id=1, source_target_pairs={{0,1},{1,2},{2,3},{3,4},{4,5},{5,6},{6,7},{7,8},{8,9},{9,10},{10,1... | collective-permute-start | bytes 1474568 | tf_op jit(solution)/shard_map/ppermute | solution.py:402
  6.4 136.2 %collective-permute-start.3 = (bf16[24,80,128]{2,1,0:T(8,128)(2,1)}, bf16[24,80,128]{2,1,0:T(8,128)(2,1)}, u32[]{:S(2)}, u32[]{:S(2)}) collective-permute-start(bf16[24,80,128]{2,1,0:T(8,128)(2,1)} %get-tuple-element.20.refs_4_), channel_id=1, source_target_pairs={{1,0},{2,1},{3,2},{4,3},{5,4},{6,5},{7,6},{8,7},{9,8},{10,9},{11,1... | collective-permute-start | bytes 1474568 | tf_op jit(solution)/shard_map/ppermute | solution.py:403
  13.5 1.0 copy-start.2
  14.5 1.0 copy-start.4
  15.5 0.7 copy-start.9
  22.7 51.2 %copy-start.18 = (bf16[8,2,64,64]{3,2,1,0:T(8,128)(2,1)S(1)}, bf16[8,2,64,64]{3,2,1,0:T(8,128)(2,1)}, u32[]{:S(2)}) copy-start(bf16[8,2,64,64]{3,2,1,0:T(8,128)(2,1)} %param.30) | copy-start | bytes 393220
  22.7 115.1 %collective-permute-start = (bf16[15,64,128]{2,1,0:T(8,128)(2,1)}, bf16[15,64,128]{2,1,0:T(8,128)(2,1)}, u32[]{:S(2)}, u32[]{:S(2)}) collective-permute-start(bf16[15,64,128]{2,1,0:T(8,128)(2,1)} %get-tuple-element.23.mine), channel_id=1, source_target_pairs={{0,1},{1,2},{2,3},{3,4},{4,5},{5,6},{6,7},{7,8},{8,9},{9,10},{10,1... | collective-permute-start | bytes 737288 | tf_op jit(solution)/shard_map/ppermute | solution.py:402
  24.7 113.1 %collective-permute-start.1 = (bf16[15,64,128]{2,1,0:T(8,128)(2,1)}, bf16[15,64,128]{2,1,0:T(8,128)(2,1)}, u32[]{:S(2)}, u32[]{:S(2)}) collective-permute-start(bf16[15,64,128]{2,1,0:T(8,128)(2,1)} %get-tuple-element.23.mine), channel_id=1, source_target_pairs={{1,0},{2,1},{3,2},{4,3},{5,4},{6,5},{7,6},{8,7},{9,8},{10,9},{11,1... | collective-permute-start | bytes 737288 | tf_op jit(solution)/shard_map/ppermute | solution.py:403
  73.8 1.0 copy-start.19
  74.8 1.0 copy-start.20
  76.1 0.7 copy-start.23
  76.1 0.7 copy-start.24
  76.1 1.0 copy-start.15
  95.8 40.5 %copy-start.17 = (bf16[4,2,64,64]{3,2,1,0:T(8,128)(2,1)S(1)}, bf16[4,2,64,64]{3,2,1,0:T(8,128)(2,1)}, u32[]{:S(2)}) copy-start(bf16[4,2,64,64]{3,2,1,0:T(8,128)(2,1)} %get-tuple-element.31) | copy-start | bytes 196612
  95.8 42.0 %copy-start.12 = (bf16[32,64,64]{2,1,0:T(8,128)(2,1)S(1)}, bf16[32,64,64]{2,1,0:T(8,128)(2,1)}, u32[]{:S(2)}) copy-start(bf16[32,64,64]{2,1,0:T(8,128)(2,1)} %box_matrices.1) | copy-start | bytes 786436
  97.3 40.6 %copy-start.11 = (bf16[32,64,64]{2,1,0:T(8,128)(2,1)S(1)}, bf16[32,64,64]{2,1,0:T(8,128)(2,1)}, u32[]{:S(2)}) copy-start(bf16[32,64,64]{2,1,0:T(8,128)(2,1)} %matrices.1) | copy-start | bytes 786436
  136.3 0.7 copy-start.21
  137.0 0.7 copy-start.22
  137.8 4.7 %copy-start.14 = (bf16[24,32,128]{2,1,0:T(8,128)(2,1)S(1)}, bf16[24,32,128]{2,1,0:T(8,128)(2,1)}, u32[]{:S(2)}) copy-start(bf16[24,32,128]{2,1,0:T(8,128)(2,1)} %copy-done.13) | copy-start | bytes 589828
  137.9 4.7 %copy-start.16 = (bf16[128,1024]{1,0:T(8,128)(2,1)S(1)}, bf16[128,1024]{1,0:T(8,128)(2,1)}, u32[]{:S(2)}) copy-start(bf16[128,1024]{1,0:T(8,128)(2,1)} %constant.15.clone.refs_3_) | copy-start | bytes 786436
  142.6 35.8 %copy-start.3 = (bf16[64,3072]{1,0:T(8,128)(2,1)S(1)}, bf16[64,3072]{1,0:T(8,128)(2,1)}, u32[]{:S(2)}) copy-start(bf16[64,3072]{1,0:T(8,128)(2,1)} %basis.3) | copy-start | bytes 1179652
  142.6 35.8 %copy-start.5 = (bf16[24,64,64]{2,1,0:T(8,128)(2,1)S(1)}, bf16[24,64,64]{2,1,0:T(8,128)(2,1)}, u32[]{:S(2)}) copy-start(bf16[24,64,64]{2,1,0:T(8,128)(2,1)} %leaf_down.1) | copy-start | bytes 589828
  142.6 35.8 %copy-start.7 = (bf16[6,64,64]{2,1,0:T(8,128)(2,1)S(1)}, bf16[6,64,64]{2,1,0:T(8,128)(2,1)}, u32[]{:S(2)}) copy-start(bf16[6,64,64]{2,1,0:T(8,128)(2,1)} %box_down.1) | copy-start | bytes 147460
  178.4 0.7 copy-start.10

commit v2 on v1

v2 whole, which is shorter than its diff:
```python
import math

import jax
import jax.numpy as jnp
import numpy as np
from jax import lax
from jax.experimental import pallas as pl
from jax.experimental.pallas import tpu as pltpu
from jax.sharding import PartitionSpec as P

BF = jnp.bfloat16
F32 = jnp.float32
AXES = ("box", "rhs")

R = 64
K = 64
M = 128
LD = 24
BX = 6
ADM = 16
ADMB = 8
NEAR = 27
FR = 16
ROWS = R + FR
FX = 32
UNROLL = 8
PAIRS = (LD + BX) // 2
SENT = LD + PAIRS * R // ROWS
SLOTS = LD * (NEAR + 1) + 2 * UNROLL

DELTA2 = 0.0001
INV_SCALE = 2.0 * math.sqrt(NEAR * M)
CENTRE = 1.1

PARTS = ((0, 0), (0, 1), (0, 2), (1, 0), (1, 1), (1, 2), (2, 0), (2, 1))

VMEM = pl.BlockSpec(memory_space=pltpu.VMEM)
SMEM = pl.BlockSpec(memory_space=pltpu.SMEM)
ANY = pl.BlockSpec(memory_space=pl.ANY)


def params():
    return pltpu.CompilerParams(vmem_limit_bytes=24 * 1024 * 1024)


def sds(shape, dtype):
    return jax.ShapeDtypeStruct(shape, dtype)


def dot(a, b):
    return jnp.dot(a, b, preferred_element_type=F32)


def dot_nt(a, b):
    return lax.dot_general(a, b, (((1,), (1,)), ((), ())), preferred_element_type=F32)


def dot2(x, m):
    hi = x.astype(BF)
    lo = (x - hi.astype(F32)).astype(BF)
    return dot(hi, m) + dot(lo, m)


def expansion():
    out = np.zeros((8 * FR, 8, M), np.float32)
    for leaf in range(8):
        e = 0
        for a, _ in PARTS:
            for c in range(3):
                out[FR * leaf + 3 * a + c, leaf, e] = 1.0
                e += 1
        for c in range(3):
            out[FR * leaf + 9 + c, leaf, e] = 1.0
            e += 1
        for c in range(3):
            out[FR * leaf + 12, leaf, e] = 1.0
            e += 1
    return out.reshape(8 * FR, 8 * M)


def split3(x):
    hi = x.astype(BF).astype(F32)
    rest = x - hi
    mid = rest.astype(BF).astype(F32)
    return hi, mid, rest - mid


def load(copies):
    for copy in copies:
        copy.start()
    return copies


def first_body(charges_in, points_in, basis_in, leaf_up_in, box_up_in, parents, code, sent, target, ascent, own, left, right, sizes, charges, points, basis, leaf_up, box_up, feat, wide, acc, sems):
    moves = ((points_in, points), (charges_in, charges), (basis_in, basis), (leaf_up_in, leaf_up), (box_up_in, box_up))
    copies = load([pltpu.make_async_copy(a, b, sems.at[n]) for n, (a, b) in enumerate(moves)])
    acc[...] = jnp.zeros(acc.shape, F32)
    copies[1].wait()
    copies[2].wait()
    copies[3].wait()
    lists = (own, left, right)
    at = [jnp.int32(0)] * 3
    for group in range(LD // 8):
        leaves = range(8 * group, 8 * group + 8)
        c = [dot_nt(charges[:, pl.ds(leaf * M, M)], basis[:, pl.ds(leaf * M, M)]) for leaf in leaves]
        raised = [dot(c[i].astype(BF), leaf_up[leaf]) for i, leaf in enumerate(leaves)]
        for leaf in leaves:
            for s in range(NEAR):
                x = code[leaf, s]
                for n in range(3):
                    lists[n][at[n]] = x
                    at[n] = at[n] + ((x >> (16 + n)) & 1)
            for n in range(3):
                lists[n][at[n]] = leaf << 8 | LD
                at[n] = (at[n] + 1) & -2
        for i in range(0, 8, 2):
            put_coef(sent, (8 * group + i) // 2, jnp.concatenate([c[i], c[i + 1]], axis=1).astype(BF))
        for i, leaf in enumerate(leaves):
            acc[parents[leaf]] += raised[i]
    for n in range(3):
        for i in range(2 * UNROLL):
            lists[n][at[n] + i] = LD << 8 | LD
        sizes[n] = (at[n] // 2 + UNROLL - 1) // UNROLL
    copies[4].wait()
    copies[0].wait()
    boxes = [acc[box] for box in range(BX)]
    raised = [dot(boxes[box].astype(BF), box_up[box]) for box in range(BX)]
    ascent[...] = (raised[0] + raised[1] + (raised[2] + raised[3]) + (raised[4] + raised[5])).astype(BF)
    for box in range(0, BX, 2):
        put_coef(sent, (LD + box) // 2, jnp.concatenate([boxes[box], boxes[box + 1]], axis=1).astype(BF))

    p = (points[...] - CENTRE) * INV_SCALE
    parts = split3(p)
    norm = p[0:1] * p[0:1] + p[1:2] * p[1:2] + p[2:3] * p[2:3]
    source_norm = split3(norm)
    target_norm = split3(norm + DELTA2 * INV_SCALE * INV_SCALE)
    feat[...] = jnp.zeros(feat.shape, F32)
    wide[...] = jnp.zeros(wide.shape, F32)
    one = jnp.ones(norm.shape, F32)
    for a in range(3):
        feat[3 * a : 3 * a + 3, :] = parts[a]
        feat[9 + a : 10 + a, :] = source_norm[a]
    feat[12:13, :] = one
    for n, (_, b) in enumerate(PARTS):
        wide[3 * n : 3 * n + 3, :] = -2.0 * parts[b]
    base = 3 * len(PARTS)
    for a in range(3):
        wide[base + a : base + a + 1, :] = one
        wide[base + 3 + a : base + 4 + a, :] = target_norm[a]
    turned = []
    for o in range(LD // 8):
        rows = jnp.concatenate([feat[:, pl.ds((8 * o + i) * M, M)] for i in range(8)], axis=0)
        turned.append(rows.T.astype(BF))
    for leaf in range(LD):
        cols = pl.ds(leaf * M, M)
        sent[leaf, 0:R, :] = charges[:, cols]
        i = leaf % 8
        sent[leaf, R:ROWS, :] = turned[leaf // 8][FR * i : FR * (i + 1), :]
        target[leaf, :, :] = wide[:, cols].astype(BF)


def coef_places(pair):
    rows = [pair * R + 16 * i for i in range(R // 16)]
    return [(r // ROWS, r % ROWS) for r in rows]


def put_coef(sent, pair, value):
    for i, (block, row) in enumerate(coef_places(pair)):
        sent[LD + block, row : row + 16, :] = value[16 * i : 16 * i + 16]


def first(charges, points, basis, leaf_up, box_up, parents, code):
    return pl.pallas_call(
        first_body,
        in_specs=[ANY] * 5 + [SMEM, SMEM],
        out_specs=[VMEM] * 3 + [SMEM] * 4,
        out_shape=[
            sds((SENT, ROWS, M), BF),
            sds((LD, FX, M), BF),
            sds((R, K), BF),
            sds((SLOTS,), jnp.int32),
            sds((SLOTS,), jnp.int32),
            sds((SLOTS,), jnp.int32),
            sds((3,), jnp.int32),
        ],
        scratch_shapes=[
            pltpu.VMEM((R, LD * M), BF),
            pltpu.VMEM((3, LD * M), F32),
            pltpu.VMEM((K, LD * M), BF),
            pltpu.VMEM((LD, K, K), BF),
            pltpu.VMEM((BX, K, K), BF),
            pltpu.VMEM((FR, LD * M), F32),
            pltpu.VMEM((FX, LD * M), F32),
            pltpu.VMEM((BX, R, K), F32),
            pltpu.SemaphoreType.DMA((5,)),
        ],
        compiler_params=params(),
        name="points_to_group",
    )(charges, points, basis, leaf_up, box_up, parents, code)


def near_body(which, sizes, slots, target, expand, source, *rest):
    if which:
        start_from, _, acc, table, feats, sem = rest
    else:
        _, acc, table, feats, sem = rest
    copy = pltpu.make_async_copy(source.at[pl.ds(0, LD)], table.at[pl.ds(0, LD)], sem)
    copy.start()
    if which:
        acc[...] = start_from[...]
    else:
        acc[...] = jnp.zeros(acc.shape, F32)
    table[LD] = jnp.zeros((ROWS, M), BF)
    lane = lax.broadcasted_iota(jnp.int32, (M, M), 1)
    ones = 3 * len(PARTS) + 3
    feats[LD] = jnp.where((lane >= ones) & (lane < ones + 3), 1.0, 0.0).astype(BF)
    copy.wait()
    for o in range(LD // 8):
        rows = jnp.concatenate([table[8 * o + i, R:ROWS, :] for i in range(8)], axis=0)
        spread = dot(rows, expand[...]).astype(BF)
        for i in range(8):
            feats[8 * o + i] = spread[:, M * i : M * (i + 1)]
    pad = jnp.zeros((M - FX, M), BF)

    def step(it, _):
        t, kernels, weights = [], [], []
        for u in range(UNROLL):
            at = (it * UNROLL + u) * 2
            first, second = slots[at], slots[at + 1]
            s0, s1 = first & 255, second & 255
            t.append((first >> 8) & 255)
            rows = jnp.concatenate([feats[s0], feats[s1]], axis=0)
            square = dot(rows, jnp.concatenate([target[jnp.minimum(t[u], LD - 1)], pad], axis=0))
            kernels.append(lax.rsqrt(square).astype(BF))
            weights.append(jnp.concatenate([table[s0, 0:R, :], table[s1, 0:R, :]], axis=1))
        terms = [dot(weights[u], kernels[u]) for u in range(UNROLL)]
        for u in range(UNROLL):
            acc[t[u]] += terms[u]
        return 0

    lax.fori_loop(0, sizes[which], step, 0)


def near(which, sizes, slots, target, expand, source, extra):
    pairs = 100
    return pl.pallas_call(
        lambda *refs: near_body(which, *refs),
        in_specs=[SMEM, SMEM, VMEM, VMEM, ANY] + ([VMEM, ANY] if which else [ANY]),
        out_specs=VMEM,
        out_shape=sds((LD + 1, R, M), F32),
        scratch_shapes=[
            pltpu.VMEM((LD + 1, ROWS, M), BF),
            pltpu.VMEM((LD + 1, M, M), BF),
            pltpu.SemaphoreType.DMA,
        ],
        compiler_params=params(),
        cost_estimate=pl.CostEstimate(
            flops=pairs * 2 * 256 * 128 * 320, bytes_accessed=2 << 20, transcendentals=pairs << 15
        ),
        name=("near_own", "near_left", "near_right")[which],
    )(sizes, slots, target, expand, source, *extra)


def bottom_body(place, mine, one, two, three, up, coupling, pair, field, held):
    q = place[0] & 3
    for k, ref in enumerate((mine, one, two, three)):
        held[q ^ k] = ref[...]
    left = jnp.concatenate([held[0], held[2]], axis=0)
    right = jnp.concatenate([held[1], held[3]], axis=0)
    raised = dot(left, up[0, 0]) + dot(right, up[0, 1])
    field[0] = dot(held[q ^ 2], coupling[0, 0]) + dot(held[q ^ 3], coupling[0, 1])
    pair[...] = raised.astype(BF).reshape(2, R, K)


def level_body(h, place, mine, one, two, three, up, coupling, _, pair, field, held, above):
    q = place[0] >> h
    s = (q >> 1) & 3
    for k, ref in enumerate((mine, one, two, three)):
        held[pl.ds(2 * (s ^ k), 2)] = ref[...]
    left = jnp.concatenate([held[2 * i] for i in range(4)], axis=0)
    right = jnp.concatenate([held[2 * i + 1] for i in range(4)], axis=0)
    raised = dot(left, up[h, 0]) + dot(right, up[h, 1])
    far = (q & 7) ^ 2
    low_field = dot(held[far], coupling[h, 0]) + dot(held[far ^ 1], coupling[h, 1])
    left = jnp.concatenate([raised[0:R], raised[2 * R : 3 * R]], axis=0)
    right = jnp.concatenate([raised[R : 2 * R], raised[3 * R :]], axis=0)
    top = dot2(left, up[h + 1, 0]) + dot2(right, up[h + 1, 1])
    above[...] = raised.reshape(4, R, K)
    pair[...] = top.astype(BF).reshape(2, R, K)
    field[0] = low_field
    far = s ^ 2
    field[1] = dot2(above[far], coupling[h + 1, 0]) + dot2(above[far ^ 1], coupling[h + 1, 1])


def level(h, place, mine, others, up, coupling, order):
    bottom = h < 0
    out = pl.pallas_call(
        bottom_body if bottom else lambda *refs: level_body(h, *refs),
        in_specs=[SMEM] + [VMEM] * 6 + ([] if bottom else [ANY]),
        out_specs=[VMEM, VMEM],
        out_shape=[sds((2, R, K), BF), sds((1 if bottom else 2, R, K), F32)],
        scratch_shapes=[pltpu.VMEM((4, R, K), BF)]
        if bottom
        else [pltpu.VMEM((8, R, K), BF), pltpu.VMEM((4, R, K), F32)],
        compiler_params=params(),
        name="coarse_levels",
    )
    return out(place, mine, *others, up, coupling, *order)


def couple_body(codes, box_codes, place, matrices, box_matrices, f0, f12, f34, f56, down, coupling, left, mine, right, leaf_field, box_field, base, tip, table, low, high, sems):
    blocks = SENT - LD
    copies = load(
        [
            pltpu.make_async_copy(src.at[pl.ds(LD, blocks)], table.at[pl.ds(n * blocks, blocks)], sems.at[n])
            for n, src in enumerate((left, mine, right))
        ]
    )
    me = place[0]
    fields = (f0[0], f12[0], f12[1], f34[0], f34[1], f56[0], f56[1])
    total = fields[6]
    chain = down[6, (me >> 6) & 1].astype(F32)
    for h in range(5, -1, -1):
        both = dot2(jnp.concatenate([total, chain], axis=0), down[h, (me >> h) & 1])
        total = fields[h] + both[:R]
        chain = both[R:]
    chain_high = chain.astype(BF)
    chain_low = (chain - chain_high.astype(F32)).astype(BF)
    for i in range(2):
        product = dot(coupling[7, i], chain_high) + dot(coupling[7, i], chain_low)
        upper = product.astype(BF)
        tip[i, 0] = upper
        tip[i, 1] = (product - upper.astype(F32)).astype(BF)
    base[...] = total
    for copy in copies:
        copy.wait()
    first = lax.broadcasted_iota(jnp.int32, (R, 2 * K), 1) < K
    for n in range(3):
        for group in range(PAIRS // 5):
            ready = []
            for i in range(5 * group, 5 * group + 5):
                x = jnp.concatenate(
                    [table[n * blocks + b, r : r + 16, :] for b, r in coef_places(i)], axis=0
                ).astype(F32)
                y = pltpu.roll(x, K, 1)
                ready.append(
                    [
                        jnp.where(first, x, 0.0).astype(BF),
                        jnp.where(first, y, 0.0).astype(BF),
                        jnp.where(first, 0.0, y).astype(BF),
                        jnp.where(first, 0.0, x).astype(BF),
                    ]
                )
            for i in range(5):
                at = 2 * (n * PAIRS + 5 * group + i)
                low[at], low[at + 1], high[at], high[at + 1] = ready[i]

    def gather(codes, row, mats, width):
        total = jnp.zeros((R, K), F32)
        for g in range(width // 4):
            c = [codes[row, 4 * g + i] for i in range(4)]
            s = [x & 255 for x in c]
            vec = jnp.concatenate([low[s[0]] + high[s[1]], low[s[2]] + high[s[3]]], axis=1)
            mat = jnp.concatenate([mats[x >> 8] for x in c], axis=0)
            total = total + dot(vec, mat)
        return total

    def step(it, _):
        rows = [it * 8 + u for u in range(8)]
        got = [gather(codes, row, matrices, ADM) for row in rows]
        for row, value in zip(rows, got):
            leaf_field[row] = value
        return 0

    lax.fori_loop(0, LD // 8, step, 0)
    got = [gather(box_codes, box, box_matrices, ADMB) for box in range(BX)]
    for box in range(BX):
        box_field[box] = got[box]


def couple(codes, box_codes, place, matrices, box_matrices, fields, down, coupling, sents):
    return pl.pallas_call(
        couple_body,
        in_specs=[SMEM] * 3 + [VMEM] * 8 + [ANY] * 3,
        out_specs=[VMEM] * 4,
        out_shape=[
            sds((LD, R, K), F32),
            sds((BX, R, K), F32),
            sds((R, K), F32),
            sds((2, 2, K, K), BF),
        ],
        scratch_shapes=[
            pltpu.VMEM((3 * (SENT - LD), ROWS, M), BF),
            pltpu.VMEM((6 * PAIRS, R, 2 * K), BF),
            pltpu.VMEM((6 * PAIRS, R, 2 * K), BF),
            pltpu.SemaphoreType.DMA((3,)),
        ],
        compiler_params=params(),
        cost_estimate=pl.CostEstimate(flops=1 << 30, bytes_accessed=1 << 20, transcendentals=0),
        name="couple_levels",
    )(codes, box_codes, place, matrices, box_matrices, *fields, down, coupling, *sents)


def final_body(place, other, base, tip, parents, leaf_field, box_field, box_down, leaf_down, basis, near_part, out, boxes):
    q = (place[0] >> 7) & 1
    total = base[...]
    for i in range(2):
        node = other[q ^ i]
        total = total + (dot(node, tip[i, 0]) + dot(node, tip[i, 1]))
    group = total.astype(BF)
    got = [(box_field[box] + dot(group, box_down[box])).astype(BF) for box in range(BX)]
    for box in range(BX):
        boxes[box] = got[box]
    for part in range(LD // 8):
        leaves = range(8 * part, 8 * part + 8)
        field = [
            (leaf_field[leaf] + dot(boxes[parents[leaf]], leaf_down[leaf])).astype(BF) for leaf in leaves
        ]
        got = [
            near_part[leaf] + dot(field[i], basis[:, pl.ds(leaf * M, M)]) for i, leaf in enumerate(leaves)
        ]
        for i, leaf in enumerate(leaves):
            out[:, pl.ds(leaf * M, M)] = got[i]


def finish(place, other, base, tip, parents, fields, box_down, leaf_down, basis, near_part):
    return pl.pallas_call(
        final_body,
        in_specs=[SMEM] + [VMEM] * 3 + [SMEM] + [VMEM] * 6,
        out_specs=VMEM,
        out_shape=sds((R, LD * M), F32),
        scratch_shapes=[pltpu.VMEM((BX, R, K), BF)],
        compiler_params=params(),
        name="group_to_points",
    )(place, other, base, tip, parents, *fields, box_down, leaf_down, basis, near_part)


def exchange(x):
    count = lax.axis_size(AXES)
    left = lax.ppermute(x, AXES, [(i, i + 1) for i in range(count - 1)])
    right = lax.ppermute(x, AXES, [(i + 1, i) for i in range(count - 1)])
    return left, right


def partners(x, bit, ways):
    count = lax.axis_size(AXES)
    return [lax.ppermute(x, AXES, [(i, i ^ (k << bit)) for i in range(count)]) for k in range(1, ways)]


def local(
    charges,
    points,
    leaf_basis,
    leaf_parent,
    leaf_up,
    leaf_down,
    box_up,
    box_down,
    top_up,
    top_down,
    top_coupling,
    leaf_sources,
    leaf_classes,
    leaf_coupling,
    box_sources,
    box_classes,
    box_coupling,
    near_leaves,
    near_count,
):
    device = lax.axis_index(AXES)
    place = device.astype(jnp.int32).reshape(1)
    parents = leaf_parent[0]

    rel = near_leaves - device * LD
    used = jnp.arange(NEAR, dtype=jnp.int32)[None, :] < near_count[:, None]
    side = jnp.where(rel < 0, 2, jnp.where(rel < LD, 1, 4))
    row = rel + jnp.where(rel < 0, LD, jnp.where(rel < LD, 0, -LD))
    leaf_ids = jnp.arange(LD, dtype=jnp.int32)[:, None]
    code = row | leaf_ids << 8 | jnp.where(used, side, 0) << 16

    sent, target, ascent, own, left, right, sizes = first(
        charges, points, leaf_basis, leaf_up, box_up, parents, code
    )
    expand = jnp.asarray(expansion(), BF)

    pair, f0 = level(-1, place, ascent, partners(ascent, 0, 4), top_up, top_coupling, ())
    sent_left, sent_right = exchange(sent)
    others = partners(pair, 2, 4)
    near_part = near(0, sizes, own, target, expand, sent, (f0,))
    pair, f12 = level(1, place, pair, others, top_up, top_coupling, (near_part,))
    others = partners(pair, 4, 4)
    near_part = near(1, sizes, left, target, expand, sent_left, (near_part, f12))
    pair, f34 = level(3, place, pair, others, top_up, top_coupling, (near_part,))
    others = partners(pair, 6, 4)
    near_part = near(2, sizes, right, target, expand, sent_right, (near_part, f34))
    pair, f56 = level(5, place, pair, others, top_up, top_coupling, (near_part,))
    (other,) = partners(pair, 8, 2)

    def table_row(sources, classes, width, start):
        rel = sources - (device - 1) * width
        block = (rel >= width).astype(jnp.int32) + (rel >= 2 * width).astype(jnp.int32)
        return rel + block * (2 * PAIRS - width) + start | classes << 8

    codes = table_row(leaf_sources, leaf_classes, LD, 0)
    box_codes = table_row(box_sources, box_classes, BX, LD)
    leaf_field, box_field, base, tip = couple(
        codes,
        box_codes,
        place,
        leaf_coupling,
        box_coupling,
        (f0, f12, f34, f56),
        top_down,
        top_coupling,
        (sent_left, sent, sent_right),
    )
    return finish(
        place, other, base, tip, parents, (leaf_field, box_field), box_down, leaf_down, leaf_basis, near_part
    )


def solution(mesh):
    split = P(AXES)
    return jax.shard_map(
        local,
        mesh=mesh,
        in_specs=(
            P(None, AXES),
            P(None, AXES),
            P(None, AXES),
            split,
            split,
            split,
            split,
            split,
            P(),
            P(),
            P(),
            split,
            split,
            P(),
            split,
            split,
            P(),
            split,
            split,
        ),
        out_specs=P(None, AXES),
        check_vma=False,
    )
```

time: 184 us -> 113 us (0.61)
  the two profiles are of different devices: /device:TPU:32 before, /device:TPU:4 now
where the time goes in v2:
time: 113 us; the launch traced here: 112 us
  starting transfers between devices  65.3 us (58%)
  Pallas kernels  34.1 us (30%)
  local copies, waits for them, and re-layouts  6.93 us (6%)
  waiting for transfers between devices  5.13 us (5%)
    ppermute x13, starting transfers between devices, partners(): lax.ppermute(x, AXES, [(i, i ^ k << bit) for i in range(count)])  58.5 us
    pallas_call x3, Pallas kernels, near(): pl.pallas_call(lambda *refs: near_body(which, *refs), in_specs=[SMEM, SME...  19.3 us
    unnamed x44, local copies, waits for them, and re-layouts  6.93 us
    pallas_call x1, Pallas kernels, first(): pl.pallas_call(first_body, in_specs=[ANY] * 5 + [SMEM, SMEM], out_specs=[...  5.83 us
    pallas_call x1, Pallas kernels, couple(): pl.pallas_call(couple_body, in_specs=[SMEM] * 3 + [VMEM] * 8 + [ANY] * 3,...  5.29 us
    ppermute x13, waiting for transfers between devices, partners(): lax.ppermute(x, AXES, [(i, i ^ k << bit) for i in range(count)])  5.12 us
    ppermute x1, starting transfers between devices, exchange(): left = lax.ppermute(x, AXES, [(i, i + 1) for i in range(count - 1)])  3.48 us
    ppermute x1, starting transfers between devices, exchange(): right = lax.ppermute(x, AXES, [(i + 1, i) for i in range(count - 1)])  3.35 us
  transfers between devices with their start and end apart: 15, of which 2 were waited for; matrix products, arithmetic and copies ran while one was open for 0% of the time, Pallas kernels for 23%

profile of v2, /device:TPU:4, one launch (start us, length us, event | category | flops | bytes accessed | tf_op | source)
XLA Modules:
  0.0 112.0 jit_solution(17772456821559879076)
XLA Ops:
  0.0 0.7 copy-done.15
  0.8 0.7 copy-done.13
  1.4 1.0 copy-done.2
  2.4 1.0 copy-done.6
  3.4 1.0 copy-done.7
  4.4 0.9 copy-done.10
  5.3 0.8 copy-done.12
  6.1 5.8 %points_to_group.1 = (bf16[36,80,128]{2,1,0:T(8,128)(2,1)S(1)}, bf16[24,32,128]{2,1,0:T(8,128)(2,1)S(1)}, bf16[64,64]{1,0:T(8,128)(2,1)S(1)}, s32[688]{0:T(1024)...) custom-call(bf16[64,3072]{1,0:T(8,128)(2,1)S(1)} %copy-done.6, f32[3,3072]{1,0:T(4,128)S(1)} %copy-done.12, ...), custom_call_target="tpu_custom_call" | custom-call | tf_op jit(solution)/shard_map/points_to_group/pallas_call | solution.py:173
  12.0 3.5 %collective-permute-start.9 = (bf16[36,80,128]{2,1,0:T(8,128)(2,1)S(1)}, bf16[36,80,128]{2,1,0:T(8,128)(2,1)S(1)}, u32[]{:S(2)}, u32[]{:S(2)}) collective-permute-start(bf16[36,80,128]{2,1,0:T(8,128)(2,1)S(1)} %get-tuple-element.29.refs_4_.mine), channel_id=1, source_target_pairs={{0,1},{1,2},{2,3},{3,4},{4,5},{5,6},{6,7},{7,8},{8,9},{9,10},{10,1... | collective-permute-start | bytes 2211848 | tf_op jit(solution)/shard_map/ppermute | solution.py:440
  15.5 3.5 %collective-permute-start = (bf16[64,64]{1,0:T(8,128)(2,1)S(1)}, bf16[64,64]{1,0:T(8,128)(2,1)S(1)}, u32[]{:S(2)}, u32[]{:S(2)}) collective-permute-start(bf16[64,64]{1,0:T(8,128)(2,1)S(1)} %get-tuple-element.24.mine), channel_id=1, source_target_pairs={{0,1},{1,0},{2,3},{3,2},{4,5},{5,4},{6,7},{7,6},{8,9},{9,8},{10,11... | collective-permute-start | bytes 24584 | tf_op jit(solution)/shard_map/ppermute | solution.py:447
  19.0 3.2 %collective-permute-start.1 = (bf16[64,64]{1,0:T(8,128)(2,1)S(1)}, bf16[64,64]{1,0:T(8,128)(2,1)S(1)}, u32[]{:S(2)}, u32[]{:S(2)}) collective-permute-start(bf16[64,64]{1,0:T(8,128)(2,1)S(1)} %get-tuple-element.24.mine), channel_id=1, source_target_pairs={{0,2},{1,3},{2,0},{3,1},{4,6},{5,7},{6,4},{7,5},{8,10},{9,11},{10,... | collective-permute-start | bytes 24584 | tf_op jit(solution)/shard_map/ppermute | solution.py:447
  22.2 3.7 %collective-permute-start.2 = (bf16[64,64]{1,0:T(8,128)(2,1)S(1)}, bf16[64,64]{1,0:T(8,128)(2,1)S(1)}, u32[]{:S(2)}, u32[]{:S(2)}) collective-permute-start(bf16[64,64]{1,0:T(8,128)(2,1)S(1)} %get-tuple-element.24.mine), channel_id=1, source_target_pairs={{0,3},{1,2},{2,1},{3,0},{4,7},{5,6},{6,5},{7,4},{8,11},{9,10},{10,... | collective-permute-start | bytes 24584 | tf_op jit(solution)/shard_map/ppermute | solution.py:447
  25.9 3.3 %collective-permute-start.13 = (bf16[36,80,128]{2,1,0:T(8,128)(2,1)S(1)}, bf16[36,80,128]{2,1,0:T(8,128)(2,1)S(1)}, u32[]{:S(2)}, u32[]{:S(2)}) collective-permute-start(bf16[36,80,128]{2,1,0:T(8,128)(2,1)S(1)} %get-tuple-element.29.refs_4_.mine), channel_id=1, source_target_pairs={{1,0},{2,1},{3,2},{4,3},{5,4},{6,5},{7,6},{8,7},{9,8},{10,9},{11,1... | collective-permute-start | bytes 2211848 | tf_op jit(solution)/shard_map/ppermute | solution.py:441
  29.5 0.7 copy-done.18
  30.2 1.6 %collective-permute-done.one = bf16[64,64]{1,0:T(8,128)(2,1)S(1)} collective-permute-done((bf16[64,64]{1,0:T(8,128)(2,1)S(1)}, bf16[64,64]{1,0:T(8,128)(2,1)S(1)}, u32[]{:S(2)}, u32[]{:S(2)}) %collective-permute-start) | collective-permute-done | bytes 8224 | tf_op jit(solution)/shard_map/ppermute | solution.py:447
  31.7 3.5 %collective-permute-done.1.two = bf16[64,64]{1,0:T(8,128)(2,1)S(1)} collective-permute-done((bf16[64,64]{1,0:T(8,128)(2,1)S(1)}, bf16[64,64]{1,0:T(8,128)(2,1)S(1)}, u32[]{:S(2)}, u32[]{:S(2)}) %collective-permute-start.1) | collective-permute-done | bytes 8224 | tf_op jit(solution)/shard_map/ppermute | solution.py:447
  35.5 1.9 %collective-permute-start.3 = (bf16[2,64,64]{2,1,0:T(8,128)(2,1)S(1)}, bf16[2,64,64]{2,1,0:T(8,128)(2,1)S(1)}, u32[]{:S(2)}, u32[]{:S(2)}) collective-permute-start(bf16[2,64,64]{2,1,0:T(8,128)(2,1)S(1)} %get-tuple-element.25.refs_1_), channel_id=1, source_target_pairs={{0,4},{1,5},{2,6},{3,7},{4,0},{5,1},{6,2},{7,3},{8,12},{9,13},{10,... | collective-permute-start | bytes 49160 | tf_op jit(solution)/shard_map/ppermute | solution.py:447
  37.4 3.1 %collective-permute-start.4 = (bf16[2,64,64]{2,1,0:T(8,128)(2,1)S(1)}, bf16[2,64,64]{2,1,0:T(8,128)(2,1)S(1)}, u32[]{:S(2)}, u32[]{:S(2)}) collective-permute-start(bf16[2,64,64]{2,1,0:T(8,128)(2,1)S(1)} %get-tuple-element.25.refs_1_), channel_id=1, source_target_pairs={{0,8},{1,9},{2,10},{3,11},{4,12},{5,13},{6,14},{7,15},{8,0},{9,1},... | collective-permute-start | bytes 49160 | tf_op jit(solution)/shard_map/ppermute | solution.py:447
  40.5 2.6 %collective-permute-start.5 = (bf16[2,64,64]{2,1,0:T(8,128)(2,1)S(1)}, bf16[2,64,64]{2,1,0:T(8,128)(2,1)S(1)}, u32[]{:S(2)}, u32[]{:S(2)}) collective-permute-start(bf16[2,64,64]{2,1,0:T(8,128)(2,1)S(1)} %get-tuple-element.25.refs_1_), channel_id=1, source_target_pairs={{0,12},{1,13},{2,14},{3,15},{4,8},{5,9},{6,10},{7,11},{8,4},{9,5},... | collective-permute-start | bytes 49160 | tf_op jit(solution)/shard_map/ppermute | solution.py:447
  43.1 6.4 %near_own.1.refs_7_.refs_5_ = f32[25,64,128]{2,1,0:T(8,128)S(1)} custom-call(s32[3]{0:T(128)S(1)} %get-tuple-element.26.refs_0_, s32[688]{0:T(1024)S(1)} %get-tuple-element.27.refs_1_, bf16[24,32,128]{2,1,0:T(8,128)(2,1)S(1)} %get-tuple-element.28.refs_2_, bf16[128,1024]{1,0:T(8,128)(2,1)S(1)} %copy-done.14, ...), custom_call_target="tpu_custom_call" | custom-call | flops 2097152000 | bytes 2097152 | tf_op jit(solution)/shard_map/near_own/pallas_call | solution.py:246
  49.9 2.4 %collective-permute-start.6 = (bf16[2,64,64]{2,1,0:T(8,128)(2,1)S(1)}, bf16[2,64,64]{2,1,0:T(8,128)(2,1)S(1)}, u32[]{:S(2)}, u32[]{:S(2)}) collective-permute-start(bf16[2,64,64]{2,1,0:T(8,128)(2,1)S(1)} %get-tuple-element.31.refs_1_), channel_id=1, source_target_pairs={{0,16},{1,17},{2,18},{3,19},{4,20},{5,21},{6,22},{7,23},{8,24},{9,... | collective-permute-start | bytes 49160 | tf_op jit(solution)/shard_map/ppermute | solution.py:447
  52.3 2.4 %collective-permute-start.7 = (bf16[2,64,64]{2,1,0:T(8,128)(2,1)S(1)}, bf16[2,64,64]{2,1,0:T(8,128)(2,1)S(1)}, u32[]{:S(2)}, u32[]{:S(2)}) collective-permute-start(bf16[2,64,64]{2,1,0:T(8,128)(2,1)S(1)} %get-tuple-element.31.refs_1_), channel_id=1, source_target_pairs={{0,32},{1,33},{2,34},{3,35},{4,36},{5,37},{6,38},{7,39},{8,40},{9,... | collective-permute-start | bytes 49160 | tf_op jit(solution)/shard_map/ppermute | solution.py:447
  54.8 5.9 %collective-permute-start.8 = (bf16[2,64,64]{2,1,0:T(8,128)(2,1)S(1)}, bf16[2,64,64]{2,1,0:T(8,128)(2,1)S(1)}, u32[]{:S(2)}, u32[]{:S(2)}) collective-permute-start(bf16[2,64,64]{2,1,0:T(8,128)(2,1)S(1)} %get-tuple-element.31.refs_1_), channel_id=1, source_target_pairs={{0,48},{1,49},{2,50},{3,51},{4,52},{5,53},{6,54},{7,55},{8,56},{9,... | collective-permute-start | bytes 49160 | tf_op jit(solution)/shard_map/ppermute | solution.py:447
  60.7 6.0 %near_left.1.refs_7_.refs_5_ = f32[25,64,128]{2,1,0:T(8,128)S(1)} custom-call(s32[3]{0:T(128)S(1)} %get-tuple-element.26.refs_0_, s32[688]{0:T(1024)S(1)} %get-tuple-element.32.refs_1_, bf16[24,32,128]{2,1,0:T(8,128)(2,1)S(1)} %get-tuple-element.28.refs_2_, bf16[128,1024]{1,0:T(8,128)(2,1)S(1)} %copy-done.14, ...), custom_call_target="tpu_custom_call" | custom-call | flops 2097152000 | bytes 2097152 | tf_op jit(solution)/shard_map/near_left/pallas_call | solution.py:246
  67.1 7.0 %collective-permute-start.10 = (bf16[2,64,64]{2,1,0:T(8,128)(2,1)S(1)}, bf16[2,64,64]{2,1,0:T(8,128)(2,1)S(1)}, u32[]{:S(2)}, u32[]{:S(2)}) collective-permute-start(bf16[2,64,64]{2,1,0:T(8,128)(2,1)S(1)} %get-tuple-element.34.refs_1_), channel_id=1, source_target_pairs={{0,64},{1,65},{2,66},{3,67},{4,68},{5,69},{6,70},{7,71},{8,72},{9,... | collective-permute-start | bytes 49160 | tf_op jit(solution)/shard_map/ppermute | solution.py:447
  74.1 4.5 %collective-permute-start.11 = (bf16[2,64,64]{2,1,0:T(8,128)(2,1)S(1)}, bf16[2,64,64]{2,1,0:T(8,128)(2,1)S(1)}, u32[]{:S(2)}, u32[]{:S(2)}) collective-permute-start(bf16[2,64,64]{2,1,0:T(8,128)(2,1)S(1)} %get-tuple-element.34.refs_1_), channel_id=1, source_target_pairs={{0,128},{1,129},{2,130},{3,131},{4,132},{5,133},{6,134},{7,135},{8... | collective-permute-start | bytes 49160 | tf_op jit(solution)/shard_map/ppermute | solution.py:447
  78.6 4.7 %collective-permute-start.12 = (bf16[2,64,64]{2,1,0:T(8,128)(2,1)S(1)}, bf16[2,64,64]{2,1,0:T(8,128)(2,1)S(1)}, u32[]{:S(2)}, u32[]{:S(2)}) collective-permute-start(bf16[2,64,64]{2,1,0:T(8,128)(2,1)S(1)} %get-tuple-element.34.refs_1_), channel_id=1, source_target_pairs={{0,192},{1,193},{2,194},{3,195},{4,196},{5,197},{6,198},{7,199},{8... | collective-permute-start | bytes 49160 | tf_op jit(solution)/shard_map/ppermute | solution.py:447
  83.3 6.9 %near_right.1.refs_7_.near_part = f32[25,64,128]{2,1,0:T(8,128)S(1)} custom-call(s32[3]{0:T(128)S(1)} %get-tuple-element.26.refs_0_, s32[688]{0:T(1024)S(1)} %get-tuple-element.35.refs_1_, bf16[24,32,128]{2,1,0:T(8,128)(2,1)S(1)} %get-tuple-element.28.refs_2_, bf16[128,1024]{1,0:T(8,128)(2,1)S(1)} %copy-done.14, ...), custom_call_target="tpu_custom_call" | custom-call | flops 2097152000 | bytes 2097152 | tf_op jit(solution)/shard_map/near_right/pallas_call | solution.py:246
  90.3 0.4 coarse_levels.7
  90.7 13.5 %collective-permute-start.14 = (bf16[2,64,64]{2,1,0:T(8,128)(2,1)S(1)}, bf16[2,64,64]{2,1,0:T(8,128)(2,1)S(1)}, u32[]{:S(2)}, u32[]{:S(2)}) collective-permute-start(bf16[2,64,64]{2,1,0:T(8,128)(2,1)S(1)} %get-tuple-element.37), channel_id=1, source_target_pairs={{0,256},{1,257},{2,258},{3,259},{4,260},{5,261},{6,262},{7,263},{8... | collective-permute-start | bytes 49160 | tf_op jit(solution)/shard_map/ppermute | solution.py:447
  104.3 5.3 %couple_levels.1 = (f32[24,64,64]{2,1,0:T(8,128)S(1)}, f32[6,64,64]{2,1,0:T(8,128)S(1)}, f32[64,64]{1,0:T(8,128)S(1)}, bf16[2,2,64,64]{3,2,1,0:T(8,128)(2,1)S(1)}) custom-call(s32[24,16]{1,0:T(8,128)S(1)} %shift-left_or_fusion.codes, s32[6,8]{1,0:T(8,128)S(1)} %shift-left_or_fusion.2.box_codes, s32[1]{0:T(128)} %bitcast.place.refs_0_, ...), custom_call_target="tpu_custom_call" | custom-call | flops 1073741824 | bytes 1048576 | tf_op jit(solution)/shard_map/couple_levels/pallas_call | solution.py:382
  109.6 2.4 %group_to_points.1 = f32[64,3072]{1,0:T(8,128)} custom-call(s32[1]{0:T(128)} %bitcast.place.refs_0_, bf16[2,64,64]{2,1,0:T(8,128)(2,1)S(1)} %collective-permute-done.14.other, f32[64,64]{1,0:T(8,128)S(1)} %get-tuple-element.39.base, bf16[2,2,64,64]{3,2,1,0:T(8,128)(2,1)S(1)} %get-tuple-element.40.tip, s32[24]{0:T(128)S(1)} %bitcast.3, ...), custom_call_target="tpu_custom_call" | custom-call | tf_op jit(solution)/shard_map/group_to_points/pallas_call | solution.py:427
  (56 shorter events, 1.3 us)
Async XLA Ops:
  0.0 0.7 copy-start.15
  1.4 1.0 copy-start.2
  2.4 1.0 copy-start.6
  3.4 1.0 copy-start.7
  4.4 0.9 copy-start.10
  5.3 0.8 copy-start.12
  6.1 23.2 %copy-start.16 = (s32[24,16]{0,1:T(8,128)S(1)}, s32[24,16]{0,1:T(8,128)}, u32[]{:S(2)}) copy-start(s32[24,16]{0,1:T(8,128)} %param.32) | copy-start | bytes 4612
  6.1 29.1 %copy-start = (bf16[8,2,64,64]{3,2,1,0:T(8,128)(2,1)S(1)}, bf16[8,2,64,64]{3,2,1,0:T(8,128)(2,1)}, u32[]{:S(2)}) copy-start(bf16[8,2,64,64]{3,2,1,0:T(8,128)(2,1)} %coupling.3) | copy-start | bytes 393220
  6.1 29.1 %copy-start.1 = (bf16[8,2,64,64]{3,2,1,0:T(8,128)(2,1)S(1)}, bf16[8,2,64,64]{3,2,1,0:T(8,128)(2,1)}, u32[]{:S(2)}) copy-start(bf16[8,2,64,64]{3,2,1,0:T(8,128)(2,1)} %refs_5_.5) | copy-start | bytes 393220
  12.0 48.7 %collective-permute-start.9 = (bf16[36,80,128]{2,1,0:T(8,128)(2,1)S(1)}, bf16[36,80,128]{2,1,0:T(8,128)(2,1)S(1)}, u32[]{:S(2)}, u32[]{:S(2)}) collective-permute-start(bf16[36,80,128]{2,1,0:T(8,128)(2,1)S(1)} %get-tuple-element.29.refs_4_.mine), channel_id=1, source_target_pairs={{0,1},{1,2},{2,3},{3,4},{4,5},{5,6},{6,7},{7,8},{8,9},{9,10},{10,1... | collective-permute-start | bytes 2211848 | tf_op jit(solution)/shard_map/ppermute | solution.py:440
  15.5 13.9 %copy-start.17 = (s32[24,16]{0,1:T(8,128)S(1)}, s32[24,16]{0,1:T(8,128)}, u32[]{:S(2)}) copy-start(s32[24,16]{0,1:T(8,128)} %param.31) | copy-start | bytes 4612
  15.5 16.2 %collective-permute-start = (bf16[64,64]{1,0:T(8,128)(2,1)S(1)}, bf16[64,64]{1,0:T(8,128)(2,1)S(1)}, u32[]{:S(2)}, u32[]{:S(2)}) collective-permute-start(bf16[64,64]{1,0:T(8,128)(2,1)S(1)} %get-tuple-element.24.mine), channel_id=1, source_target_pairs={{0,1},{1,0},{2,3},{3,2},{4,5},{5,4},{6,7},{7,6},{8,9},{9,8},{10,11... | collective-permute-start | bytes 24584 | tf_op jit(solution)/shard_map/ppermute | solution.py:447
  19.0 16.3 %collective-permute-start.1 = (bf16[64,64]{1,0:T(8,128)(2,1)S(1)}, bf16[64,64]{1,0:T(8,128)(2,1)S(1)}, u32[]{:S(2)}, u32[]{:S(2)}) collective-permute-start(bf16[64,64]{1,0:T(8,128)(2,1)S(1)} %get-tuple-element.24.mine), channel_id=1, source_target_pairs={{0,2},{1,3},{2,0},{3,1},{4,6},{5,7},{6,4},{7,5},{8,10},{9,11},{10,... | collective-permute-start | bytes 24584 | tf_op jit(solution)/shard_map/ppermute | solution.py:447
  22.2 13.0 %collective-permute-start.2 = (bf16[64,64]{1,0:T(8,128)(2,1)S(1)}, bf16[64,64]{1,0:T(8,128)(2,1)S(1)}, u32[]{:S(2)}, u32[]{:S(2)}) collective-permute-start(bf16[64,64]{1,0:T(8,128)(2,1)S(1)} %get-tuple-element.24.mine), channel_id=1, source_target_pairs={{0,3},{1,2},{2,1},{3,0},{4,7},{5,6},{6,5},{7,4},{8,11},{9,10},{10,... | collective-permute-start | bytes 24584 | tf_op jit(solution)/shard_map/ppermute | solution.py:447
  25.9 57.4 %collective-permute-start.13 = (bf16[36,80,128]{2,1,0:T(8,128)(2,1)S(1)}, bf16[36,80,128]{2,1,0:T(8,128)(2,1)S(1)}, u32[]{:S(2)}, u32[]{:S(2)}) collective-permute-start(bf16[36,80,128]{2,1,0:T(8,128)(2,1)S(1)} %get-tuple-element.29.refs_4_.mine), channel_id=1, source_target_pairs={{1,0},{2,1},{3,2},{4,3},{5,4},{6,5},{7,6},{8,7},{9,8},{10,9},{11,1... | collective-permute-start | bytes 2211848 | tf_op jit(solution)/shard_map/ppermute | solution.py:441
  35.3 7.8 %copy-start.14 = (bf16[128,1024]{1,0:T(8,128)(2,1)S(1)}, bf16[128,1024]{1,0:T(8,128)(2,1)}, u32[]{:S(2)}) copy-start(bf16[128,1024]{1,0:T(8,128)(2,1)} %constant.13.clone.refs_3_) | copy-start | bytes 786436
  35.5 14.0 %collective-permute-start.3 = (bf16[2,64,64]{2,1,0:T(8,128)(2,1)S(1)}, bf16[2,64,64]{2,1,0:T(8,128)(2,1)S(1)}, u32[]{:S(2)}, u32[]{:S(2)}) collective-permute-start(bf16[2,64,64]{2,1,0:T(8,128)(2,1)S(1)} %get-tuple-element.25.refs_1_), channel_id=1, source_target_pairs={{0,4},{1,5},{2,6},{3,7},{4,0},{5,1},{6,2},{7,3},{8,12},{9,13},{10,... | collective-permute-start | bytes 49160 | tf_op jit(solution)/shard_map/ppermute | solution.py:447
  37.4 12.1 %collective-permute-start.4 = (bf16[2,64,64]{2,1,0:T(8,128)(2,1)S(1)}, bf16[2,64,64]{2,1,0:T(8,128)(2,1)S(1)}, u32[]{:S(2)}, u32[]{:S(2)}) collective-permute-start(bf16[2,64,64]{2,1,0:T(8,128)(2,1)S(1)} %get-tuple-element.25.refs_1_), channel_id=1, source_target_pairs={{0,8},{1,9},{2,10},{3,11},{4,12},{5,13},{6,14},{7,15},{8,0},{9,1},... | collective-permute-start | bytes 49160 | tf_op jit(solution)/shard_map/ppermute | solution.py:447
  40.5 9.0 %collective-permute-start.5 = (bf16[2,64,64]{2,1,0:T(8,128)(2,1)S(1)}, bf16[2,64,64]{2,1,0:T(8,128)(2,1)S(1)}, u32[]{:S(2)}, u32[]{:S(2)}) collective-permute-start(bf16[2,64,64]{2,1,0:T(8,128)(2,1)S(1)} %get-tuple-element.25.refs_1_), channel_id=1, source_target_pairs={{0,12},{1,13},{2,14},{3,15},{4,8},{5,9},{6,10},{7,11},{8,4},{9,5},... | collective-permute-start | bytes 49160 | tf_op jit(solution)/shard_map/ppermute | solution.py:447
  49.9 16.7 %collective-permute-start.6 = (bf16[2,64,64]{2,1,0:T(8,128)(2,1)S(1)}, bf16[2,64,64]{2,1,0:T(8,128)(2,1)S(1)}, u32[]{:S(2)}, u32[]{:S(2)}) collective-permute-start(bf16[2,64,64]{2,1,0:T(8,128)(2,1)S(1)} %get-tuple-element.31.refs_1_), channel_id=1, source_target_pairs={{0,16},{1,17},{2,18},{3,19},{4,20},{5,21},{6,22},{7,23},{8,24},{9,... | collective-permute-start | bytes 49160 | tf_op jit(solution)/shard_map/ppermute | solution.py:447
  52.3 14.3 %collective-permute-start.7 = (bf16[2,64,64]{2,1,0:T(8,128)(2,1)S(1)}, bf16[2,64,64]{2,1,0:T(8,128)(2,1)S(1)}, u32[]{:S(2)}, u32[]{:S(2)}) collective-permute-start(bf16[2,64,64]{2,1,0:T(8,128)(2,1)S(1)} %get-tuple-element.31.refs_1_), channel_id=1, source_target_pairs={{0,32},{1,33},{2,34},{3,35},{4,36},{5,37},{6,38},{7,39},{8,40},{9,... | collective-permute-start | bytes 49160 | tf_op jit(solution)/shard_map/ppermute | solution.py:447
  54.8 11.9 %collective-permute-start.8 = (bf16[2,64,64]{2,1,0:T(8,128)(2,1)S(1)}, bf16[2,64,64]{2,1,0:T(8,128)(2,1)S(1)}, u32[]{:S(2)}, u32[]{:S(2)}) collective-permute-start(bf16[2,64,64]{2,1,0:T(8,128)(2,1)S(1)} %get-tuple-element.31.refs_1_), channel_id=1, source_target_pairs={{0,48},{1,49},{2,50},{3,51},{4,52},{5,53},{6,54},{7,55},{8,56},{9,... | collective-permute-start | bytes 49160 | tf_op jit(solution)/shard_map/ppermute | solution.py:447
  67.1 23.2 %collective-permute-start.10 = (bf16[2,64,64]{2,1,0:T(8,128)(2,1)S(1)}, bf16[2,64,64]{2,1,0:T(8,128)(2,1)S(1)}, u32[]{:S(2)}, u32[]{:S(2)}) collective-permute-start(bf16[2,64,64]{2,1,0:T(8,128)(2,1)S(1)} %get-tuple-element.34.refs_1_), channel_id=1, source_target_pairs={{0,64},{1,65},{2,66},{3,67},{4,68},{5,69},{6,70},{7,71},{8,72},{9,... | collective-permute-start | bytes 49160 | tf_op jit(solution)/shard_map/ppermute | solution.py:447
  74.1 16.2 %collective-permute-start.11 = (bf16[2,64,64]{2,1,0:T(8,128)(2,1)S(1)}, bf16[2,64,64]{2,1,0:T(8,128)(2,1)S(1)}, u32[]{:S(2)}, u32[]{:S(2)}) collective-permute-start(bf16[2,64,64]{2,1,0:T(8,128)(2,1)S(1)} %get-tuple-element.34.refs_1_), channel_id=1, source_target_pairs={{0,128},{1,129},{2,130},{3,131},{4,132},{5,133},{6,134},{7,135},{8... | collective-permute-start | bytes 49160 | tf_op jit(solution)/shard_map/ppermute | solution.py:447
  78.6 11.7 %collective-permute-start.12 = (bf16[2,64,64]{2,1,0:T(8,128)(2,1)S(1)}, bf16[2,64,64]{2,1,0:T(8,128)(2,1)S(1)}, u32[]{:S(2)}, u32[]{:S(2)}) collective-permute-start(bf16[2,64,64]{2,1,0:T(8,128)(2,1)S(1)} %get-tuple-element.34.refs_1_), channel_id=1, source_target_pairs={{0,192},{1,193},{2,194},{3,195},{4,196},{5,197},{6,198},{7,199},{8... | collective-permute-start | bytes 49160 | tf_op jit(solution)/shard_map/ppermute | solution.py:447
  90.2 14.0 %copy-start.4 = (bf16[32,64,64]{2,1,0:T(8,128)(2,1)S(1)}, bf16[32,64,64]{2,1,0:T(8,128)(2,1)}, u32[]{:S(2)}) copy-start(bf16[32,64,64]{2,1,0:T(8,128)(2,1)} %matrices.1) | copy-start | bytes 786436
  90.2 14.0 %copy-start.5 = (bf16[32,64,64]{2,1,0:T(8,128)(2,1)S(1)}, bf16[32,64,64]{2,1,0:T(8,128)(2,1)}, u32[]{:S(2)}) copy-start(bf16[32,64,64]{2,1,0:T(8,128)(2,1)} %box_matrices.1) | copy-start | bytes 786436
  90.2 14.0 %copy-start.9 = (bf16[8,2,64,64]{3,2,1,0:T(8,128)(2,1)S(1)}, bf16[8,2,64,64]{3,2,1,0:T(8,128)(2,1)}, u32[]{:S(2)}) copy-start(bf16[8,2,64,64]{3,2,1,0:T(8,128)(2,1)} %down.1) | copy-start | bytes 393220
  90.7 18.9 %collective-permute-start.14 = (bf16[2,64,64]{2,1,0:T(8,128)(2,1)S(1)}, bf16[2,64,64]{2,1,0:T(8,128)(2,1)S(1)}, u32[]{:S(2)}, u32[]{:S(2)}) collective-permute-start(bf16[2,64,64]{2,1,0:T(8,128)(2,1)S(1)} %get-tuple-element.37), channel_id=1, source_target_pairs={{0,256},{1,257},{2,258},{3,259},{4,260},{5,261},{6,262},{7,263},{8... | collective-permute-start | bytes 49160 | tf_op jit(solution)/shard_map/ppermute | solution.py:447
  104.3 5.3 %copy-start.3 = (bf16[64,3072]{1,0:T(8,128)(2,1)S(1)}, bf16[64,3072]{1,0:T(8,128)(2,1)}, u32[]{:S(2)}) copy-start(bf16[64,3072]{1,0:T(8,128)(2,1)} %basis.1) | copy-start | bytes 1179652
  104.3 5.3 %copy-start.8 = (bf16[24,64,64]{2,1,0:T(8,128)(2,1)S(1)}, bf16[24,64,64]{2,1,0:T(8,128)(2,1)}, u32[]{:S(2)}) copy-start(bf16[24,64,64]{2,1,0:T(8,128)(2,1)} %leaf_down.1) | copy-start | bytes 589828
  104.3 5.3 %copy-start.11 = (bf16[6,64,64]{2,1,0:T(8,128)(2,1)S(1)}, bf16[6,64,64]{2,1,0:T(8,128)(2,1)}, u32[]{:S(2)}) copy-start(bf16[6,64,64]{2,1,0:T(8,128)(2,1)} %box_down.1) | copy-start | bytes 147460
  (4 other events, 2.8 us)

commit v3 on v2

--- a/solution.py
+++ b/solution.py
@@ -24,6 +24,7 @@
 ROWS = R + FR
 FX = 32
 UNROLL = 8
+LOW = 32
 PAIRS = (LD + BX) // 2
 SENT = LD + PAIRS * R // ROWS
 SLOTS = LD * (NEAR + 1) + 2 * UNROLL
@@ -37,10 +38,11 @@
 VMEM = pl.BlockSpec(memory_space=pltpu.VMEM)
 SMEM = pl.BlockSpec(memory_space=pltpu.SMEM)
 ANY = pl.BlockSpec(memory_space=pl.ANY)
-
-
-def params():
-    return pltpu.CompilerParams(vmem_limit_bytes=24 * 1024 * 1024)
+HBM = pl.BlockSpec(memory_space=pltpu.HBM)
+
+
+def params(mib=24):
+    return pltpu.CompilerParams(vmem_limit_bytes=mib * 1024 * 1024)
 
 
 def sds(shape, dtype):
@@ -61,21 +63,13 @@
     return dot(hi, m) + dot(lo, m)
 
 
-def expansion():
-    out = np.zeros((8 * FR, 8, M), np.float32)
-    for leaf in range(8):
-        e = 0
-        for a, _ in PARTS:
-            for c in range(3):
-                out[FR * leaf + 3 * a + c, leaf, e] = 1.0
-                e += 1
-        for c in range(3):
-            out[FR * leaf + 9 + c, leaf, e] = 1.0
-            e += 1
-        for c in range(3):
-            out[FR * leaf + 12, leaf, e] = 1.0
-            e += 1
-    return out.reshape(8 * FR, 8 * M)
+def expansion(leaf):
+    row = lax.broadcasted_iota(jnp.int32, (8 * FR, M), 0) - FR * leaf
+    e = lax.broadcasted_iota(jnp.int32, (8 * FR, M), 1)
+    third = (e * 43) >> 7
+    part = jnp.where(e < 9, 0, jnp.where(e < 18, 3, 6))
+    source = jnp.where(e < 24, part + e - 3 * third, jnp.where(e < 27, e - 15, jnp.where(e < 30, 12, -M)))
+    return jnp.where(row == source, 1.0, 0.0).astype(BF)
 
 
 def split3(x):
@@ -105,11 +99,12 @@
         c = [dot_nt(charges[:, pl.ds(leaf * M, M)], basis[:, pl.ds(leaf * M, M)]) for leaf in leaves]
         raised = [dot(c[i].astype(BF), leaf_up[leaf]) for i, leaf in enumerate(leaves)]
         for leaf in leaves:
-            for s in range(NEAR):
-                x = code[leaf, s]
-                for n in range(3):
-                    lists[n][at[n]] = x
-                    at[n] = at[n] + ((x >> (16 + n)) & 1)
+            for part in range(0, NEAR, 9):
+                row = [code[leaf, part + s] for s in range(9)]
+                for x in row:
+                    for n in range(3):
+                        lists[n][at[n]] = x
+                        at[n] = at[n] + ((x >> (16 + n)) & 1)
             for n in range(3):
                 lists[n][at[n]] = leaf << 8 | LD
                 at[n] = (at[n] + 1) & -2
@@ -172,7 +167,7 @@
 def first(charges, points, basis, leaf_up, box_up, parents, code):
     return pl.pallas_call(
         first_body,
-        in_specs=[ANY] * 5 + [SMEM, SMEM],
+        in_specs=[HBM] * 5 + [SMEM, SMEM],
         out_specs=[VMEM] * 3 + [SMEM] * 4,
         out_shape=[
             sds((SENT, ROWS, M), BF),
@@ -194,16 +189,16 @@
             pltpu.VMEM((BX, R, K), F32),
             pltpu.SemaphoreType.DMA((5,)),
         ],
-        compiler_params=params(),
+        compiler_params=params(60),
         name="points_to_group",
     )(charges, points, basis, leaf_up, box_up, parents, code)
 
 
-def near_body(which, sizes, slots, target, expand, source, *rest):
+def near_body(which, sizes, slots, target, source, *rest):
     if which:
         start_from, _, acc, table, feats, sem = rest
     else:
-        _, acc, table, feats, sem = rest
+        acc, table, feats, sem = rest
     copy = pltpu.make_async_copy(source.at[pl.ds(0, LD)], table.at[pl.ds(0, LD)], sem)
     copy.start()
     if which:
@@ -215,11 +210,12 @@
     ones = 3 * len(PARTS) + 3
     feats[LD] = jnp.where((lane >= ones) & (lane < ones + 3), 1.0, 0.0).astype(BF)
     copy.wait()
+    expand = [expansion(i) for i in range(8)]
     for o in range(LD // 8):
         rows = jnp.concatenate([table[8 * o + i, R:ROWS, :] for i in range(8)], axis=0)
-        spread = dot(rows, expand[...]).astype(BF)
+        spread = [dot(rows, expand[i]).astype(BF) for i in range(8)]
         for i in range(8):
-            feats[8 * o + i] = spread[:, M * i : M * (i + 1)]
+            feats[8 * o + i] = spread[i]
     pad = jnp.zeros((M - FX, M), BF)
 
     def step(it, _):
@@ -241,11 +237,11 @@
     lax.fori_loop(0, sizes[which], step, 0)
 
 
-def near(which, sizes, slots, target, expand, source, extra):
+def near(which, sizes, slots, target, source, extra):
     pairs = 100
     return pl.pallas_call(
         lambda *refs: near_body(which, *refs),
-        in_specs=[SMEM, SMEM, VMEM, VMEM, ANY] + ([VMEM, ANY] if which else [ANY]),
+        in_specs=[SMEM, SMEM, VMEM, ANY] + ([VMEM, ANY] if which else []),
         out_specs=VMEM,
         out_shape=sds((LD + 1, R, M), F32),
         scratch_shapes=[
@@ -258,57 +254,57 @@
             flops=pairs * 2 * 256 * 128 * 320, bytes_accessed=2 << 20, transcendentals=pairs << 15
         ),
         name=("near_own", "near_left", "near_right")[which],
-    )(sizes, slots, target, expand, source, *extra)
-
-
-def bottom_body(place, mine, one, two, three, up, coupling, pair, field, held):
-    q = place[0] & 3
-    for k, ref in enumerate((mine, one, two, three)):
-        held[q ^ k] = ref[...]
-    left = jnp.concatenate([held[0], held[2]], axis=0)
-    right = jnp.concatenate([held[1], held[3]], axis=0)
-    raised = dot(left, up[0, 0]) + dot(right, up[0, 1])
-    field[0] = dot(held[q ^ 2], coupling[0, 0]) + dot(held[q ^ 3], coupling[0, 1])
-    pair[...] = raised.astype(BF).reshape(2, R, K)
-
-
-def level_body(h, place, mine, one, two, three, up, coupling, _, pair, field, held, above):
-    q = place[0] >> h
-    s = (q >> 1) & 3
-    for k, ref in enumerate((mine, one, two, three)):
-        held[pl.ds(2 * (s ^ k), 2)] = ref[...]
-    left = jnp.concatenate([held[2 * i] for i in range(4)], axis=0)
-    right = jnp.concatenate([held[2 * i + 1] for i in range(4)], axis=0)
-    raised = dot(left, up[h, 0]) + dot(right, up[h, 1])
-    far = (q & 7) ^ 2
-    low_field = dot(held[far], coupling[h, 0]) + dot(held[far ^ 1], coupling[h, 1])
-    left = jnp.concatenate([raised[0:R], raised[2 * R : 3 * R]], axis=0)
-    right = jnp.concatenate([raised[R : 2 * R], raised[3 * R :]], axis=0)
-    top = dot2(left, up[h + 1, 0]) + dot2(right, up[h + 1, 1])
-    above[...] = raised.reshape(4, R, K)
-    pair[...] = top.astype(BF).reshape(2, R, K)
-    field[0] = low_field
-    far = s ^ 2
-    field[1] = dot2(above[far], coupling[h + 1, 0]) + dot2(above[far ^ 1], coupling[h + 1, 1])
-
-
-def level(h, place, mine, others, up, coupling, order):
-    bottom = h < 0
-    out = pl.pallas_call(
-        bottom_body if bottom else lambda *refs: level_body(h, *refs),
-        in_specs=[SMEM] + [VMEM] * 6 + ([] if bottom else [ANY]),
+    )(sizes, slots, target, source, *extra)
+
+
+def raise_nodes(nodes, matrices):
+    count = nodes.shape[0] // 2
+    left = jnp.concatenate([nodes[2 * i] for i in range(count)], axis=0)
+    right = jnp.concatenate([nodes[2 * i + 1] for i in range(count)], axis=0)
+    mul = dot if nodes.dtype == BF else dot2
+    return (mul(left, matrices[0]) + mul(right, matrices[1])).reshape(count, R, K)
+
+
+def low_body(place, nodes, up, coupling, _, top, field, held):
+    levels = [nodes[...]]
+    for h in range(4):
+        levels.append(raise_nodes(levels[h], (up[h, 0], up[h, 1])))
+    top[...] = levels[4].astype(BF)
+    start = 0
+    for h in range(1, 4):
+        held[start : start + (LOW >> h)] = levels[h]
+        start += LOW >> h
+    me = place[0] & (LOW - 1)
+    near = me ^ 2
+    out = [dot(nodes[near], coupling[0, 0]) + dot(nodes[near ^ 1], coupling[0, 1])]
+    start = 0
+    for h in range(1, 4):
+        near = ((me >> h) ^ 2) + start
+        far = ((me >> h) ^ 3) + start
+        out.append(dot2(held[near], coupling[h, 0]) + dot2(held[far], coupling[h, 1]))
+        start += LOW >> h
+    for h in range(4):
+        field[h] = out[h]
+
+
+def low_tree(place, nodes, up, coupling, order):
+    return pl.pallas_call(
+        low_body,
+        in_specs=[SMEM, VMEM, VMEM, VMEM, ANY],
         out_specs=[VMEM, VMEM],
-        out_shape=[sds((2, R, K), BF), sds((1 if bottom else 2, R, K), F32)],
-        scratch_shapes=[pltpu.VMEM((4, R, K), BF)]
-        if bottom
-        else [pltpu.VMEM((8, R, K), BF), pltpu.VMEM((4, R, K), F32)],
+        out_shape=[sds((2, R, K), BF), sds((4, R, K), F32)],
+        scratch_shapes=[pltpu.VMEM((LOW, R, K), F32)],
         compiler_params=params(),
-        name="coarse_levels",
-    )
-    return out(place, mine, *others, up, coupling, *order)
-
-
-def couple_body(codes, box_codes, place, matrices, box_matrices, f0, f12, f34, f56, down, coupling, left, mine, right, leaf_field, box_field, base, tip, table, low, high, sems):
+        name="coarse_low",
+    )(place, nodes, up, coupling, order)
+
+
+def split2(x):
+    hi = x.astype(BF)
+    return hi, (x - hi.astype(F32)).astype(BF)
+
+
+def couple_body(codes, box_codes, place, matrices, box_matrices, low_field, down, coupling, left, mine, right, leaf_field, box_field, base, tip, table, low, high, sems):
     blocks = SENT - LD
     copies = load(
         [
@@ -317,21 +313,24 @@
         ]
     )
     me = place[0]
-    fields = (f0[0], f12[0], f12[1], f34[0], f34[1], f56[0], f56[1])
-    total = fields[6]
-    chain = down[6, (me >> 6) & 1].astype(F32)
-    for h in range(5, -1, -1):
+    total = low_field[3]
+    chain = down[3, (me >> 3) & 1].astype(F32)
+    for h in range(2, -1, -1):
         both = dot2(jnp.concatenate([total, chain], axis=0), down[h, (me >> h) & 1])
-        total = fields[h] + both[:R]
+        total = low_field[h] + both[:R]
         chain = both[R:]
-    chain_high = chain.astype(BF)
-    chain_low = (chain - chain_high.astype(F32)).astype(BF)
-    for i in range(2):
-        product = dot(coupling[7, i], chain_high) + dot(coupling[7, i], chain_low)
-        upper = product.astype(BF)
-        tip[i, 0] = upper
-        tip[i, 1] = (product - upper.astype(F32)).astype(BF)
+    tips = []
+    for h in range(4, 8):
+        hi, lo = split2(chain)
+        stack = jnp.concatenate([coupling[h, 0], coupling[h, 1], down[min(h, 6), (me >> h) & 1]], axis=0)
+        product = dot(stack, hi) + dot(stack, lo)
+        tips.append((split2(product[0:K]), split2(product[K : 2 * K])))
+        chain = product[2 * K :]
     base[...] = total
+    for h in range(4):
+        for i in range(2):
+            for n in range(2):
+                tip[h, i, n] = tips[h][i][n]
     for copy in copies:
         copy.wait()
     first = lax.broadcasted_iota(jnp.int32, (R, 2 * K), 1) < K
@@ -378,16 +377,16 @@
         box_field[box] = got[box]
 
 
-def couple(codes, box_codes, place, matrices, box_matrices, fields, down, coupling, sents):
+def couple(codes, box_codes, place, matrices, box_matrices, low_field, down, coupling, sents):
     return pl.pallas_call(
         couple_body,
-        in_specs=[SMEM] * 3 + [VMEM] * 8 + [ANY] * 3,
+        in_specs=[SMEM] * 3 + [VMEM] * 5 + [ANY] * 3,
         out_specs=[VMEM] * 4,
         out_shape=[
             sds((LD, R, K), F32),
             sds((BX, R, K), F32),
             sds((R, K), F32),
-            sds((2, 2, K, K), BF),
+            sds((4, 2, 2, K, K), BF),
         ],
         scratch_shapes=[
             pltpu.VMEM((3 * (SENT - LD), ROWS, M), BF),
@@ -398,15 +397,26 @@
         compiler_params=params(),
         cost_estimate=pl.CostEstimate(flops=1 << 30, bytes_accessed=1 << 20, transcendentals=0),
         name="couple_levels",
-    )(codes, box_codes, place, matrices, box_matrices, *fields, down, coupling, *sents)
-
-
-def final_body(place, other, base, tip, parents, leaf_field, box_field, box_down, leaf_down, basis, near_part, out, boxes):
-    q = (place[0] >> 7) & 1
+    )(codes, box_codes, place, matrices, box_matrices, low_field, down, coupling, *sents)
+
+
+def final_body(place, nodes, up, base, tip, parents, leaf_field, box_field, box_down, leaf_down, basis, near_part, out, boxes, held):
+    block = nodes[...].reshape(LOW, R, K)
+    start = 0
+    levels = [block]
+    for h in range(3):
+        levels.append(raise_nodes(levels[h], (up[4 + h, 0], up[4 + h, 1])))
+    for h in range(4):
+        held[start : start + (LOW >> h)] = levels[h].astype(F32)
+        start += LOW >> h
+    me = (place[0] >> 4) & (LOW - 1)
     total = base[...]
-    for i in range(2):
-        node = other[q ^ i]
-        total = total + (dot(node, tip[i, 0]) + dot(node, tip[i, 1]))
+    start = 0
+    for h in range(4):
+        for i in range(2):
+            hi, lo = split2(held[((me >> h) ^ (2 + i)) + start])
+            total = total + (dot(hi, tip[h, i, 0]) + dot(hi, tip[h, i, 1]) + dot(lo, tip[h, i, 0]))
+        start += LOW >> h
     group = total.astype(BF)
     got = [(box_field[box] + dot(group, box_down[box])).astype(BF) for box in range(BX)]
     for box in range(BX):
@@ -423,16 +433,16 @@
             out[:, pl.ds(leaf * M, M)] = got[i]
 
 
-def finish(place, other, base, tip, parents, fields, box_down, leaf_down, basis, near_part):
+def finish(place, nodes, up, base, tip, parents, fields, box_down, leaf_down, basis, near_part):
     return pl.pallas_call(
         final_body,
-        in_specs=[SMEM] + [VMEM] * 3 + [SMEM] + [VMEM] * 6,
+        in_specs=[SMEM] + [VMEM] * 4 + [SMEM] + [VMEM] * 6,
         out_specs=VMEM,
         out_shape=sds((R, LD * M), F32),
-        scratch_shapes=[pltpu.VMEM((BX, R, K), BF)],
+        scratch_shapes=[pltpu.VMEM((BX, R, K), BF), pltpu.VMEM((2 * LOW, R, K), F32)],
         compiler_params=params(),
         name="group_to_points",
-    )(place, other, base, tip, parents, *fields, box_down, leaf_down, basis, near_part)
+    )(place, nodes, up, base, tip, parents, *fields, box_down, leaf_down, basis, near_part)
 
 
 def exchange(x):
@@ -442,9 +452,9 @@
     return left, right
 
 
-def partners(x, bit, ways):
-    count = lax.axis_size(AXES)
-    return [lax.ppermute(x, AXES, [(i, i ^ (k << bit)) for i in range(count)]) for k in range(1, ways)]
+def gather_groups(x, groups):
+    many = jnp.broadcast_to(x[None], (len(groups[0]),) + x.shape)
+    return lax.all_to_all(many, AXES, 0, 0, axis_index_groups=groups, tiled=True)
 
 
 def local(
@@ -482,20 +492,18 @@
     sent, target, ascent, own, left, right, sizes = first(
         charges, points, leaf_basis, leaf_up, box_up, parents, code
     )
-    expand = jnp.asarray(expansion(), BF)
-
-    pair, f0 = level(-1, place, ascent, partners(ascent, 0, 4), top_up, top_coupling, ())
+
+    blocks = lax.axis_size(AXES) // LOW
+    low_groups = [[b * LOW + i for i in range(LOW)] for b in range(blocks)]
+    high_groups = [[b * LOW + i for b in range(blocks)] for i in range(LOW)]
+
+    low_nodes = gather_groups(ascent, low_groups)
     sent_left, sent_right = exchange(sent)
-    others = partners(pair, 2, 4)
-    near_part = near(0, sizes, own, target, expand, sent, (f0,))
-    pair, f12 = level(1, place, pair, others, top_up, top_coupling, (near_part,))
-    others = partners(pair, 4, 4)
-    near_part = near(1, sizes, left, target, expand, sent_left, (near_part, f12))
-    pair, f34 = level(3, place, pair, others, top_up, top_coupling, (near_part,))
-    others = partners(pair, 6, 4)
-    near_part = near(2, sizes, right, target, expand, sent_right, (near_part, f34))
-    pair, f56 = level(5, place, pair, others, top_up, top_coupling, (near_part,))
-    (other,) = partners(pair, 8, 2)
+    near_part = near(0, sizes, own, target, sent, ())
+    top, low_field = low_tree(place, low_nodes, top_up, top_coupling, near_part)
+    high_nodes = gather_groups(top, high_groups)
+    near_part = near(1, sizes, left, target, sent_left, (near_part, low_field))
+    near_part = near(2, sizes, right, target, sent_right, (near_part, low_field))
 
     def table_row(sources, classes, width, start):
         rel = sources - (device - 1) * width
@@ -510,13 +518,13 @@
         place,
         leaf_coupling,
         box_coupling,
-        (f0, f12, f34, f56),
+        low_field,
         top_down,
         top_coupling,
         (sent_left, sent, sent_right),
     )
     return finish(
-        place, other, base, tip, parents, (leaf_field, box_field), box_down, leaf_down, leaf_basis, near_part
+        place, high_nodes, top_up, base, tip, parents, (leaf_field, box_field), box_down, leaf_down, leaf_basis, near_part
     )
 
 

time: 113 us -> 86.8 us (0.77)
  the two profiles are of different devices: /device:TPU:4 before, /device:TPU:32 now
where the time goes in v3:
time: 86.8 us; the launch traced here: 85.9 us
  Pallas kernels  35.2 us (41%)
  starting transfers between devices  31.6 us (36%)
  local copies, waits for them, and re-layouts  18 us (21%)
    all_to_all x2, starting transfers between devices, gather_groups(): lax.all_to_all(many, AXES, 0, 0, axis_index_groups=groups, tiled=True)  20.9 us
    pallas_call x3, Pallas kernels, near(): pl.pallas_call(lambda *refs: near_body(which, *refs), in_specs=[SMEM, SME...  19.1 us
    unnamed x68, local copies, waits for them, and re-layouts  16.3 us
    ppermute x1, starting transfers between devices, exchange(): right = lax.ppermute(x, AXES, [(i + 1, i) for i in range(count - 1)])  7.14 us
    pallas_call x1, Pallas kernels, first(): pl.pallas_call(first_body, in_specs=[HBM] * 5 + [SMEM, SMEM], out_specs=[...  6.74 us
    pallas_call x1, Pallas kernels, couple(): pl.pallas_call(couple_body, in_specs=[SMEM] * 3 + [VMEM] * 5 + [ANY] * 3,...  4.76 us
    ppermute x1, starting transfers between devices, exchange(): left = lax.ppermute(x, AXES, [(i, i + 1) for i in range(count - 1)])  3.63 us
    pallas_call x1, Pallas kernels, finish(): pl.pallas_call(final_body, in_specs=[SMEM] + [VMEM] * 4 + [SMEM] + [VMEM]...  3.46 us
  transfers between devices with their start and end apart: 4, of which 0 were waited for; matrix products, arithmetic and copies ran while one was open for 5% of the time, Pallas kernels for 29%

profile of v3, /device:TPU:32, one launch (start us, length us, event | category | flops | bytes accessed | tf_op | source)
XLA Modules:
  0.0 85.9 jit_solution(8220772912170880284)
XLA Ops:
  0.0 0.7 copy-done.25
  0.7 0.7 shift-left_or_fusion.1.code
  1.4 6.7 %points_to_group.1 = (bf16[36,80,128]{2,1,0:T(8,128)(2,1)}, bf16[24,32,128]{2,1,0:T(8,128)(2,1)}, bf16[64,64]{1,0:T(8,128)(2,1)}, s32[688]{0:T(1024)}, s32[688]{0:T(1024)}, /*index=5*/s32[688]{0:T(1024)}, s32[3]{0:T(128)}) custom-call(bf16[64,3072]{1,0:T(8,128)(2,1)} %charges_in.1, f32[3,3072]{1,0:T(4,128)} %points_in.1, bf16[64,3072]{1,0:T(8,128)(2,1)} %basis.1, ...), custom_call_target="tpu_custom_call" | custom-call | tf_op jit(solution)/shard_map/points_to_group/pallas_call | solution.py:168
  8.1 0.8 broadcast_in_dim.41
  9.0 1.1 %reshape.12 = bf16[32,2,2048]{2,1,0:T(2,128)(2,1)} reshape(bf16[32,64,64]{2,1,0:T(8,128)(2,1)S(1)} %broadcast_in_dim.41) | data formatting | bytes 524288
  10.1 7.6 %all-to-all-start = ((bf16[32,2,2048]{2,1,0:T(2,128)(2,1)}), bf16[32,2,2048]{2,1,0:T(2,128)(2,1)}, u32[]{:S(2)}, u32[]{:S(2)}) async-start(bf16[32,2,2048]{2,1,0:T(2,128)(2,1)} %reshape.12), calls=%async_computation | async-start | bytes 524288 | tf_op jit(solution)/shard_map/all_to_all | solution.py:457
  17.7 3.6 %collective-permute-start = (bf16[36,80,128]{2,1,0:T(8,128)(2,1)S(1)}, bf16[36,80,128]{2,1,0:T(8,128)(2,1)}, u32[]{:S(2)}, u32[]{:S(2)}) collective-permute-start(bf16[36,80,128]{2,1,0:T(8,128)(2,1)S(1)} %copy-done.10), channel_id=1, source_target_pairs={{0,1},{1,2},{2,3},{3,4},{4,5},{5,6},{6,7},{7,8},{8,9},{9,10},{10,1... | collective-permute-start | bytes 2211848 | tf_op jit(solution)/shard_map/ppermute | solution.py:450
  21.3 7.1 %collective-permute-start.1 = (bf16[36,80,128]{2,1,0:T(8,128)(2,1)S(1)}, bf16[36,80,128]{2,1,0:T(8,128)(2,1)S(1)}, u32[]{:S(2)}, u32[]{:S(2)}) collective-permute-start(bf16[36,80,128]{2,1,0:T(8,128)(2,1)S(1)} %copy-done.10), channel_id=1, source_target_pairs={{1,0},{2,1},{3,2},{4,3},{5,4},{6,5},{7,6},{8,7},{9,8},{10,9},{11,1... | collective-permute-start | bytes 2211848 | tf_op jit(solution)/shard_map/ppermute | solution.py:451
  28.5 0.6 copy-done.24
  29.1 6.9 %near_own.1._.refs_4_ = f32[25,64,128]{2,1,0:T(8,128)S(1)} custom-call(s32[3]{0:T(128)S(1)} %copy-done.24, s32[688]{0:T(1024)S(1)} %copy-done.23, bf16[24,32,128]{2,1,0:T(8,128)(2,1)S(1)} %copy-done.17, bf16[36,80,128]{2,1,0:T(8,128)(2,1)S(1)} %copy-done.10), custom_call_target="tpu_custom_call" | custom-call | flops 2097152000 | bytes 2097152 | tf_op jit(solution)/shard_map/near_own/pallas_call | solution.py:242
  36.0 1.4 %reshape.13.nodes = bf16[32,64,64]{2,1,0:T(8,128)(2,1)S(1)} reshape(bf16[32,2,2048]{2,1,0:T(2,128)(2,1)} %all-to-all-done) | data formatting | bytes 524288
  37.4 1.2 %coarse_low.1 = (bf16[2,64,64]{2,1,0:T(8,128)(2,1)S(1)}, f32[4,64,64]{2,1,0:T(8,128)S(1)}) custom-call(s32[1]{0:T(128)} %bitcast.place, bf16[32,64,64]{2,1,0:T(8,128)(2,1)S(1)} %reshape.13.nodes, bf16[8,2,64,64]{3,2,1,0:T(8,128)(2,1)S(1)} %copy-done.1, bf16[8,2,64,64]{3,2,1,0:T(8,128)(2,1)S(1)} %copy-done.3, f32[25,64,128]{2,1,0:T(8,128)S(1)} %near_own.1._.refs_4_), custom_call_target="tpu_custom_call" | custom-call | tf_op jit(solution)/shard_map/coarse_low/pallas_call | solution.py:291
  38.6 0.6 copy-done.19
  39.2 0.9 %broadcast_in_dim.42 = bf16[16,2,64,64]{3,2,1,0:T(8,128)(2,1)} broadcast(bf16[2,64,64]{2,1,0:T(8,128)(2,1)S(1)} %get-tuple-element.23), dimensions={1,2,3} | broadcast | bytes 278528 | tf_op jit(solution)/shard_map/broadcast_in_dim | solution.py:456
  40.2 2.2 %reshape.14 = bf16[16,2,4096]{2,1,0:T(2,128)(2,1)} reshape(bf16[16,2,64,64]{3,2,1,0:T(8,128)(2,1)} %broadcast_in_dim.42) | data formatting | bytes 524288
  42.4 13.3 %all-to-all-start.1 = ((bf16[16,2,4096]{2,1,0:T(2,128)(2,1)}), bf16[16,2,4096]{2,1,0:T(2,128)(2,1)}, u32[]{:S(2)}, u32[]{:S(2)}) async-start(bf16[16,2,4096]{2,1,0:T(2,128)(2,1)} %reshape.14), calls=%async_computation.1 | async-start | bytes 524288 | tf_op jit(solution)/shard_map/all_to_all | solution.py:457
  55.7 0.1 copy.22
  55.8 0.6 copy-done.27
  56.4 0.1 copy.24
  56.5 0.9 %copy-done.12 = bf16[36,80,128]{2,1,0:T(8,128)(2,1)} copy-done((bf16[36,80,128]{2,1,0:T(8,128)(2,1)}, bf16[36,80,128]{2,1,0:T(8,128)(2,1)S(1)}, u32[]{:S(2)}) %copy-start.12) | copy-done | bytes 737304
  57.4 1.1 %copy-done.11 = bf16[36,80,128]{2,1,0:T(8,128)(2,1)S(1)} copy-done((bf16[36,80,128]{2,1,0:T(8,128)(2,1)S(1)}, bf16[36,80,128]{2,1,0:T(8,128)(2,1)}, u32[]{:S(2)}) %copy-start.11) | copy-done | bytes 737304
  58.5 1.1 %copy-done.13 = bf16[36,80,128]{2,1,0:T(8,128)(2,1)S(1)} copy-done((bf16[36,80,128]{2,1,0:T(8,128)(2,1)S(1)}, bf16[36,80,128]{2,1,0:T(8,128)(2,1)}, u32[]{:S(2)}) %copy-start.13) | copy-done | bytes 737304
  59.7 1.0 %copy-done.15 = bf16[32,64,64]{2,1,0:T(8,128)(2,1)S(1)} copy-done((bf16[32,64,64]{2,1,0:T(8,128)(2,1)S(1)}, bf16[32,64,64]{2,1,0:T(8,128)(2,1)}, u32[]{:S(2)}) %copy-start.15) | copy-done | bytes 262168
  60.7 0.9 %copy-done.16 = bf16[8,2,64,64]{3,2,1,0:T(8,128)(2,1)S(1)} copy-done((bf16[8,2,64,64]{3,2,1,0:T(8,128)(2,1)S(1)}, bf16[8,2,64,64]{3,2,1,0:T(8,128)(2,1)}, u32[]{:S(2)}) %copy-start.16) | copy-done | bytes 131096
  61.7 4.8 %couple_levels.1 = (f32[24,64,64]{2,1,0:T(8,128)S(1)}, f32[6,64,64]{2,1,0:T(8,128)S(1)}, f32[64,64]{1,0:T(8,128)S(1)}, bf16[4,2,2,64,64]{4,3,2,1,0:T(8,128)(2,1)S(1)}) custom-call(s32[24,16]{1,0:T(8,128)S(1)} %shift-left_or_fusion.codes, s32[6,8]{1,0:T(8,128)S(1)} %shift-left_or_fusion.2.box_codes, s32[1]{0:T(128)} %bitcast.place, ...), custom_call_target="tpu_custom_call" | custom-call | flops 1073741824 | bytes 1048576 | tf_op jit(solution)/shard_map/couple_levels/pallas_call | solution.py:381
  66.5 6.2 %near_left.1.refs_4_ = f32[25,64,128]{2,1,0:T(8,128)S(1)} custom-call(s32[3]{0:T(128)S(1)} %copy-done.24, s32[688]{0:T(1024)S(1)} %copy-done.22, bf16[24,32,128]{2,1,0:T(8,128)(2,1)S(1)} %copy-done.18, bf16[36,80,128]{2,1,0:T(8,128)(2,1)} %collective-permute-done.left.refs_3_, f32[25,64,128]{2,1,0:T(8,128)S(1)} %near_own.1._.refs_4_, f32[4,64,64]{2,1,0:T(8,128)S(1)} %copy-done.20), custom_call_target="tpu_custom_call" | custom-call | flops 2097152000 | bytes 2097152 | tf_op jit(solution)/shard_map/near_left/pallas_call | solution.py:242
  72.7 6.0 %near_right.1.near_part = f32[25,64,128]{2,1,0:T(8,128)S(1)} custom-call(s32[3]{0:T(128)S(1)} %copy-done.24, s32[688]{0:T(1024)S(1)} %copy-done.21, bf16[24,32,128]{2,1,0:T(8,128)(2,1)S(1)} %copy-done.18, bf16[36,80,128]{2,1,0:T(8,128)(2,1)S(1)} %copy-done.13, f32[25,64,128]{2,1,0:T(8,128)S(1)} %near_left.1.refs_4_, f32[4,64,64]{2,1,0:T(8,128)S(1)} %copy-done.20), custom_call_target="tpu_custom_call" | custom-call | flops 2097152000 | bytes 2097152 | tf_op jit(solution)/shard_map/near_right/pallas_call | solution.py:242
  78.7 1.4 %reshape.15.nodes = bf16[16,2,64,64]{3,2,1,0:T(8,128)(2,1)S(1)} reshape(bf16[16,2,4096]{2,1,0:T(2,128)(2,1)} %all-to-all-done.1) | data formatting | bytes 524288
  80.2 0.6 copy-done.9
  80.8 0.9 %copy-done.5 = f32[6,64,64]{2,1,0:T(8,128)S(1)} copy-done((f32[6,64,64]{2,1,0:T(8,128)S(1)}, f32[6,64,64]{2,1,0:T(8,128)}, u32[]{:S(2)}) %copy-start.5) | copy-done | bytes 98328
  81.7 0.8 copy-done.8
  82.5 3.5 %group_to_points.1 = f32[64,3072]{1,0:T(8,128)} custom-call(s32[1]{0:T(128)} %bitcast.place, bf16[16,2,64,64]{3,2,1,0:T(8,128)(2,1)S(1)} %reshape.15.nodes, bf16[8,2,64,64]{3,2,1,0:T(8,128)(2,1)S(1)} %copy-done.1, f32[64,64]{1,0:T(8,128)S(1)} %copy-done.8, bf16[4,2,2,64,64]{4,3,2,1,0:T(8,128)(2,1)S(1)} %get-tuple-element.26.tip, s32[24]{0:T(128)S(1)} %bitcast.3, ...), custom_call_target="tpu_custom_call" | custom-call | tf_op jit(solution)/shard_map/group_to_points/pallas_call | solution.py:437
  (57 shorter events, 0.1 us)
Async XLA Ops:
  0.0 0.7 copy-start.25
  0.0 0.7 copy-start.30
  9.0 8.7 %copy-start.10 = (bf16[36,80,128]{2,1,0:T(8,128)(2,1)S(1)}, bf16[36,80,128]{2,1,0:T(8,128)(2,1)}, u32[]{:S(2)}) copy-start(bf16[36,80,128]{2,1,0:T(8,128)(2,1)} %get-tuple-element.22.refs_3_.mine) | copy-start | bytes 2211844
  10.1 18.4 %copy-start.17 = (bf16[24,32,128]{2,1,0:T(8,128)(2,1)S(1)}, bf16[24,32,128]{2,1,0:T(8,128)(2,1)}, u32[]{:S(2)}) copy-start(bf16[24,32,128]{2,1,0:T(8,128)(2,1)} %get-tuple-element.21.refs_2_) | copy-start | bytes 589828
  10.1 25.9 %all-to-all-start = ((bf16[32,2,2048]{2,1,0:T(2,128)(2,1)}), bf16[32,2,2048]{2,1,0:T(2,128)(2,1)}, u32[]{:S(2)}, u32[]{:S(2)}) async-start(bf16[32,2,2048]{2,1,0:T(2,128)(2,1)} %reshape.12), calls=%async_computation | async-start | bytes 524288 | tf_op jit(solution)/shard_map/all_to_all | solution.py:457
  17.7 10.8 %copy-start.23 = (s32[688]{0:T(1024)S(1)}, s32[688]{0:T(1024)}, u32[]{:S(2)}) copy-start(s32[688]{0:T(1024)} %get-tuple-element.20.refs_1_) | copy-start | bytes 8260
  17.7 38.8 %collective-permute-start = (bf16[36,80,128]{2,1,0:T(8,128)(2,1)S(1)}, bf16[36,80,128]{2,1,0:T(8,128)(2,1)}, u32[]{:S(2)}, u32[]{:S(2)}) collective-permute-start(bf16[36,80,128]{2,1,0:T(8,128)(2,1)S(1)} %copy-done.10), channel_id=1, source_target_pairs={{0,1},{1,2},{2,3},{3,4},{4,5},{5,6},{6,7},{7,8},{8,9},{9,10},{10,1... | collective-permute-start | bytes 2211848 | tf_op jit(solution)/shard_map/ppermute | solution.py:450
  21.3 35.2 %collective-permute-start.1 = (bf16[36,80,128]{2,1,0:T(8,128)(2,1)S(1)}, bf16[36,80,128]{2,1,0:T(8,128)(2,1)S(1)}, u32[]{:S(2)}, u32[]{:S(2)}) collective-permute-start(bf16[36,80,128]{2,1,0:T(8,128)(2,1)S(1)} %copy-done.10), channel_id=1, source_target_pairs={{1,0},{2,1},{3,2},{4,3},{5,4},{6,5},{7,6},{8,7},{9,8},{10,9},{11,1... | collective-permute-start | bytes 2211848 | tf_op jit(solution)/shard_map/ppermute | solution.py:451
  36.0 1.4 %copy-start.1 = (bf16[8,2,64,64]{3,2,1,0:T(8,128)(2,1)S(1)}, bf16[8,2,64,64]{3,2,1,0:T(8,128)(2,1)}, u32[]{:S(2)}) copy-start(bf16[8,2,64,64]{3,2,1,0:T(8,128)(2,1)} %up.3) | copy-start | bytes 393220
  36.0 1.4 %copy-start.3 = (bf16[8,2,64,64]{3,2,1,0:T(8,128)(2,1)S(1)}, bf16[8,2,64,64]{3,2,1,0:T(8,128)(2,1)}, u32[]{:S(2)}) copy-start(bf16[8,2,64,64]{3,2,1,0:T(8,128)(2,1)} %coupling.3) | copy-start | bytes 393220
  40.2 17.2 %copy-start.14 = (bf16[32,64,64]{2,1,0:T(8,128)(2,1)S(1)}, bf16[32,64,64]{2,1,0:T(8,128)(2,1)}, u32[]{:S(2)}) copy-start(bf16[32,64,64]{2,1,0:T(8,128)(2,1)} %matrices.1) | copy-start | bytes 786436
  42.4 13.3 %copy-start.26 = (s32[24,16]{0,1:T(8,128)S(1)}, s32[24,16]{0,1:T(8,128)}, u32[]{:S(2)}) copy-start(s32[24,16]{0,1:T(8,128)} %param.30) | copy-start | bytes 4612
  42.4 14.1 %copy-start.28 = (s32[6,8]{1,0:T(8,128)S(1)}, s32[6,8]{1,0:T(8,128)}, u32[]{:S(2)}) copy-start(s32[6,8]{1,0:T(8,128)} %param.34) | copy-start | bytes 580
  42.4 14.1 %copy-start.29 = (s32[6,8]{1,0:T(8,128)S(1)}, s32[6,8]{1,0:T(8,128)}, u32[]{:S(2)}) copy-start(s32[6,8]{1,0:T(8,128)} %param.33) | copy-start | bytes 580
  42.4 15.0 %copy-start.20 = (f32[4,64,64]{2,1,0:T(8,128)S(1)}, f32[4,64,64]{2,1,0:T(8,128)}, u32[]{:S(2)}) copy-start(f32[4,64,64]{2,1,0:T(8,128)} %copy-done.19) | copy-start | bytes 196612
  42.4 36.3 %all-to-all-start.1 = ((bf16[16,2,4096]{2,1,0:T(2,128)(2,1)}), bf16[16,2,4096]{2,1,0:T(2,128)(2,1)}, u32[]{:S(2)}, u32[]{:S(2)}) async-start(bf16[16,2,4096]{2,1,0:T(2,128)(2,1)} %reshape.14), calls=%async_computation.1 | async-start | bytes 524288 | tf_op jit(solution)/shard_map/all_to_all | solution.py:457
  55.7 0.7 copy-start.27
  56.5 0.9 %copy-start.12 = (bf16[36,80,128]{2,1,0:T(8,128)(2,1)}, bf16[36,80,128]{2,1,0:T(8,128)(2,1)S(1)}, u32[]{:S(2)}) copy-start(bf16[36,80,128]{2,1,0:T(8,128)(2,1)S(1)} %collective-permute-done.1.right.refs_3_) | copy-start | bytes 2211844
  57.4 1.1 %copy-start.11 = (bf16[36,80,128]{2,1,0:T(8,128)(2,1)S(1)}, bf16[36,80,128]{2,1,0:T(8,128)(2,1)}, u32[]{:S(2)}) copy-start(bf16[36,80,128]{2,1,0:T(8,128)(2,1)} %get-tuple-element.22.refs_3_.mine) | copy-start | bytes 2211844
  58.5 1.1 %copy-start.13 = (bf16[36,80,128]{2,1,0:T(8,128)(2,1)S(1)}, bf16[36,80,128]{2,1,0:T(8,128)(2,1)}, u32[]{:S(2)}) copy-start(bf16[36,80,128]{2,1,0:T(8,128)(2,1)} %copy-done.12) | copy-start | bytes 2211844
  59.7 1.0 %copy-start.15 = (bf16[32,64,64]{2,1,0:T(8,128)(2,1)S(1)}, bf16[32,64,64]{2,1,0:T(8,128)(2,1)}, u32[]{:S(2)}) copy-start(bf16[32,64,64]{2,1,0:T(8,128)(2,1)} %box_matrices.1) | copy-start | bytes 786436
  60.7 0.9 %copy-start.16 = (bf16[8,2,64,64]{3,2,1,0:T(8,128)(2,1)S(1)}, bf16[8,2,64,64]{3,2,1,0:T(8,128)(2,1)}, u32[]{:S(2)}) copy-start(bf16[8,2,64,64]{3,2,1,0:T(8,128)(2,1)} %down.1) | copy-start | bytes 393220
  61.7 4.8 %copy-start.18 = (bf16[24,32,128]{2,1,0:T(8,128)(2,1)S(1)}, bf16[24,32,128]{2,1,0:T(8,128)(2,1)}, u32[]{:S(2)}) copy-start(bf16[24,32,128]{2,1,0:T(8,128)(2,1)} %get-tuple-element.21.refs_2_) | copy-start | bytes 589828
  61.7 4.8 %copy-start.22 = (s32[688]{0:T(1024)S(1)}, s32[688]{0:T(1024)}, u32[]{:S(2)}) copy-start(s32[688]{0:T(1024)} %get-tuple-element.30.refs_1_) | copy-start | bytes 8260
  66.4 6.2 %copy-start.4 = (f32[6,64,64]{2,1,0:T(8,128)}, f32[6,64,64]{2,1,0:T(8,128)S(1)}, u32[]{:S(2)}) copy-start(f32[6,64,64]{2,1,0:T(8,128)S(1)} %get-tuple-element.28.box_field) | copy-start | bytes 294916
  66.4 6.2 %copy-start.7 = (f32[64,64]{1,0:T(8,128)}, f32[64,64]{1,0:T(8,128)S(1)}, u32[]{:S(2)}) copy-start(f32[64,64]{1,0:T(8,128)S(1)} %get-tuple-element.25.base) | copy-start | bytes 49156
  66.5 6.2 %copy-start.21 = (s32[688]{0:T(1024)S(1)}, s32[688]{0:T(1024)}, u32[]{:S(2)}) copy-start(s32[688]{0:T(1024)} %get-tuple-element.29.refs_1_) | copy-start | bytes 8260
  72.7 7.5 %copy-start.6 = (bf16[6,64,64]{2,1,0:T(8,128)(2,1)S(1)}, bf16[6,64,64]{2,1,0:T(8,128)(2,1)}, u32[]{:S(2)}) copy-start(bf16[6,64,64]{2,1,0:T(8,128)(2,1)} %box_down.1) | copy-start | bytes 147460
  78.7 1.5 %copy-start = (bf16[64,3072]{1,0:T(8,128)(2,1)S(1)}, bf16[64,3072]{1,0:T(8,128)(2,1)}, u32[]{:S(2)}) copy-start(bf16[64,3072]{1,0:T(8,128)(2,1)} %basis.1) | copy-start | bytes 1179652
  78.7 1.5 %copy-start.2 = (bf16[24,64,64]{2,1,0:T(8,128)(2,1)S(1)}, bf16[24,64,64]{2,1,0:T(8,128)(2,1)}, u32[]{:S(2)}) copy-start(bf16[24,64,64]{2,1,0:T(8,128)(2,1)} %leaf_down.1) | copy-start | bytes 589828
  80.8 0.9 %copy-start.5 = (f32[6,64,64]{2,1,0:T(8,128)S(1)}, f32[6,64,64]{2,1,0:T(8,128)}, u32[]{:S(2)}) copy-start(f32[6,64,64]{2,1,0:T(8,128)} %copy-done.4) | copy-start | bytes 294916
  81.7 0.8 copy-start.8
  (3 other events, 1.9 us)

commit v4 on v3

v4 whole, which is shorter than its diff:
```python
import math

import jax
import jax.numpy as jnp
import numpy as np
from jax import lax
from jax.experimental import pallas as pl
from jax.experimental.pallas import tpu as pltpu
from jax.sharding import PartitionSpec as P

BF = jnp.bfloat16
F32 = jnp.float32
AXES = ("box", "rhs")

R = 64
K = 64
M = 128
LD = 24
BX = 6
ADM = 16
ADMB = 8
NEAR = 27
FR = 16
ROWS = R + FR
FX = 32
UNROLL = 16
LOW = 32
PAIRS = (LD + BX) // 2
SENT = LD + PAIRS * R // ROWS
SLOTS = LD * (NEAR + 1) + 2 * UNROLL + 32
ALL = 3 * LD

DELTA2 = 0.0001
INV_SCALE = 2.0 * math.sqrt(NEAR * M)
CENTRE = 1.1

PARTS = ((0, 0), (0, 1), (0, 2), (1, 0), (1, 1), (1, 2), (2, 0), (2, 1))

VMEM = pl.BlockSpec(memory_space=pltpu.VMEM)
SMEM = pl.BlockSpec(memory_space=pltpu.SMEM)
ANY = pl.BlockSpec(memory_space=pl.ANY)
HBM = pl.BlockSpec(memory_space=pltpu.HBM)


def params(mib=24):
    return pltpu.CompilerParams(vmem_limit_bytes=mib * 1024 * 1024)


def sds(shape, dtype):
    return jax.ShapeDtypeStruct(shape, dtype)


def dot(a, b):
    return jnp.dot(a, b, preferred_element_type=F32)


def dot_nt(a, b):
    return lax.dot_general(a, b, (((1,), (1,)), ((), ())), preferred_element_type=F32)


def dot2(x, m):
    hi = x.astype(BF)
    lo = (x - hi.astype(F32)).astype(BF)
    return dot(hi, m) + dot(lo, m)


def expansion(leaf):
    row = lax.broadcasted_iota(jnp.int32, (8 * FR, M), 0) - FR * leaf
    e = lax.broadcasted_iota(jnp.int32, (8 * FR, M), 1)
    third = (e * 43) >> 7
    part = jnp.where(e < 9, 0, jnp.where(e < 18, 3, 6))
    source = jnp.where(e < 24, part + e - 3 * third, jnp.where(e < 27, e - 15, jnp.where(e < 30, 12, -M)))
    return jnp.where(row == source, 1.0, 0.0).astype(BF)


def split3(x):
    hi = x.astype(BF).astype(F32)
    rest = x - hi
    mid = rest.astype(BF).astype(F32)
    return hi, mid, rest - mid


def load(copies):
    for copy in copies:
        copy.start()
    return copies


def first_body(charges_in, points_in, basis_in, leaf_up_in, box_up_in, parents, sent, target, ascent, charges, points, basis, leaf_up, box_up, feat, wide, acc, sems):
    moves = ((points_in, points), (charges_in, charges), (basis_in, basis), (leaf_up_in, leaf_up), (box_up_in, box_up))
    copies = load([pltpu.make_async_copy(a, b, sems.at[n]) for n, (a, b) in enumerate(moves)])
    acc[...] = jnp.zeros(acc.shape, F32)
    copies[1].wait()
    copies[2].wait()
    copies[3].wait()
    for group in range(LD // 8):
        leaves = range(8 * group, 8 * group + 8)
        c = [dot_nt(charges[:, pl.ds(leaf * M, M)], basis[:, pl.ds(leaf * M, M)]) for leaf in leaves]
        raised = [dot(c[i].astype(BF), leaf_up[leaf]) for i, leaf in enumerate(leaves)]
        for i in range(0, 8, 2):
            put_coef(sent, (8 * group + i) // 2, jnp.concatenate([c[i], c[i + 1]], axis=1).astype(BF))
        for i, leaf in enumerate(leaves):
            acc[parents[leaf]] += raised[i]
    copies[4].wait()
    copies[0].wait()
    boxes = [acc[box] for box in range(BX)]
    raised = [dot(boxes[box].astype(BF), box_up[box]) for box in range(BX)]
    total = raised[0] + raised[1] + (raised[2] + raised[3]) + (raised[4] + raised[5])
    packed = jnp.concatenate([total[: R // 2], total[R // 2 :]], axis=1).astype(BF)
    for i in range(LOW):
        ascent[i] = packed
    for box in range(0, BX, 2):
        put_coef(sent, (LD + box) // 2, jnp.concatenate([boxes[box], boxes[box + 1]], axis=1).astype(BF))

    p = (points[...] - CENTRE) * INV_SCALE
    parts = split3(p)
    norm = p[0:1] * p[0:1] + p[1:2] * p[1:2] + p[2:3] * p[2:3]
    source_norm = split3(norm)
    target_norm = split3(norm + DELTA2 * INV_SCALE * INV_SCALE)
    feat[...] = jnp.zeros(feat.shape, F32)
    wide[...] = jnp.zeros(wide.shape, F32)
    one = jnp.ones(norm.shape, F32)
    for a in range(3):
        feat[3 * a : 3 * a + 3, :] = parts[a]
        feat[9 + a : 10 + a, :] = source_norm[a]
    feat[12:13, :] = one
    for n, (_, b) in enumerate(PARTS):
        wide[3 * n : 3 * n + 3, :] = -2.0 * parts[b]
    base = 3 * len(PARTS)
    for a in range(3):
        wide[base + a : base + a + 1, :] = one
        wide[base + 3 + a : base + 4 + a, :] = target_norm[a]
    turned = []
    for o in range(LD // 8):
        rows = jnp.concatenate([feat[:, pl.ds((8 * o + i) * M, M)] for i in range(8)], axis=0)
        turned.append(rows.T.astype(BF))
    for leaf in range(LD):
        cols = pl.ds(leaf * M, M)
        sent[leaf, 0:R, :] = charges[:, cols]
        i = leaf % 8
        sent[leaf, R:ROWS, :] = turned[leaf // 8][FR * i : FR * (i + 1), :]
        target[leaf, :, :] = wide[:, cols].astype(BF)


def coef_places(pair):
    rows = [pair * R + 16 * i for i in range(R // 16)]
    return [(r // ROWS, r % ROWS) for r in rows]


def put_coef(sent, pair, value):
    for i, (block, row) in enumerate(coef_places(pair)):
        sent[LD + block, row : row + 16, :] = value[16 * i : 16 * i + 16]


def first(charges, points, basis, leaf_up, box_up, parents):
    return pl.pallas_call(
        first_body,
        in_specs=[HBM] * 5 + [SMEM],
        out_specs=[VMEM] * 3,
        out_shape=[
            sds((SENT, ROWS, M), BF),
            sds((LD, FX, M), BF),
            sds((LOW, R // 2, 2 * K), BF),
        ],
        scratch_shapes=[
            pltpu.VMEM((R, LD * M), BF),
            pltpu.VMEM((3, LD * M), F32),
            pltpu.VMEM((K, LD * M), BF),
            pltpu.VMEM((LD, K, K), BF),
            pltpu.VMEM((BX, K, K), BF),
            pltpu.VMEM((FR, LD * M), F32),
            pltpu.VMEM((FX, LD * M), F32),
            pltpu.VMEM((BX, R, K), F32),
            pltpu.SemaphoreType.DMA((5,)),
        ],
        compiler_params=params(60),
        name="points_to_group",
    )(charges, points, basis, leaf_up, box_up, parents)


def twice(m):
    zero = jnp.zeros_like(m)
    return jnp.concatenate([jnp.concatenate([m, zero], axis=1), jnp.concatenate([zero, m], axis=1)], axis=0)


def unpack(x):
    return jnp.concatenate([x[:, :K], x[:, K:]], axis=0)


def raise_nodes(nodes, matrices):
    count = nodes.shape[0] // 2
    left = jnp.concatenate([nodes[2 * i] for i in range(count)], axis=0)
    right = jnp.concatenate([nodes[2 * i + 1] for i in range(count)], axis=0)
    mul = dot if nodes.dtype == BF else dot2
    return (mul(left, twice(matrices[0])) + mul(right, twice(matrices[1]))).reshape(count, R // 2, 2 * K)


def low_body(place, nodes, up, coupling, top, field, held):
    levels = [nodes[...]]
    for h in range(4):
        levels.append(raise_nodes(levels[h], (up[h, 0], up[h, 1])))
    packed = levels[4].astype(BF).reshape(R, 2 * K)
    for i in range(top.shape[0]):
        top[i] = packed
    start = 0
    for h in range(4):
        held[start : start + (LOW >> h)] = levels[h].astype(F32)
        start += LOW >> h
    me = place[0] & (LOW - 1)
    start = 0
    out = []
    for h in range(4):
        q = me >> h
        near, far = unpack(held[(q ^ 2) + start]), unpack(held[(q ^ 3) + start])
        out.append(dot2(near, coupling[h, 0]) + dot2(far, coupling[h, 1]))
        start += LOW >> h
    for h in range(4):
        field[h] = out[h]


def low_tree(place, nodes, up, coupling, blocks):
    return pl.pallas_call(
        low_body,
        in_specs=[SMEM, VMEM, VMEM, VMEM],
        out_specs=[VMEM, VMEM],
        out_shape=[sds((blocks, R, 2 * K), BF), sds((4, R, K), F32)],
        scratch_shapes=[pltpu.VMEM((2 * LOW, R // 2, 2 * K), F32)],
        compiler_params=params(),
        name="coarse_low",
    )(place, nodes, up, coupling)


def split2(x):
    hi = x.astype(BF)
    return hi, (x - hi.astype(F32)).astype(BF)


def fields_body(near_leaves, near_count, leaf_sources, leaf_classes, box_sources, box_classes, place, low_field, down, coupling, target_in, matrices_in, box_matrices_in, left, mine, right, acc, leaf_field, box_field, base, tip, table, coefs, feats, target, matrices, box_matrices, low, high, slots, sems):
    blocks = SENT - LD
    sources = (left, mine, right)
    moves = [(src.at[pl.ds(0, LD)], table.at[pl.ds(n * LD, LD)]) for n, src in enumerate(sources)]
    moves += [(src.at[pl.ds(LD, blocks)], coefs.at[pl.ds(n * blocks, blocks)]) for n, src in enumerate(sources)]
    moves += [(target_in, target), (matrices_in, matrices), (box_matrices_in, box_matrices)]
    copies = load([pltpu.make_async_copy(a, b, sems.at[n]) for n, (a, b) in enumerate(moves)])

    me = place[0]
    at = jnp.int32(0)
    for t in range(LD):
        shift = (t << 8) - (me - 1) * LD
        for part in range(0, NEAR, 9):
            row = [near_leaves[t, part + s] for s in range(9)]
            for s in range(9):
                slots[at + part + s] = row[s] + shift
        slots[at + near_count[t]] = t << 8 | ALL
        at = at + ((near_count[t] + 1) & -2)
    for i in range(2 * UNROLL):
        slots[at + i] = LD << 8 | ALL

    total = low_field[3]
    chain = down[3, (me >> 3) & 1].astype(F32)
    for h in range(2, -1, -1):
        both = dot2(jnp.concatenate([total, chain], axis=0), down[h, (me >> h) & 1])
        total = low_field[h] + both[:R]
        chain = both[R:]
    tips = []
    for h in range(4, 8):
        hi, lo = split2(chain)
        stack = jnp.concatenate([coupling[h, 0], coupling[h, 1], down[min(h, 6), (me >> h) & 1]], axis=0)
        product = dot(stack, hi) + dot(stack, lo)
        tips.append((split2(product[0:K]), split2(product[K : 2 * K])))
        chain = product[2 * K :]
    base[...] = total
    for h in range(4):
        for i in range(2):
            for n in range(2):
                tip[h, i, n] = tips[h][i][n]

    acc[...] = jnp.zeros(acc.shape, F32)
    table[ALL] = jnp.zeros((ROWS, M), BF)
    lane = lax.broadcasted_iota(jnp.int32, (M, M), 1)
    ones = 3 * len(PARTS) + 3
    feats[ALL] = jnp.where((lane >= ones) & (lane < ones + 3), 1.0, 0.0).astype(BF)
    for copy in copies:
        copy.wait()

    first = lax.broadcasted_iota(jnp.int32, (R, 2 * K), 1) < K
    for n in range(3):
        for group in range(PAIRS // 5):
            ready = []
            for i in range(5 * group, 5 * group + 5):
                x = jnp.concatenate(
                    [coefs[n * blocks + b, r : r + 16, :] for b, r in coef_places(i)], axis=0
                ).astype(F32)
                y = pltpu.roll(x, K, 1)
                ready.append(
                    [
                        jnp.where(first, x, 0.0).astype(BF),
                        jnp.where(first, y, 0.0).astype(BF),
                        jnp.where(first, 0.0, y).astype(BF),
                        jnp.where(first, 0.0, x).astype(BF),
                    ]
                )
            for i in range(5):
                at_row = 2 * (5 * group + i)
                row = n * LD + at_row if at_row < LD else ALL + n * BX + at_row - LD
                low[row], low[row + 1], high[row], high[row + 1] = ready[i]

    def gather(sources, classes, row, mats, width, shift):
        total = jnp.zeros((R, K), F32)
        for g in range(width // 4):
            s = [sources[row, 4 * g + i] - shift for i in range(4)]
            vec = jnp.concatenate([low[s[0]] + high[s[1]], low[s[2]] + high[s[3]]], axis=1)
            mat = jnp.concatenate([mats[classes[row, 4 * g + i]] for i in range(4)], axis=0)
            total = total + dot(vec, mat)
        return total

    def couple(it, _):
        rows = [it * 8 + u for u in range(8)]
        got = [gather(leaf_sources, leaf_classes, row, matrices, ADM, (me - 1) * LD) for row in rows]
        for row, value in zip(rows, got):
            leaf_field[row] = value
        return 0

    lax.fori_loop(0, LD // 8, couple, 0)
    got = [gather(box_sources, box_classes, box, box_matrices, ADMB, (me - 1) * BX - ALL) for box in range(BX)]
    for box in range(BX):
        box_field[box] = got[box]

    expand = [expansion(i) for i in range(8)]
    for o in range(ALL // 8):
        rows = jnp.concatenate([table[8 * o + i, R:ROWS, :] for i in range(8)], axis=0)
        spread = [dot(rows, expand[i]).astype(BF) for i in range(8)]
        for i in range(8):
            feats[8 * o + i] = spread[i]
    pad = jnp.zeros((M - FX, M), BF)

    def near(it, _):
        t, kernels, weights = [], [], []
        for u in range(UNROLL):
            place_of = (it * UNROLL + u) * 2
            one, two = slots[place_of], slots[place_of + 1]
            s0, s1 = one & 255, two & 255
            t.append(one >> 8)
            rows = jnp.concatenate([feats[s0], feats[s1]], axis=0)
            square = dot(rows, jnp.concatenate([target[jnp.minimum(t[u], LD - 1)], pad], axis=0))
            kernels.append(lax.rsqrt(square).astype(BF))
            weights.append(jnp.concatenate([table[s0, 0:R, :], table[s1, 0:R, :]], axis=1))
        terms = [dot(weights[u], kernels[u]) for u in range(UNROLL)]
        for u in range(UNROLL):
            acc[t[u]] += terms[u]
        return 0

    lax.fori_loop(0, (at // 2 + UNROLL - 1) // UNROLL, near, 0)


def fields(indices, place, low_field, down, coupling, target, matrices, box_matrices, sents):
    return pl.pallas_call(
        fields_body,
        in_specs=[SMEM] * 7 + [VMEM] * 3 + [ANY] * 6,
        out_specs=[VMEM] * 5,
        out_shape=[
            sds((LD + 1, R, M), F32),
            sds((LD, R, K), F32),
            sds((BX, R, K), F32),
            sds((R, K), F32),
            sds((4, 2, 2, K, K), BF),
        ],
        scratch_shapes=[
            pltpu.VMEM((ALL + 1, ROWS, M), BF),
            pltpu.VMEM((3 * (SENT - LD), ROWS, M), BF),
            pltpu.VMEM((ALL + 1, M, M), BF),
            pltpu.VMEM((LD, FX, M), BF),
            pltpu.VMEM((matrices.shape[0], K, K), BF),
            pltpu.VMEM((matrices.shape[0], K, K), BF),
            pltpu.VMEM((6 * PAIRS, R, 2 * K), BF),
            pltpu.VMEM((6 * PAIRS, R, 2 * K), BF),
            pltpu.SMEM((SLOTS,), jnp.int32),
            pltpu.SemaphoreType.DMA((9,)),
        ],
        compiler_params=params(),
        cost_estimate=pl.CostEstimate(flops=8 << 30, bytes_accessed=4 << 20, transcendentals=8 << 20),
        name="near_and_coupled_fields",
    )(*indices, place, low_field, down, coupling, target, matrices, box_matrices, *sents)


def final_body(place, nodes, up, base, tip, parents, leaf_field_in, box_field, box_down, leaf_down_in, basis_in, near_in, out, boxes, held, leaf_field, leaf_down, basis, near_part, sems):
    moves = ((leaf_field_in, leaf_field), (leaf_down_in, leaf_down), (basis_in, basis), (near_in, near_part))
    copies = load([pltpu.make_async_copy(a, b, sems.at[n]) for n, (a, b) in enumerate(moves)])
    levels = [nodes[...].reshape(LOW, R // 2, 2 * K)]
    for h in range(3):
        levels.append(raise_nodes(levels[h], (up[4 + h, 0], up[4 + h, 1])))
    start = 0
    for h in range(4):
        held[start : start + (LOW >> h)] = levels[h].astype(F32)
        start += LOW >> h
    me = (place[0] >> 4) & (LOW - 1)
    total = base[...]
    start = 0
    for h in range(4):
        for i in range(2):
            hi, lo = split2(unpack(held[((me >> h) ^ (2 + i)) + start]))
            total = total + (dot(hi, tip[h, i, 0]) + dot(hi, tip[h, i, 1]) + dot(lo, tip[h, i, 0]))
        start += LOW >> h
    for copy in copies:
        copy.wait()
    group = total.astype(BF)
    got = [(box_field[box] + dot(group, box_down[box])).astype(BF) for box in range(BX)]
    for box in range(BX):
        boxes[box] = got[box]
    for part in range(LD // 8):
        leaves = range(8 * part, 8 * part + 8)
        field = [
            (leaf_field[leaf] + dot(boxes[parents[leaf]], leaf_down[leaf])).astype(BF) for leaf in leaves
        ]
        got = [
            near_part[leaf] + dot(field[i], basis[:, pl.ds(leaf * M, M)]) for i, leaf in enumerate(leaves)
        ]
        for i, leaf in enumerate(leaves):
            out[:, pl.ds(leaf * M, M)] = got[i]


def finish(place, nodes, up, base, tip, parents, leaf_field, box_field, box_down, leaf_down, basis, near_part):
    return pl.pallas_call(
        final_body,
        in_specs=[SMEM] + [VMEM] * 4 + [SMEM, ANY, VMEM, VMEM] + [ANY] * 3,
        out_specs=VMEM,
        out_shape=sds((R, LD * M), F32),
        scratch_shapes=[
            pltpu.VMEM((BX, R, K), BF),
            pltpu.VMEM((2 * LOW, R // 2, 2 * K), F32),
            pltpu.VMEM((LD, R, K), F32),
            pltpu.VMEM((LD, K, K), BF),
            pltpu.VMEM((K, LD * M), BF),
            pltpu.VMEM((LD + 1, R, M), F32),
            pltpu.SemaphoreType.DMA((4,)),
        ],
        compiler_params=params(),
        name="group_to_points",
    )(place, nodes, up, base, tip, parents, leaf_field, box_field, box_down, leaf_down, basis, near_part)


def exchange(x):
    count = lax.axis_size(AXES)
    left = lax.ppermute(x, AXES, [(i, i + 1) for i in range(count - 1)])
    right = lax.ppermute(x, AXES, [(i + 1, i) for i in range(count - 1)])
    return left, right


def gather_groups(copies, groups):
    return lax.all_to_all(copies, AXES, 0, 0, axis_index_groups=groups, tiled=True)


def local(
    charges,
    points,
    leaf_basis,
    leaf_parent,
    leaf_up,
    leaf_down,
    box_up,
    box_down,
    top_up,
    top_down,
    top_coupling,
    leaf_sources,
    leaf_classes,
    leaf_coupling,
    box_sources,
    box_classes,
    box_coupling,
    near_leaves,
    near_count,
):
    device = lax.axis_index(AXES)
    place = device.astype(jnp.int32).reshape(1)
    parents = leaf_parent[0]

    sent, target, ascent = first(charges, points, leaf_basis, leaf_up, box_up, parents)

    blocks = lax.axis_size(AXES) // LOW
    low_groups = [[b * LOW + i for i in range(LOW)] for b in range(blocks)]
    high_groups = [[b * LOW + i for b in range(blocks)] for i in range(LOW)]
    low_nodes = gather_groups(ascent, low_groups)
    sent_left, sent_right = exchange(sent)
    top, low_field = low_tree(place, low_nodes, top_up, top_coupling, blocks)
    high_nodes = gather_groups(top, high_groups)

    near_part, leaf_field, box_field, base, tip = fields(
        (near_leaves, near_count, leaf_sources, leaf_classes, box_sources, box_classes),
        place,
        low_field,
        top_down,
        top_coupling,
        target,
        leaf_coupling,
        box_coupling,
        (sent_left, sent, sent_right),
    )
    return finish(
        place, high_nodes, top_up, base, tip, parents, leaf_field, box_field, box_down, leaf_down, leaf_basis, near_part
    )


def solution(mesh):
    split = P(AXES)
    return jax.shard_map(
        local,
        mesh=mesh,
        in_specs=(
            P(None, AXES),
            P(None, AXES),
            P(None, AXES),
            split,
            split,
            split,
            split,
            split,
            P(),
            P(),
            P(),
            split,
            split,
            P(),
            split,
            split,
            P(),
            split,
            split,
        ),
        out_specs=P(None, AXES),
        check_vma=False,
    )
```

time: 86.8 us -> 91.7 us (1.056)
  the two profiles are of different devices: /device:TPU:32 before, /device:TPU:7 now
where the time goes in v4:
time: 91.7 us; the launch traced here: 90.8 us
  starting transfers between devices  31.8 us (35%)
  Pallas kernels  27 us (29%)
  local copies, waits for them, and re-layouts  18.4 us (20%)
  waiting for transfers between devices  13.4 us (15%)
    all_to_all x2, starting transfers between devices, gather_groups(): lax.all_to_all(copies, AXES, 0, 0, axis_index_groups=groups, tiled=True)  24.6 us
    unnamed x58, local copies, waits for them, and re-layouts  18.4 us
    pallas_call x1, Pallas kernels, fields(): pl.pallas_call(fields_body, in_specs=[SMEM] * 7 + [VMEM] * 3 + [ANY] * 6,...  17.5 us
    all_to_all x2, waiting for transfers between devices, gather_groups(): lax.all_to_all(copies, AXES, 0, 0, axis_index_groups=groups, tiled=True)  13.4 us
    ppermute x1, starting transfers between devices, exchange(): right = lax.ppermute(x, AXES, [(i + 1, i) for i in range(count - 1)])  5.2 us
    pallas_call x1, Pallas kernels, first(): pl.pallas_call(first_body, in_specs=[HBM] * 5 + [SMEM], out_specs=[VMEM]...  4.01 us
    pallas_call x1, Pallas kernels, finish(): pl.pallas_call(final_body, in_specs=[SMEM] + [VMEM] * 4 + [SMEM, ANY, VME...  3.9 us
    ppermute x1, starting transfers between devices, exchange(): left = lax.ppermute(x, AXES, [(i, i + 1) for i in range(count - 1)])  1.92 us
  transfers between devices with their start and end apart: 4, of which 1 were waited for; matrix products, arithmetic and copies ran while one was open for 1% of the time, Pallas kernels for 21%

profile of v4, /device:TPU:7, one launch (start us, length us, event | category | flops | bytes accessed | tf_op | source)
XLA Modules:
  0.0 90.8 jit_solution(16776944203600368764)
XLA Ops:
  0.0 4.0 %points_to_group.1 = (bf16[36,80,128]{2,1,0:T(8,128)(2,1)}, bf16[24,32,128]{2,1,0:T(8,128)(2,1)}, bf16[32,32,128]{2,1,0:T(8,128)(2,1)}) custom-call(bf16[64,3072]{1,0:T(8,128)(2,1)} %charges_in.1, f32[3,3072]{1,0:T(4,128)} %points_in.1, bf16[64,3072]{1,0:T(8,128)(2,1)} %basis_in.3, bf16[24,64,64]{2,1,0:T(8,128)(2,1)} %leaf_up_in.1, ...), custom_call_target="tpu_custom_call" | custom-call | tf_op jit(solution)/shard_map/points_to_group/pallas_call | solution.py:156
  4.0 5.2 %collective-permute-start.1 = (bf16[36,80,128]{2,1,0:T(8,128)(2,1)}, bf16[36,80,128]{2,1,0:T(8,128)(2,1)S(1)}, u32[]{:S(2)}, u32[]{:S(2)}) collective-permute-start(bf16[36,80,128]{2,1,0:T(8,128)(2,1)} %get-tuple-element.19.mine), channel_id=1, source_target_pairs={{1,0},{2,1},{3,2},{4,3},{5,4},{6,5},{7,6},{8,7},{9,8},{10,9},{11,1... | collective-permute-start | bytes 2211848 | tf_op jit(solution)/shard_map/ppermute | solution.py:445
  9.2 1.9 %collective-permute-start = (bf16[36,80,128]{2,1,0:T(8,128)(2,1)}, bf16[36,80,128]{2,1,0:T(8,128)(2,1)S(1)}, u32[]{:S(2)}, u32[]{:S(2)}) collective-permute-start(bf16[36,80,128]{2,1,0:T(8,128)(2,1)} %get-tuple-element.19.mine), channel_id=1, source_target_pairs={{0,1},{1,2},{2,3},{3,4},{4,5},{5,6},{6,7},{7,8},{8,9},{9,10},{10,1... | collective-permute-start | bytes 2211848 | tf_op jit(solution)/shard_map/ppermute | solution.py:444
  11.2 9.7 %all-to-all-start = ((bf16[32,32,128]{2,1,0:T(8,128)(2,1)}), bf16[32,32,128]{2,1,0:T(8,128)(2,1)S(1)}, u32[]{:S(2)}, u32[]{:S(2)}) async-start(bf16[32,32,128]{2,1,0:T(8,128)(2,1)} %get-tuple-element.15), calls=%async_computation | async-start | bytes 524288 | tf_op jit(solution)/shard_map/all_to_all | solution.py:450
  20.9 13.4 %all-to-all-done.nodes = bf16[32,32,128]{2,1,0:T(8,128)(2,1)S(1)} async-done(((bf16[32,32,128]{2,1,0:T(8,128)(2,1)}), bf16[32,32,128]{2,1,0:T(8,128)(2,1)S(1)}, u32[]{:S(2)}, u32[]{:S(2)}) %all-to-all-start) | async-done | bytes 262176 | tf_op jit(solution)/shard_map/all_to_all | solution.py:450
  34.4 1.6 %coarse_low.1 = (bf16[16,64,128]{2,1,0:T(8,128)(2,1)}, f32[4,64,64]{2,1,0:T(8,128)S(1)}) custom-call(s32[1]{0:T(128)} %bitcast.place, bf16[32,32,128]{2,1,0:T(8,128)(2,1)S(1)} %all-to-all-done.nodes, bf16[8,2,64,64]{3,2,1,0:T(8,128)(2,1)S(1)} %copy-done.1, bf16[8,2,64,64]{3,2,1,0:T(8,128)(2,1)S(1)} %copy-done.3), custom_call_target="tpu_custom_call" | custom-call | tf_op jit(solution)/shard_map/coarse_low/pallas_call | solution.py:222
  36.0 0.6 copy-done.20
  36.6 14.9 %all-to-all-start.1 = ((bf16[16,64,128]{2,1,0:T(8,128)(2,1)}), bf16[16,64,128]{2,1,0:T(8,128)(2,1)S(1)}, u32[]{:S(2)}, u32[]{:S(2)}) async-start(bf16[16,64,128]{2,1,0:T(8,128)(2,1)} %get-tuple-element.16), calls=%async_computation.1 | async-start | bytes 524288 | tf_op jit(solution)/shard_map/all_to_all | solution.py:450
  51.6 0.1 copy.20.leaf_sources
  51.7 0.6 copy-done.27
  52.3 0.7 copy.21.leaf_classes
  52.9 0.9 %copy-done.12 = bf16[36,80,128]{2,1,0:T(8,128)(2,1)} copy-done((bf16[36,80,128]{2,1,0:T(8,128)(2,1)}, bf16[36,80,128]{2,1,0:T(8,128)(2,1)S(1)}, u32[]{:S(2)}) %copy-start.12) | copy-done | bytes 737304
  53.9 0.9 copy-done.14
  54.8 0.7 copy-done.25
  55.4 0.7 copy-done.9
  56.1 1.1 %copy-done.11 = bf16[36,80,128]{2,1,0:T(8,128)(2,1)S(1)} copy-done((bf16[36,80,128]{2,1,0:T(8,128)(2,1)S(1)}, bf16[36,80,128]{2,1,0:T(8,128)(2,1)}, u32[]{:S(2)}) %copy-start.11) | copy-done | bytes 737304
  57.2 1.1 %copy-done.13 = bf16[36,80,128]{2,1,0:T(8,128)(2,1)S(1)} copy-done((bf16[36,80,128]{2,1,0:T(8,128)(2,1)S(1)}, bf16[36,80,128]{2,1,0:T(8,128)(2,1)}, u32[]{:S(2)}) %copy-start.13) | copy-done | bytes 737304
  58.4 1.1 %copy-done.15 = bf16[36,80,128]{2,1,0:T(8,128)(2,1)S(1)} copy-done((bf16[36,80,128]{2,1,0:T(8,128)(2,1)S(1)}, bf16[36,80,128]{2,1,0:T(8,128)(2,1)}, u32[]{:S(2)}) %copy-start.15) | copy-done | bytes 737304
  59.5 1.0 %copy-done.16 = bf16[32,64,64]{2,1,0:T(8,128)(2,1)S(1)} copy-done((bf16[32,64,64]{2,1,0:T(8,128)(2,1)S(1)}, bf16[32,64,64]{2,1,0:T(8,128)(2,1)}, u32[]{:S(2)}) %copy-start.16) | copy-done | bytes 262168
  60.5 1.0 %copy-done.17 = bf16[32,64,64]{2,1,0:T(8,128)(2,1)S(1)} copy-done((bf16[32,64,64]{2,1,0:T(8,128)(2,1)S(1)}, bf16[32,64,64]{2,1,0:T(8,128)(2,1)}, u32[]{:S(2)}) %copy-start.17) | copy-done | bytes 262168
  61.6 0.9 %copy-done.18 = bf16[8,2,64,64]{3,2,1,0:T(8,128)(2,1)S(1)} copy-done((bf16[8,2,64,64]{3,2,1,0:T(8,128)(2,1)S(1)}, bf16[8,2,64,64]{3,2,1,0:T(8,128)(2,1)}, u32[]{:S(2)}) %copy-start.18) | copy-done | bytes 131096
  62.5 0.9 %copy-done.19 = bf16[24,32,128]{2,1,0:T(8,128)(2,1)S(1)} copy-done((bf16[24,32,128]{2,1,0:T(8,128)(2,1)S(1)}, bf16[24,32,128]{2,1,0:T(8,128)(2,1)}, u32[]{:S(2)}) %copy-start.19) | copy-done | bytes 196632
  63.4 0.9 copy-done.21
  64.3 0.7 copy-done.22
  65.1 0.7 copy-done.24
  65.7 17.5 %near_and_coupled_fields.1 = (f32[25,64,128]{2,1,0:T(8,128)S(1)}, f32[24,64,64]{2,1,0:T(8,128)S(1)}, f32[6,64,64]{2,1,0:T(8,128)S(1)}, f32[64,64]{1,0:T(8,128)S(1)}, bf16[4,2,2,64,64]{4,3,2,1,0:T(8,128)(2,1)S(1)}) custom-call(s32[24,27]{1,0:T(8,128)S(1)} %copy-done.22, s32[24]{0:T(128)S(1)} %copy-done.25, s32[24,16]{1,0:T(8,128)S(1)} %copy.20.leaf_sources, ...), custom_call_target="tpu_custom_call" | custom-call | flops 8589934592 | bytes 4194304 | tf_op jit(solution)/shard_map/near_and_coupled_fields/pallas_call | solution.py:357
  83.3 0.7 copy-done.4
  83.9 0.6 copy-done.7
  84.6 0.6 copy-done.10
  85.2 0.9 %copy-done.5 = f32[6,64,64]{2,1,0:T(8,128)S(1)} copy-done((f32[6,64,64]{2,1,0:T(8,128)S(1)}, f32[6,64,64]{2,1,0:T(8,128)}, u32[]{:S(2)}) %copy-start.5) | copy-done | bytes 98328
  86.1 0.8 copy-done.8
  86.9 3.9 %group_to_points.1 = f32[64,3072]{1,0:T(8,128)} custom-call(s32[1]{0:T(128)} %bitcast.place, bf16[16,64,128]{2,1,0:T(8,128)(2,1)S(1)} %all-to-all-done.1.nodes, bf16[8,2,64,64]{3,2,1,0:T(8,128)(2,1)S(1)} %copy-done.1, f32[64,64]{1,0:T(8,128)S(1)} %copy-done.8, bf16[4,2,2,64,64]{4,3,2,1,0:T(8,128)(2,1)S(1)} %get-tuple-element.21.tip, s32[24]{0:T(128)S(1)} %bitcast.3, ...), custom_call_target="tpu_custom_call" | custom-call | tf_op jit(solution)/shard_map/group_to_points/pallas_call | solution.py:423
  (38 shorter events, 0.1 us)
Async XLA Ops:
  4.0 48.9 %collective-permute-start.1 = (bf16[36,80,128]{2,1,0:T(8,128)(2,1)}, bf16[36,80,128]{2,1,0:T(8,128)(2,1)S(1)}, u32[]{:S(2)}, u32[]{:S(2)}) collective-permute-start(bf16[36,80,128]{2,1,0:T(8,128)(2,1)} %get-tuple-element.19.mine), channel_id=1, source_target_pairs={{1,0},{2,1},{3,2},{4,3},{5,4},{6,5},{7,6},{8,7},{9,8},{10,9},{11,1... | collective-permute-start | bytes 2211848 | tf_op jit(solution)/shard_map/ppermute | solution.py:445
  9.2 44.6 %collective-permute-start = (bf16[36,80,128]{2,1,0:T(8,128)(2,1)}, bf16[36,80,128]{2,1,0:T(8,128)(2,1)S(1)}, u32[]{:S(2)}, u32[]{:S(2)}) collective-permute-start(bf16[36,80,128]{2,1,0:T(8,128)(2,1)} %get-tuple-element.19.mine), channel_id=1, source_target_pairs={{0,1},{1,2},{2,3},{3,4},{4,5},{5,6},{6,7},{7,8},{8,9},{9,10},{10,1... | collective-permute-start | bytes 2211848 | tf_op jit(solution)/shard_map/ppermute | solution.py:444
  11.2 23.2 %copy-start.1 = (bf16[8,2,64,64]{3,2,1,0:T(8,128)(2,1)S(1)}, bf16[8,2,64,64]{3,2,1,0:T(8,128)(2,1)}, u32[]{:S(2)}) copy-start(bf16[8,2,64,64]{3,2,1,0:T(8,128)(2,1)} %up.3) | copy-start | bytes 393220
  11.2 23.2 %copy-start.3 = (bf16[8,2,64,64]{3,2,1,0:T(8,128)(2,1)S(1)}, bf16[8,2,64,64]{3,2,1,0:T(8,128)(2,1)}, u32[]{:S(2)}) copy-start(bf16[8,2,64,64]{3,2,1,0:T(8,128)(2,1)} %coupling.3) | copy-start | bytes 393220
  11.2 23.2 %all-to-all-start = ((bf16[32,32,128]{2,1,0:T(8,128)(2,1)}), bf16[32,32,128]{2,1,0:T(8,128)(2,1)S(1)}, u32[]{:S(2)}, u32[]{:S(2)}) async-start(bf16[32,32,128]{2,1,0:T(8,128)(2,1)} %get-tuple-element.15), calls=%async_computation | async-start | bytes 524288 | tf_op jit(solution)/shard_map/all_to_all | solution.py:450
  36.0 0.7 copy-start.20
  36.0 15.6 %copy-start.26 = (s32[24,16]{0,1:T(8,128)S(1)}, s32[24,16]{0,1:T(8,128)}, u32[]{:S(2)}) copy-start(s32[24,16]{0,1:T(8,128)} %param.30) | copy-start | bytes 4612
  36.6 47.9 %all-to-all-start.1 = ((bf16[16,64,128]{2,1,0:T(8,128)(2,1)}), bf16[16,64,128]{2,1,0:T(8,128)(2,1)S(1)}, u32[]{:S(2)}, u32[]{:S(2)}) async-start(bf16[16,64,128]{2,1,0:T(8,128)(2,1)} %get-tuple-element.16), calls=%async_computation.1 | async-start | bytes 524288 | tf_op jit(solution)/shard_map/all_to_all | solution.py:450
  51.6 0.7 copy-start.27
  52.3 2.5 %copy-start.23 = (s32[6,8]{1,0:T(8,128)S(1)}, s32[6,8]{1,0:T(8,128)}, u32[]{:S(2)}) copy-start(s32[6,8]{1,0:T(8,128)} %box_sources.1) | copy-start | bytes 580
  52.9 0.9 %copy-start.12 = (bf16[36,80,128]{2,1,0:T(8,128)(2,1)}, bf16[36,80,128]{2,1,0:T(8,128)(2,1)S(1)}, u32[]{:S(2)}) copy-start(bf16[36,80,128]{2,1,0:T(8,128)(2,1)S(1)} %collective-permute-done.1.right) | copy-start | bytes 2211844
  53.9 0.9 copy-start.14
  54.8 0.7 copy-start.25
  55.4 0.7 copy-start.9
  56.1 1.1 %copy-start.11 = (bf16[36,80,128]{2,1,0:T(8,128)(2,1)S(1)}, bf16[36,80,128]{2,1,0:T(8,128)(2,1)}, u32[]{:S(2)}) copy-start(bf16[36,80,128]{2,1,0:T(8,128)(2,1)} %get-tuple-element.19.mine) | copy-start | bytes 2211844
  57.2 1.1 %copy-start.13 = (bf16[36,80,128]{2,1,0:T(8,128)(2,1)S(1)}, bf16[36,80,128]{2,1,0:T(8,128)(2,1)}, u32[]{:S(2)}) copy-start(bf16[36,80,128]{2,1,0:T(8,128)(2,1)} %copy-done.12) | copy-start | bytes 2211844
  58.4 1.1 %copy-start.15 = (bf16[36,80,128]{2,1,0:T(8,128)(2,1)S(1)}, bf16[36,80,128]{2,1,0:T(8,128)(2,1)}, u32[]{:S(2)}) copy-start(bf16[36,80,128]{2,1,0:T(8,128)(2,1)} %copy-done.14) | copy-start | bytes 2211844
  59.5 1.0 %copy-start.16 = (bf16[32,64,64]{2,1,0:T(8,128)(2,1)S(1)}, bf16[32,64,64]{2,1,0:T(8,128)(2,1)}, u32[]{:S(2)}) copy-start(bf16[32,64,64]{2,1,0:T(8,128)(2,1)} %matrices_in.1) | copy-start | bytes 786436
  60.5 1.0 %copy-start.17 = (bf16[32,64,64]{2,1,0:T(8,128)(2,1)S(1)}, bf16[32,64,64]{2,1,0:T(8,128)(2,1)}, u32[]{:S(2)}) copy-start(bf16[32,64,64]{2,1,0:T(8,128)(2,1)} %box_matrices_in.1) | copy-start | bytes 786436
  61.6 0.9 %copy-start.18 = (bf16[8,2,64,64]{3,2,1,0:T(8,128)(2,1)S(1)}, bf16[8,2,64,64]{3,2,1,0:T(8,128)(2,1)}, u32[]{:S(2)}) copy-start(bf16[8,2,64,64]{3,2,1,0:T(8,128)(2,1)} %down.1) | copy-start | bytes 393220
  62.5 0.9 %copy-start.19 = (bf16[24,32,128]{2,1,0:T(8,128)(2,1)S(1)}, bf16[24,32,128]{2,1,0:T(8,128)(2,1)}, u32[]{:S(2)}) copy-start(bf16[24,32,128]{2,1,0:T(8,128)(2,1)} %get-tuple-element.18.target_in) | copy-start | bytes 589828
  63.4 0.9 copy-start.21
  64.3 0.7 copy-start.22
  65.0 0.7 copy-start.24
  65.7 18.8 %copy-start = (bf16[64,3072]{1,0:T(8,128)(2,1)S(1)}, bf16[64,3072]{1,0:T(8,128)(2,1)}, u32[]{:S(2)}) copy-start(bf16[64,3072]{1,0:T(8,128)(2,1)} %basis_in.3) | copy-start | bytes 1179652
  65.7 18.8 %copy-start.2 = (bf16[24,64,64]{2,1,0:T(8,128)(2,1)S(1)}, bf16[24,64,64]{2,1,0:T(8,128)(2,1)}, u32[]{:S(2)}) copy-start(bf16[24,64,64]{2,1,0:T(8,128)(2,1)} %leaf_down_in.1) | copy-start | bytes 589828
  65.7 18.8 %copy-start.6 = (bf16[6,64,64]{2,1,0:T(8,128)(2,1)S(1)}, bf16[6,64,64]{2,1,0:T(8,128)(2,1)}, u32[]{:S(2)}) copy-start(bf16[6,64,64]{2,1,0:T(8,128)(2,1)} %box_down.1) | copy-start | bytes 147460
  83.3 0.7 copy-start.4
  83.9 0.6 copy-start.7
  84.6 0.7 copy-start.10
  85.2 0.9 %copy-start.5 = (f32[6,64,64]{2,1,0:T(8,128)S(1)}, f32[6,64,64]{2,1,0:T(8,128)}, u32[]{:S(2)}) copy-start(f32[6,64,64]{2,1,0:T(8,128)} %copy-done.4) | copy-start | bytes 294916
  86.1 0.8 copy-start.8

commit v5 on v4

--- a/solution.py
+++ b/solution.py
@@ -29,6 +29,7 @@
 SENT = LD + PAIRS * R // ROWS
 SLOTS = LD * (NEAR + 1) + 2 * UNROLL + 32
 ALL = 3 * LD
+BOTH = 2 * LD
 
 DELTA2 = 0.0001
 INV_SCALE = 2.0 * math.sqrt(NEAR * M)
@@ -42,8 +43,8 @@
 HBM = pl.BlockSpec(memory_space=pltpu.HBM)
 
 
-def params(mib=24):
-    return pltpu.CompilerParams(vmem_limit_bytes=mib * 1024 * 1024)
+def params(mib=60.0):
+    return pltpu.CompilerParams(vmem_limit_bytes=int(mib * 1024 * 1024))
 
 
 def sds(shape, dtype):
@@ -173,7 +174,7 @@
             pltpu.VMEM((BX, R, K), F32),
             pltpu.SemaphoreType.DMA((5,)),
         ],
-        compiler_params=params(60),
+        compiler_params=params(),
         name="points_to_group",
     )(charges, points, basis, leaf_up, box_up, parents)
 
@@ -225,7 +226,7 @@
         out_specs=[VMEM, VMEM],
         out_shape=[sds((blocks, R, 2 * K), BF), sds((4, R, K), F32)],
         scratch_shapes=[pltpu.VMEM((2 * LOW, R // 2, 2 * K), F32)],
-        compiler_params=params(),
+        compiler_params=params(63.5),
         name="coarse_low",
     )(place, nodes, up, coupling)
 
@@ -235,26 +236,102 @@
     return hi, (x - hi.astype(F32)).astype(BF)
 
 
-def fields_body(near_leaves, near_count, leaf_sources, leaf_classes, box_sources, box_classes, place, low_field, down, coupling, target_in, matrices_in, box_matrices_in, left, mine, right, acc, leaf_field, box_field, base, tip, table, coefs, feats, target, matrices, box_matrices, low, high, slots, sems):
+def used_slots(near_leaves, near_count, slots, me, halo):
+    null = BOTH if halo else LD
+    at = jnp.int32(0)
+    for t in range(LD):
+        used = near_count[t]
+        for part in range(0, NEAR, 9):
+            row = [near_leaves[t, part + s] - me * LD for s in range(9)]
+            for s, x in enumerate(row):
+                mine = jnp.logical_and(x >= 0, x < LD)
+                wanted = jnp.logical_not(mine) if halo else mine
+                if halo:
+                    x = jnp.where(x < 0, x + LD, x)
+                slots[at] = x + (t << 8)
+                at = at + jnp.where(jnp.logical_and(wanted, part + s < used), 1, 0)
+        slots[at] = t << 8 | null
+        at = (at + 1) & -2
+    for i in range(2 * UNROLL):
+        slots[at + i] = LD << 8 | null
+    return (at // 2 + UNROLL - 1) // UNROLL
+
+
+def spread_features(table, feats, count):
+    lane = lax.broadcasted_iota(jnp.int32, (M, M), 1)
+    ones = 3 * len(PARTS) + 3
+    feats[count] = jnp.where((lane >= ones) & (lane < ones + 3), 1.0, 0.0).astype(BF)
+    expand = [expansion(i) for i in range(8)]
+    for o in range(count // 8):
+        rows = jnp.concatenate([table[8 * o + i, R:ROWS, :] for i in range(8)], axis=0)
+        spread = [dot(rows, expand[i]).astype(BF) for i in range(8)]
+        for i in range(8):
+            feats[8 * o + i] = spread[i]
+
+
+def near_loop(steps, slots, table, feats, target, acc):
+    pad = jnp.zeros((M - FX, M), BF)
+
+    def near(it, _):
+        t, kernels, weights = [], [], []
+        for u in range(UNROLL):
+            place_of = (it * UNROLL + u) * 2
+            one, two = slots[place_of], slots[place_of + 1]
+            s0, s1 = one & 255, two & 255
+            t.append(one >> 8)
+            rows = jnp.concatenate([feats[s0], feats[s1]], axis=0)
+            square = dot(rows, jnp.concatenate([target[jnp.minimum(t[u], LD - 1)], pad], axis=0))
+            kernels.append(lax.rsqrt(square).astype(BF))
+            weights.append(jnp.concatenate([table[s0, 0:R, :], table[s1, 0:R, :]], axis=1))
+        terms = [dot(weights[u], kernels[u]) for u in range(UNROLL)]
+        for u in range(UNROLL):
+            acc[t[u]] += terms[u]
+        return 0
+
+    lax.fori_loop(0, steps, near, 0)
+
+
+def own_body(near_leaves, near_count, place, target_in, sent, acc, _, table, feats, target, slots, sems):
+    moves = ((sent.at[pl.ds(0, LD)], table.at[pl.ds(0, LD)]), (target_in, target))
+    copies = load([pltpu.make_async_copy(a, b, sems.at[n]) for n, (a, b) in enumerate(moves)])
+    steps = used_slots(near_leaves, near_count, slots, place[0], False)
+    acc[...] = jnp.zeros(acc.shape, F32)
+    table[LD] = jnp.zeros((ROWS, M), BF)
+    for copy in copies:
+        copy.wait()
+    spread_features(table, feats, LD)
+    near_loop(steps, slots, table, feats, target, acc)
+
+
+def near_own(near_leaves, near_count, place, target, sent):
+    return pl.pallas_call(
+        own_body,
+        in_specs=[SMEM] * 3 + [ANY] * 2,
+        out_specs=[VMEM, ANY],
+        out_shape=[sds((LD + 1, R, M), F32), sds(sent.shape, sent.dtype)],
+        input_output_aliases={4: 1},
+        scratch_shapes=[
+            pltpu.VMEM((LD + 1, ROWS, M), BF),
+            pltpu.VMEM((LD + 1, M, M), BF),
+            pltpu.VMEM((LD, FX, M), BF),
+            pltpu.SMEM((SLOTS,), jnp.int32),
+            pltpu.SemaphoreType.DMA((2,)),
+        ],
+        compiler_params=params(),
+        cost_estimate=pl.CostEstimate(flops=2 << 30, bytes_accessed=2 << 20, transcendentals=4 << 20),
+        name="near_own",
+    )(near_leaves, near_count, place, target, sent)
+
+
+def fields_body(near_leaves, near_count, leaf_sources, leaf_classes, box_sources, box_classes, place, low_field, down, coupling, near_in, target_in, matrices_in, box_matrices_in, left, mine, right, acc, leaf_field, box_field, base, tip, table, coefs, feats, target, matrices, box_matrices, low, high, slots, sems):
     blocks = SENT - LD
     sources = (left, mine, right)
-    moves = [(src.at[pl.ds(0, LD)], table.at[pl.ds(n * LD, LD)]) for n, src in enumerate(sources)]
+    moves = [(left.at[pl.ds(0, LD)], table.at[pl.ds(0, LD)]), (right.at[pl.ds(0, LD)], table.at[pl.ds(LD, LD)])]
     moves += [(src.at[pl.ds(LD, blocks)], coefs.at[pl.ds(n * blocks, blocks)]) for n, src in enumerate(sources)]
-    moves += [(target_in, target), (matrices_in, matrices), (box_matrices_in, box_matrices)]
+    moves += [(target_in, target), (matrices_in, matrices), (box_matrices_in, box_matrices), (near_in, acc)]
     copies = load([pltpu.make_async_copy(a, b, sems.at[n]) for n, (a, b) in enumerate(moves)])
-
     me = place[0]
-    at = jnp.int32(0)
-    for t in range(LD):
-        shift = (t << 8) - (me - 1) * LD
-        for part in range(0, NEAR, 9):
-            row = [near_leaves[t, part + s] for s in range(9)]
-            for s in range(9):
-                slots[at + part + s] = row[s] + shift
-        slots[at + near_count[t]] = t << 8 | ALL
-        at = at + ((near_count[t] + 1) & -2)
-    for i in range(2 * UNROLL):
-        slots[at + i] = LD << 8 | ALL
+    steps = used_slots(near_leaves, near_count, slots, me, True)
 
     total = low_field[3]
     chain = down[3, (me >> 3) & 1].astype(F32)
@@ -275,11 +352,7 @@
             for n in range(2):
                 tip[h, i, n] = tips[h][i][n]
 
-    acc[...] = jnp.zeros(acc.shape, F32)
-    table[ALL] = jnp.zeros((ROWS, M), BF)
-    lane = lax.broadcasted_iota(jnp.int32, (M, M), 1)
-    ones = 3 * len(PARTS) + 3
-    feats[ALL] = jnp.where((lane >= ones) & (lane < ones + 3), 1.0, 0.0).astype(BF)
+    table[BOTH] = jnp.zeros((ROWS, M), BF)
     for copy in copies:
         copy.wait()
 
@@ -305,58 +378,45 @@
                 row = n * LD + at_row if at_row < LD else ALL + n * BX + at_row - LD
                 low[row], low[row + 1], high[row], high[row + 1] = ready[i]
 
-    def gather(sources, classes, row, mats, width, shift):
+    def gather(source, kind, mats, width):
         total = jnp.zeros((R, K), F32)
         for g in range(width // 4):
-            s = [sources[row, 4 * g + i] - shift for i in range(4)]
+            s = [source(4 * g + i) for i in range(4)]
             vec = jnp.concatenate([low[s[0]] + high[s[1]], low[s[2]] + high[s[3]]], axis=1)
-            mat = jnp.concatenate([mats[classes[row, 4 * g + i]] for i in range(4)], axis=0)
+            mat = jnp.concatenate([mats[kind(4 * g + i)] for i in range(4)], axis=0)
             total = total + dot(vec, mat)
         return total
 
     def couple(it, _):
         rows = [it * 8 + u for u in range(8)]
-        got = [gather(leaf_sources, leaf_classes, row, matrices, ADM, (me - 1) * LD) for row in rows]
+        got = [
+            gather(
+                lambda a: leaf_sources[a, row] - (me - 1) * LD, lambda a: leaf_classes[a, row], matrices, ADM
+            )
+            for row in rows
+        ]
         for row, value in zip(rows, got):
             leaf_field[row] = value
         return 0
 
     lax.fori_loop(0, LD // 8, couple, 0)
-    got = [gather(box_sources, box_classes, box, box_matrices, ADMB, (me - 1) * BX - ALL) for box in range(BX)]
+    got = [
+        gather(
+            lambda a: box_sources[box, a] - (me - 1) * BX + ALL, lambda a: box_classes[box, a], box_matrices, ADMB
+        )
+        for box in range(BX)
+    ]
     for box in range(BX):
         box_field[box] = got[box]
 
-    expand = [expansion(i) for i in range(8)]
-    for o in range(ALL // 8):
-        rows = jnp.concatenate([table[8 * o + i, R:ROWS, :] for i in range(8)], axis=0)
-        spread = [dot(rows, expand[i]).astype(BF) for i in range(8)]
-        for i in range(8):
-            feats[8 * o + i] = spread[i]
-    pad = jnp.zeros((M - FX, M), BF)
-
-    def near(it, _):
-        t, kernels, weights = [], [], []
-        for u in range(UNROLL):
-            place_of = (it * UNROLL + u) * 2
-            one, two = slots[place_of], slots[place_of + 1]
-            s0, s1 = one & 255, two & 255
-            t.append(one >> 8)
-            rows = jnp.concatenate([feats[s0], feats[s1]], axis=0)
-            square = dot(rows, jnp.concatenate([target[jnp.minimum(t[u], LD - 1)], pad], axis=0))
-            kernels.append(lax.rsqrt(square).astype(BF))
-            weights.append(jnp.concatenate([table[s0, 0:R, :], table[s1, 0:R, :]], axis=1))
-        terms = [dot(weights[u], kernels[u]) for u in range(UNROLL)]
-        for u in range(UNROLL):
-            acc[t[u]] += terms[u]
-        return 0
-
-    lax.fori_loop(0, (at // 2 + UNROLL - 1) // UNROLL, near, 0)
-
-
-def fields(indices, place, low_field, down, coupling, target, matrices, box_matrices, sents):
+    spread_features(table, feats, BOTH)
+    near_loop(steps, slots, table, feats, target, acc)
+
+
+def fields(indices, place, low_field, down, coupling, near_part, target, matrices, box_matrices, sents):
     return pl.pallas_call(
         fields_body,
-        in_specs=[SMEM] * 7 + [VMEM] * 3 + [ANY] * 6,
+        in_specs=[SMEM] * 7 + [VMEM] * 3 + [ANY] * 7,
         out_specs=[VMEM] * 5,
         out_shape=[
             sds((LD + 1, R, M), F32),
@@ -366,9 +426,9 @@
             sds((4, 2, 2, K, K), BF),
         ],
         scratch_shapes=[
-            pltpu.VMEM((ALL + 1, ROWS, M), BF),
+            pltpu.VMEM((BOTH + 1, ROWS, M), BF),
             pltpu.VMEM((3 * (SENT - LD), ROWS, M), BF),
-            pltpu.VMEM((ALL + 1, M, M), BF),
+            pltpu.VMEM((BOTH + 1, M, M), BF),
             pltpu.VMEM((LD, FX, M), BF),
             pltpu.VMEM((matrices.shape[0], K, K), BF),
             pltpu.VMEM((matrices.shape[0], K, K), BF),
@@ -380,7 +440,7 @@
         compiler_params=params(),
         cost_estimate=pl.CostEstimate(flops=8 << 30, bytes_accessed=4 << 20, transcendentals=8 << 20),
         name="near_and_coupled_fields",
-    )(*indices, place, low_field, down, coupling, target, matrices, box_matrices, *sents)
+    )(*indices, place, low_field, down, coupling, near_part, target, matrices, box_matrices, *sents)
 
 
 def final_body(place, nodes, up, base, tip, parents, leaf_field_in, box_field, box_down, leaf_down_in, basis_in, near_in, out, boxes, held, leaf_field, leaf_down, basis, near_part, sems):
@@ -481,16 +541,18 @@
     low_groups = [[b * LOW + i for i in range(LOW)] for b in range(blocks)]
     high_groups = [[b * LOW + i for b in range(blocks)] for i in range(LOW)]
     low_nodes = gather_groups(ascent, low_groups)
+    near_part, sent = near_own(near_leaves, near_count, place, target, sent)
     sent_left, sent_right = exchange(sent)
     top, low_field = low_tree(place, low_nodes, top_up, top_coupling, blocks)
     high_nodes = gather_groups(top, high_groups)
 
     near_part, leaf_field, box_field, base, tip = fields(
-        (near_leaves, near_count, leaf_sources, leaf_classes, box_sources, box_classes),
+        (near_leaves, near_count, leaf_sources.T, leaf_classes.T, box_sources, box_classes),
         place,
         low_field,
         top_down,
         top_coupling,
+        near_part,
         target,
         leaf_coupling,
         box_coupling,

time: 91.7 us -> 85.8 us (0.936)
  the two profiles are of different devices: /device:TPU:7 before, /device:TPU:32 now
where the time goes in v5:
time: 85.8 us; the launch traced here: 85.3 us
  Pallas kernels  36.5 us (43%)
  starting transfers between devices  25.6 us (30%)
  blocking collectives  20.4 us (24%)
  waiting for transfers between devices  2.17 us (3%)
    all_to_all x1, blocking collectives, gather_groups(): lax.all_to_all(copies, AXES, 0, 0, axis_index_groups=groups, tiled=True)  20.4 us
    all_to_all x1, starting transfers between devices, gather_groups(): lax.all_to_all(copies, AXES, 0, 0, axis_index_groups=groups, tiled=True)  17.5 us
    pallas_call x1, Pallas kernels, fields(): pl.pallas_call(fields_body, in_specs=[SMEM] * 7 + [VMEM] * 3 + [ANY] * 7,...  16.2 us
    pallas_call x1, Pallas kernels, near_own(): pl.pallas_call(own_body, in_specs=[SMEM] * 3 + [ANY] * 2, out_specs=[VMEM...  8.23 us
    ppermute x1, starting transfers between devices, exchange(): right = lax.ppermute(x, AXES, [(i + 1, i) for i in range(count - 1)])  6.1 us
    pallas_call x1, Pallas kernels, finish(): pl.pallas_call(final_body, in_specs=[SMEM] + [VMEM] * 4 + [SMEM, ANY, VME...  5.3 us
    pallas_call x1, Pallas kernels, first(): pl.pallas_call(first_body, in_specs=[HBM] * 5 + [SMEM], out_specs=[VMEM]...  4.01 us
    pallas_call x1, Pallas kernels, low_tree(): pl.pallas_call(low_body, in_specs=[SMEM, VMEM, VMEM, VMEM], out_specs=[VM...  2.76 us
  transfers between devices with their start and end apart: 3, of which 1 were waited for; matrix products, arithmetic and copies ran while one was open for 0% of the time, Pallas kernels for 22%

profile of v5, /device:TPU:32, one launch (start us, length us, event | category | flops | bytes accessed | tf_op | source)
XLA Modules:
  0.0 85.3 jit_solution(6163143517417953394)
XLA Ops:
  0.0 4.0 %points_to_group.1 = (bf16[36,80,128]{2,1,0:T(8,128)(2,1)}, bf16[24,32,128]{2,1,0:T(8,128)(2,1)}, bf16[32,32,128]{2,1,0:T(8,128)(2,1)}) custom-call(bf16[64,3072]{1,0:T(8,128)(2,1)} %charges_in.1, f32[3,3072]{1,0:T(4,128)} %points_in.1, bf16[64,3072]{1,0:T(8,128)(2,1)} %basis_in.3, bf16[24,64,64]{2,1,0:T(8,128)(2,1)} %leaf_up_in.1, ...), custom_call_target="tpu_custom_call" | custom-call | tf_op jit(solution)/shard_map/points_to_group/pallas_call | solution.py:157
  4.0 0.0 copy-start.1
  4.0 8.2 %near_own.1 = (f32[25,64,128]{2,1,0:T(8,128)}, bf16[36,80,128]{2,1,0:T(8,128)(2,1)}) custom-call(s32[24,27]{1,0:T(8,128)} %near_leaves.3, s32[24]{0:T(128)} %near_count.3, s32[1]{0:T(128)} %bitcast.place, bf16[24,32,128]{2,1,0:T(8,128)(2,1)} %get-tuple-element.20.target_in, bf16[36,80,128]{2,1,0:T(8,128)(2,1)} %get-tuple-element.21.sent), custom_call_target="tpu_custom_call", output_to_operand_aliasing={{1}: (4, {})} | custom-call | flops 2147483648 | bytes 2097152 | tf_op jit(solution)/shard_map/near_own/pallas_call | solution.py:307
  12.3 6.1 %collective-permute-start.1 = (bf16[36,80,128]{2,1,0:T(8,128)(2,1)}, bf16[36,80,128]{2,1,0:T(8,128)(2,1)}, u32[]{:S(2)}, u32[]{:S(2)}) collective-permute-start(bf16[36,80,128]{2,1,0:T(8,128)(2,1)} %get-tuple-element.23.mine), channel_id=1, source_target_pairs={{1,0},{2,1},{3,2},{4,3},{5,4},{6,5},{7,6},{8,7},{9,8},{10,9},{11,1... | collective-permute-start | bytes 2211848 | tf_op jit(solution)/shard_map/ppermute | solution.py:505
  18.4 1.9 %collective-permute-start = (bf16[36,80,128]{2,1,0:T(8,128)(2,1)}, bf16[36,80,128]{2,1,0:T(8,128)(2,1)}, u32[]{:S(2)}, u32[]{:S(2)}) collective-permute-start(bf16[36,80,128]{2,1,0:T(8,128)(2,1)} %get-tuple-element.23.mine), channel_id=1, source_target_pairs={{0,1},{1,2},{2,3},{3,4},{4,5},{5,6},{6,7},{7,8},{8,9},{9,10},{10,1... | collective-permute-start | bytes 2211848 | tf_op jit(solution)/shard_map/ppermute | solution.py:504
  20.3 0.0 copy-done.1
  20.3 20.4 %all_to_all.10.nodes = bf16[32,32,128]{2,1,0:T(8,128)(2,1)} all-to-all(bf16[32,32,128]{2,1,0:T(8,128)(2,1)S(1)} %copy-done.1), channel_id=1, replica_groups={{0,1,2,3,4,5,6,7,8,9,10,11,12,13,14,15,16,17,18,19,20,21,22,23,24,25,26..., dimensions={0} | all-to-all | bytes 524288 | tf_op jit(solution)/shard_map/all_to_all | solution.py:510
  40.7 2.8 %coarse_low.1 = (bf16[16,64,128]{2,1,0:T(8,128)(2,1)}, f32[4,64,64]{2,1,0:T(8,128)}) custom-call(s32[1]{0:T(128)} %bitcast.place, bf16[32,32,128]{2,1,0:T(8,128)(2,1)} %all_to_all.10.nodes, bf16[8,2,64,64]{3,2,1,0:T(8,128)(2,1)} %up.3, bf16[8,2,64,64]{3,2,1,0:T(8,128)(2,1)} %coupling.3), custom_call_target="tpu_custom_call" | custom-call | tf_op jit(solution)/shard_map/coarse_low/pallas_call | solution.py:223
  43.4 17.5 %all-to-all-start.1 = ((bf16[16,64,128]{2,1,0:T(8,128)(2,1)}), bf16[16,64,128]{2,1,0:T(8,128)(2,1)S(1)}, u32[]{:S(2)}, u32[]{:S(2)}) async-start(bf16[16,64,128]{2,1,0:T(8,128)(2,1)} %get-tuple-element.18), calls=%async_computation.1 | async-start | bytes 524288 | tf_op jit(solution)/shard_map/all_to_all | solution.py:510
  61.0 0.0 collective-permute-done.1.right
  61.0 0.0 collective-permute-done.left
  61.0 16.2 %near_and_coupled_fields.1 = (f32[25,64,128]{2,1,0:T(8,128)}, f32[24,64,64]{2,1,0:T(8,128)}, f32[6,64,64]{2,1,0:T(8,128)}, f32[64,64]{1,0:T(8,128)}, bf16[4,2,2,64,64]{4,3,2,1,0:T(8,128)(2,1)}) custom-call(s32[24,27]{1,0:T(8,128)} %near_leaves.3, s32[24]{0:T(128)} %near_count.3, s32[16,24]{1,0:T(8,128)} %bitcast.6, s32[16,24]{1,0:T(8,128)} %bitcast.7, ...), custom_call_target="tpu_custom_call" | custom-call | flops 8589934592 | bytes 4194304 | tf_op jit(solution)/shard_map/near_and_coupled_fields/pallas_call | solution.py:417
  77.1 2.2 %all-to-all-done.1.nodes = bf16[16,64,128]{2,1,0:T(8,128)(2,1)S(1)} async-done(((bf16[16,64,128]{2,1,0:T(8,128)(2,1)}), bf16[16,64,128]{2,1,0:T(8,128)(2,1)S(1)}, u32[]{:S(2)}, u32[]{:S(2)}) %all-to-all-start.1) | async-done | bytes 262176 | tf_op jit(solution)/shard_map/all_to_all | solution.py:510
  79.3 0.0 copy-start
  79.3 0.7 copy-done
  80.0 5.3 %group_to_points.1 = f32[64,3072]{1,0:T(8,128)} custom-call(s32[1]{0:T(128)} %bitcast.place, bf16[16,64,128]{2,1,0:T(8,128)(2,1)} %copy-done, bf16[8,2,64,64]{3,2,1,0:T(8,128)(2,1)} %up.3, f32[64,64]{1,0:T(8,128)} %get-tuple-element.24.base, bf16[4,2,2,64,64]{4,3,2,1,0:T(8,128)(2,1)} %get-tuple-element.25.tip, s32[24]{0:T(128)} %bitcast.5, ...), custom_call_target="tpu_custom_call" | custom-call | tf_op jit(solution)/shard_map/group_to_points/pallas_call | solution.py:483
Async XLA Ops:
  4.0 16.3 %copy-start.1 = (bf16[32,32,128]{2,1,0:T(8,128)(2,1)S(1)}, bf16[32,32,128]{2,1,0:T(8,128)(2,1)}, u32[]{:S(2)}) copy-start(bf16[32,32,128]{2,1,0:T(8,128)(2,1)} %get-tuple-element.17) | copy-start | bytes 786436
  12.3 48.7 %collective-permute-start.1 = (bf16[36,80,128]{2,1,0:T(8,128)(2,1)}, bf16[36,80,128]{2,1,0:T(8,128)(2,1)}, u32[]{:S(2)}, u32[]{:S(2)}) collective-permute-start(bf16[36,80,128]{2,1,0:T(8,128)(2,1)} %get-tuple-element.23.mine), channel_id=1, source_target_pairs={{1,0},{2,1},{3,2},{4,3},{5,4},{6,5},{7,6},{8,7},{9,8},{10,9},{11,1... | collective-permute-start | bytes 2211848 | tf_op jit(solution)/shard_map/ppermute | solution.py:505
  18.4 42.6 %collective-permute-start = (bf16[36,80,128]{2,1,0:T(8,128)(2,1)}, bf16[36,80,128]{2,1,0:T(8,128)(2,1)}, u32[]{:S(2)}, u32[]{:S(2)}) collective-permute-start(bf16[36,80,128]{2,1,0:T(8,128)(2,1)} %get-tuple-element.23.mine), channel_id=1, source_target_pairs={{0,1},{1,2},{2,3},{3,4},{4,5},{5,6},{6,7},{7,8},{8,9},{9,10},{10,1... | collective-permute-start | bytes 2211848 | tf_op jit(solution)/shard_map/ppermute | solution.py:504
  43.4 35.9 %all-to-all-start.1 = ((bf16[16,64,128]{2,1,0:T(8,128)(2,1)}), bf16[16,64,128]{2,1,0:T(8,128)(2,1)S(1)}, u32[]{:S(2)}, u32[]{:S(2)}) async-start(bf16[16,64,128]{2,1,0:T(8,128)(2,1)} %get-tuple-element.18), calls=%async_computation.1 | async-start | bytes 524288 | tf_op jit(solution)/shard_map/all_to_all | solution.py:510
  79.3 0.7 copy-start

commit v6 on v5

--- a/solution.py
+++ b/solution.py
@@ -196,10 +196,34 @@
     return (mul(left, twice(matrices[0])) + mul(right, twice(matrices[1]))).reshape(count, R // 2, 2 * K)
 
 
-def low_body(place, nodes, up, coupling, top, field, held):
+def list_slots(code, lists, at, targets):
+    for t in targets:
+        for part in range(0, NEAR, 9):
+            row = [code[t, part + s] for s in range(9)]
+            for x in row:
+                for n in range(2):
+                    lists[n][at[n]] = x
+                    at[n] = at[n] + ((x >> (16 + n)) & 1)
+        for n in range(2):
+            lists[n][at[n]] = t << 8 | (n + 1) * LD
+            at[n] = (at[n] + 1) & -2
+
+
+def low_body(place, code, nodes_in, up_in, coupling_in, _, top, field, own, halo, sizes, __, nodes, up, coupling, held, sems):
+    moves = ((nodes_in, nodes), (up_in.at[pl.ds(0, 4)], up), (coupling_in.at[pl.ds(0, 4)], coupling))
+    copies = load([pltpu.make_async_copy(a, b, sems.at[n]) for n, (a, b) in enumerate(moves)])
+    lists, at = (own, halo), [jnp.int32(0)] * 2
+    list_slots(code, lists, at, range(LD // 2))
+    for copy in copies:
+        copy.wait()
     levels = [nodes[...]]
     for h in range(4):
         levels.append(raise_nodes(levels[h], (up[h, 0], up[h, 1])))
+    list_slots(code, lists, at, range(LD // 2, LD))
+    for n in range(2):
+        for i in range(2 * UNROLL):
+            lists[n][at[n] + i] = LD << 8 | (n + 1) * LD
+        sizes[n] = (at[n] // 2 + UNROLL - 1) // UNROLL
     packed = levels[4].astype(BF).reshape(R, 2 * K)
     for i in range(top.shape[0]):
         top[i] = packed
@@ -219,42 +243,35 @@
         field[h] = out[h]
 
 
-def low_tree(place, nodes, up, coupling, blocks):
+def low_tree(place, code, nodes, up, coupling, sent, blocks):
     return pl.pallas_call(
         low_body,
-        in_specs=[SMEM, VMEM, VMEM, VMEM],
-        out_specs=[VMEM, VMEM],
-        out_shape=[sds((blocks, R, 2 * K), BF), sds((4, R, K), F32)],
-        scratch_shapes=[pltpu.VMEM((2 * LOW, R // 2, 2 * K), F32)],
-        compiler_params=params(63.5),
+        in_specs=[SMEM] * 2 + [ANY] * 4,
+        out_specs=[VMEM, VMEM, SMEM, SMEM, SMEM, ANY],
+        out_shape=[
+            sds((blocks, R, 2 * K), BF),
+            sds((4, R, K), F32),
+            sds((SLOTS,), jnp.int32),
+            sds((SLOTS,), jnp.int32),
+            sds((2,), jnp.int32),
+            sds(sent.shape, sent.dtype),
+        ],
+        input_output_aliases={5: 5},
+        scratch_shapes=[
+            pltpu.VMEM((LOW, R // 2, 2 * K), BF),
+            pltpu.VMEM((4, 2, K, K), BF),
+            pltpu.VMEM((4, 2, K, K), BF),
+            pltpu.VMEM((2 * LOW, R // 2, 2 * K), F32),
+            pltpu.SemaphoreType.DMA((3,)),
+        ],
+        compiler_params=params(),
         name="coarse_low",
-    )(place, nodes, up, coupling)
+    )(place, code, nodes, up, coupling, sent)
 
 
 def split2(x):
     hi = x.astype(BF)
     return hi, (x - hi.astype(F32)).astype(BF)
-
-
-def used_slots(near_leaves, near_count, slots, me, halo):
-    null = BOTH if halo else LD
-    at = jnp.int32(0)
-    for t in range(LD):
-        used = near_count[t]
-        for part in range(0, NEAR, 9):
-            row = [near_leaves[t, part + s] - me * LD for s in range(9)]
-            for s, x in enumerate(row):
-                mine = jnp.logical_and(x >= 0, x < LD)
-                wanted = jnp.logical_not(mine) if halo else mine
-                if halo:
-                    x = jnp.where(x < 0, x + LD, x)
-                slots[at] = x + (t << 8)
-                at = at + jnp.where(jnp.logical_and(wanted, part + s < used), 1, 0)
-        slots[at] = t << 8 | null
-        at = (at + 1) & -2
-    for i in range(2 * UNROLL):
-        slots[at + i] = LD << 8 | null
-    return (at // 2 + UNROLL - 1) // UNROLL
 
 
 def spread_features(table, feats, count):
@@ -278,7 +295,7 @@
             place_of = (it * UNROLL + u) * 2
             one, two = slots[place_of], slots[place_of + 1]
             s0, s1 = one & 255, two & 255
-            t.append(one >> 8)
+            t.append((one >> 8) & 255)
             rows = jnp.concatenate([feats[s0], feats[s1]], axis=0)
             square = dot(rows, jnp.concatenate([target[jnp.minimum(t[u], LD - 1)], pad], axis=0))
             kernels.append(lax.rsqrt(square).astype(BF))
@@ -291,39 +308,36 @@
     lax.fori_loop(0, steps, near, 0)
 
 
-def own_body(near_leaves, near_count, place, target_in, sent, acc, _, table, feats, target, slots, sems):
+def own_body(sizes, slots, target_in, sent, acc, table, feats, target, sems):
     moves = ((sent.at[pl.ds(0, LD)], table.at[pl.ds(0, LD)]), (target_in, target))
     copies = load([pltpu.make_async_copy(a, b, sems.at[n]) for n, (a, b) in enumerate(moves)])
-    steps = used_slots(near_leaves, near_count, slots, place[0], False)
     acc[...] = jnp.zeros(acc.shape, F32)
     table[LD] = jnp.zeros((ROWS, M), BF)
     for copy in copies:
         copy.wait()
     spread_features(table, feats, LD)
-    near_loop(steps, slots, table, feats, target, acc)
-
-
-def near_own(near_leaves, near_count, place, target, sent):
+    near_loop(sizes[0], slots, table, feats, target, acc)
+
+
+def near_own(sizes, slots, target, sent):
     return pl.pallas_call(
         own_body,
-        in_specs=[SMEM] * 3 + [ANY] * 2,
-        out_specs=[VMEM, ANY],
-        out_shape=[sds((LD + 1, R, M), F32), sds(sent.shape, sent.dtype)],
-        input_output_aliases={4: 1},
+        in_specs=[SMEM] * 2 + [ANY] * 2,
+        out_specs=VMEM,
+        out_shape=sds((LD + 1, R, M), F32),
         scratch_shapes=[
             pltpu.VMEM((LD + 1, ROWS, M), BF),
             pltpu.VMEM((LD + 1, M, M), BF),
             pltpu.VMEM((LD, FX, M), BF),
-            pltpu.SMEM((SLOTS,), jnp.int32),
             pltpu.SemaphoreType.DMA((2,)),
         ],
-        compiler_params=params(),
+        compiler_params=params(63.5),
         cost_estimate=pl.CostEstimate(flops=2 << 30, bytes_accessed=2 << 20, transcendentals=4 << 20),
         name="near_own",
-    )(near_leaves, near_count, place, target, sent)
-
-
-def fields_body(near_leaves, near_count, leaf_sources, leaf_classes, box_sources, box_classes, place, low_field, down, coupling, near_in, target_in, matrices_in, box_matrices_in, left, mine, right, acc, leaf_field, box_field, base, tip, table, coefs, feats, target, matrices, box_matrices, low, high, slots, sems):
+    )(sizes, slots, target, sent)
+
+
+def fields_body(sizes, slots, leaf_sources, leaf_classes, box_sources, box_classes, place, low_field, down, coupling, near_in, target_in, matrices_in, box_matrices_in, left, mine, right, acc, leaf_field, box_field, base, tip, table, coefs, feats, target, matrices, box_matrices, low, high, sems):
     blocks = SENT - LD
     sources = (left, mine, right)
     moves = [(left.at[pl.ds(0, LD)], table.at[pl.ds(0, LD)]), (right.at[pl.ds(0, LD)], table.at[pl.ds(LD, LD)])]
@@ -331,8 +345,6 @@
     moves += [(target_in, target), (matrices_in, matrices), (box_matrices_in, box_matrices), (near_in, acc)]
     copies = load([pltpu.make_async_copy(a, b, sems.at[n]) for n, (a, b) in enumerate(moves)])
     me = place[0]
-    steps = used_slots(near_leaves, near_count, slots, me, True)
-
     total = low_field[3]
     chain = down[3, (me >> 3) & 1].astype(F32)
     for h in range(2, -1, -1):
@@ -410,7 +422,7 @@
         box_field[box] = got[box]
 
     spread_features(table, feats, BOTH)
-    near_loop(steps, slots, table, feats, target, acc)
+    near_loop(sizes[1], slots, table, feats, target, acc)
 
 
 def fields(indices, place, low_field, down, coupling, near_part, target, matrices, box_matrices, sents):
@@ -434,7 +446,6 @@
             pltpu.VMEM((matrices.shape[0], K, K), BF),
             pltpu.VMEM((6 * PAIRS, R, 2 * K), BF),
             pltpu.VMEM((6 * PAIRS, R, 2 * K), BF),
-            pltpu.SMEM((SLOTS,), jnp.int32),
             pltpu.SemaphoreType.DMA((9,)),
         ],
         compiler_params=params(),
@@ -443,12 +454,16 @@
     )(*indices, place, low_field, down, coupling, near_part, target, matrices, box_matrices, *sents)
 
 
-def final_body(place, nodes, up, base, tip, parents, leaf_field_in, box_field, box_down, leaf_down_in, basis_in, near_in, out, boxes, held, leaf_field, leaf_down, basis, near_part, sems):
-    moves = ((leaf_field_in, leaf_field), (leaf_down_in, leaf_down), (basis_in, basis), (near_in, near_part))
+def final_body(place, nodes_in, up_in, base_in, tip_in, parents, leaf_field_in, box_field_in, box_down_in, leaf_down_in, basis_in, near_in, out, boxes, held, nodes, up, base, tip, box_field, box_down, leaf_field, leaf_down, basis, near_part, sems):
+    moves = ((nodes_in, nodes), (up_in.at[pl.ds(4, 3)], up), (base_in, base), (tip_in, tip))
+    moves += ((box_field_in, box_field), (box_down_in, box_down), (leaf_down_in, leaf_down))
+    moves += ((leaf_field_in, leaf_field), (basis_in, basis), (near_in, near_part))
     copies = load([pltpu.make_async_copy(a, b, sems.at[n]) for n, (a, b) in enumerate(moves)])
+    for copy in copies[:4]:
+        copy.wait()
     levels = [nodes[...].reshape(LOW, R // 2, 2 * K)]
     for h in range(3):
-        levels.append(raise_nodes(levels[h], (up[4 + h, 0], up[4 + h, 1])))
+        levels.append(raise_nodes(levels[h], (up[h, 0], up[h, 1])))
     start = 0
     for h in range(4):
         held[start : start + (LOW >> h)] = levels[h].astype(F32)
@@ -461,7 +476,7 @@
             hi, lo = split2(unpack(held[((me >> h) ^ (2 + i)) + start]))
             total = total + (dot(hi, tip[h, i, 0]) + dot(hi, tip[h, i, 1]) + dot(lo, tip[h, i, 0]))
         start += LOW >> h
-    for copy in copies:
+    for copy in copies[4:]:
         copy.wait()
     group = total.astype(BF)
     got = [(box_field[box] + dot(group, box_down[box])).astype(BF) for box in range(BX)]
@@ -482,17 +497,23 @@
 def finish(place, nodes, up, base, tip, parents, leaf_field, box_field, box_down, leaf_down, basis, near_part):
     return pl.pallas_call(
         final_body,
-        in_specs=[SMEM] + [VMEM] * 4 + [SMEM, ANY, VMEM, VMEM] + [ANY] * 3,
+        in_specs=[SMEM] + [ANY] * 4 + [SMEM] + [ANY] * 6,
         out_specs=VMEM,
         out_shape=sds((R, LD * M), F32),
         scratch_shapes=[
             pltpu.VMEM((BX, R, K), BF),
             pltpu.VMEM((2 * LOW, R // 2, 2 * K), F32),
+            pltpu.VMEM(nodes.shape, BF),
+            pltpu.VMEM((3, 2, K, K), BF),
+            pltpu.VMEM((R, K), F32),
+            pltpu.VMEM((4, 2, 2, K, K), BF),
+            pltpu.VMEM((BX, R, K), F32),
+            pltpu.VMEM((BX, K, K), BF),
             pltpu.VMEM((LD, R, K), F32),
             pltpu.VMEM((LD, K, K), BF),
             pltpu.VMEM((K, LD * M), BF),
             pltpu.VMEM((LD + 1, R, M), F32),
-            pltpu.SemaphoreType.DMA((4,)),
+            pltpu.SemaphoreType.DMA((10,)),
         ],
         compiler_params=params(),
         name="group_to_points",
@@ -540,14 +561,23 @@
     blocks = lax.axis_size(AXES) // LOW
     low_groups = [[b * LOW + i for i in range(LOW)] for b in range(blocks)]
     high_groups = [[b * LOW + i for b in range(blocks)] for i in range(LOW)]
+    rel = near_leaves - device * LD
+    mine = (rel >= 0) & (rel < LD)
+    used = jnp.arange(NEAR, dtype=jnp.int32)[None, :] < near_count[:, None]
+    row = jnp.where(rel < 0, rel + LD, rel)
+    leaf_ids = jnp.arange(LD, dtype=jnp.int32)[:, None]
+    code = row | leaf_ids << 8 | jnp.where(used, jnp.where(mine, 1, 2), 0) << 16
+
     low_nodes = gather_groups(ascent, low_groups)
-    near_part, sent = near_own(near_leaves, near_count, place, target, sent)
+    top, low_field, own, halo, sizes, sent = low_tree(
+        place, code, low_nodes, top_up, top_coupling, sent, blocks
+    )
+    high_nodes = gather_groups(top, high_groups)
     sent_left, sent_right = exchange(sent)
-    top, low_field = low_tree(place, low_nodes, top_up, top_coupling, blocks)
-    high_nodes = gather_groups(top, high_groups)
+    near_part = near_own(sizes, own, target, sent)
 
     near_part, leaf_field, box_field, base, tip = fields(
-        (near_leaves, near_count, leaf_sources.T, leaf_classes.T, box_sources, box_classes),
+        (sizes, halo, leaf_sources.T, leaf_classes.T, box_sources, box_classes),
         place,
         low_field,
         top_down,

time: 85.8 us -> 72 us (0.84)
  the two profiles are of different devices: /device:TPU:32 before, /device:TPU:88 now
where the time goes in v6:
time: 72 us; the launch traced here: 71.4 us
  Pallas kernels  33.6 us (47%)
  starting transfers between devices  28.9 us (40%)
  waiting for transfers between devices  6.04 us (8%)
  local copies, waits for them, and re-layouts  2.1 us (3%)
    all_to_all x2, starting transfers between devices, gather_groups(): lax.all_to_all(copies, AXES, 0, 0, axis_index_groups=groups, tiled=True)  22.1 us
    pallas_call x1, Pallas kernels, fields(): pl.pallas_call(fields_body, in_specs=[SMEM] * 7 + [VMEM] * 3 + [ANY] * 7,...  13.9 us
    pallas_call x1, Pallas kernels, near_own(): pl.pallas_call(own_body, in_specs=[SMEM] * 2 + [ANY] * 2, out_specs=VMEM,...  6.58 us
    all_to_all x2, waiting for transfers between devices, gather_groups(): lax.all_to_all(copies, AXES, 0, 0, axis_index_groups=groups, tiled=True)  6.03 us
    pallas_call x1, Pallas kernels, finish(): pl.pallas_call(final_body, in_specs=[SMEM] + [ANY] * 4 + [SMEM] + [ANY] *...  4.64 us
    ppermute x1, starting transfers between devices, exchange(): left = lax.ppermute(x, AXES, [(i, i + 1) for i in range(count - 1)])  4.52 us
    pallas_call x1, Pallas kernels, low_tree(): pl.pallas_call(low_body, in_specs=[SMEM] * 2 + [ANY] * 4, out_specs=[VMEM...  4.42 us
    pallas_call x1, Pallas kernels, first(): pl.pallas_call(first_body, in_specs=[HBM] * 5 + [SMEM], out_specs=[VMEM]...  4.01 us
  transfers between devices with their start and end apart: 4, of which 1 were waited for; matrix products, arithmetic and copies ran while one was open for 1% of the time, Pallas kernels for 29%

profile of v6, /device:TPU:88, one launch (start us, length us, event | category | flops | bytes accessed | tf_op | source)
XLA Modules:
  0.0 71.4 jit_solution(5041815200098137221)
XLA Ops:
  0.0 4.0 %points_to_group.1 = (bf16[36,80,128]{2,1,0:T(8,128)(2,1)}, bf16[24,32,128]{2,1,0:T(8,128)(2,1)}, bf16[32,32,128]{2,1,0:T(8,128)(2,1)}) custom-call(bf16[64,3072]{1,0:T(8,128)(2,1)} %charges_in.1, f32[3,3072]{1,0:T(4,128)} %points_in.1, bf16[64,3072]{1,0:T(8,128)(2,1)} %basis_in.3, bf16[24,64,64]{2,1,0:T(8,128)(2,1)} %leaf_up_in.1, ...), custom_call_target="tpu_custom_call" | custom-call | tf_op jit(solution)/shard_map/points_to_group/pallas_call | solution.py:157
  4.0 7.3 %all-to-all-start = ((bf16[32,32,128]{2,1,0:T(8,128)(2,1)}), bf16[32,32,128]{2,1,0:T(8,128)(2,1)S(1)}, u32[]{:S(2)}, u32[]{:S(2)}) async-start(bf16[32,32,128]{2,1,0:T(8,128)(2,1)} %get-tuple-element.19), calls=%async_computation | async-start | bytes 524288 | tf_op jit(solution)/shard_map/all_to_all | solution.py:531
  11.3 0.0 copy-start.2
  11.4 0.0 copy-start.3
  11.4 0.7 copy-done.2
  12.1 0.0 copy-done.3
  12.1 0.7 fusion.1.code
  12.7 6.0 %all-to-all-done.nodes_in = bf16[32,32,128]{2,1,0:T(8,128)(2,1)S(1)} async-done(((bf16[32,32,128]{2,1,0:T(8,128)(2,1)}), bf16[32,32,128]{2,1,0:T(8,128)(2,1)S(1)}, u32[]{:S(2)}, u32[]{:S(2)}) %all-to-all-start) | async-done | bytes 262176 | tf_op jit(solution)/shard_map/all_to_all | solution.py:531
  18.8 0.0 copy-start.1
  18.8 0.7 copy-done.1
  19.5 4.4 %coarse_low.1 = (bf16[16,64,128]{2,1,0:T(8,128)(2,1)}, f32[4,64,64]{2,1,0:T(8,128)}, s32[736]{0:T(1024)}, s32[736]{0:T(1024)}, s32[2]{0:T(128)}, /*index=5*/bf16[36,80,128]{2,1,0:T(8,128)(2,1)}) custom-call(s32[1]{0:T(128)} %bitcast.place, s32[24,27]{1,0:T(8,128)} %fusion.1.code, bf16[32,32,128]{2,1,0:T(8,128)(2,1)} %copy-done.1, ...), custom_call_target="tpu_custom_call", output_to_operand_aliasing={{5}: (5, {})} | custom-call | tf_op jit(solution)/shard_map/coarse_low/pallas_call | solution.py:247
  23.9 2.3 %collective-permute-start.1 = (bf16[36,80,128]{2,1,0:T(8,128)(2,1)}, bf16[36,80,128]{2,1,0:T(8,128)(2,1)}, u32[]{:S(2)}, u32[]{:S(2)}) collective-permute-start(bf16[36,80,128]{2,1,0:T(8,128)(2,1)} %get-tuple-element.27.sent.mine), channel_id=1, source_target_pairs={{1,0},{2,1},{3,2},{4,3},{5,4},{6,5},{7,6},{8,7},{9,8},{10,9},{11,1... | collective-permute-start | bytes 2211848 | tf_op jit(solution)/shard_map/ppermute | solution.py:526
  26.2 4.5 %collective-permute-start = (bf16[36,80,128]{2,1,0:T(8,128)(2,1)}, bf16[36,80,128]{2,1,0:T(8,128)(2,1)}, u32[]{:S(2)}, u32[]{:S(2)}) collective-permute-start(bf16[36,80,128]{2,1,0:T(8,128)(2,1)} %get-tuple-element.27.sent.mine), channel_id=1, source_target_pairs={{0,1},{1,2},{2,3},{3,4},{4,5},{5,6},{6,7},{7,8},{8,9},{9,10},{10,1... | collective-permute-start | bytes 2211848 | tf_op jit(solution)/shard_map/ppermute | solution.py:525
  30.7 14.8 %all-to-all-start.1 = ((bf16[16,64,128]{2,1,0:T(8,128)(2,1)}), bf16[16,64,128]{2,1,0:T(8,128)(2,1)S(1)}, u32[]{:S(2)}, u32[]{:S(2)}) async-start(bf16[16,64,128]{2,1,0:T(8,128)(2,1)} %get-tuple-element.21), calls=%async_computation.1 | async-start | bytes 524288 | tf_op jit(solution)/shard_map/all_to_all | solution.py:531
  45.5 6.6 %near_own.1.near_in = f32[25,64,128]{2,1,0:T(8,128)} custom-call(s32[2]{0:T(128)} %get-tuple-element.22.sizes, s32[736]{0:T(1024)} %get-tuple-element.25.slots, bf16[24,32,128]{2,1,0:T(8,128)(2,1)} %get-tuple-element.26.target_in, bf16[36,80,128]{2,1,0:T(8,128)(2,1)} %get-tuple-element.27.sent.mine), custom_call_target="tpu_custom_call" | custom-call | flops 2147483648 | bytes 2097152 | tf_op jit(solution)/shard_map/near_own/pallas_call | solution.py:323
  52.1 0.0 collective-permute-done.1.right
  52.1 0.0 collective-permute-done.left
  52.1 13.9 %near_and_coupled_fields.1 = (f32[25,64,128]{2,1,0:T(8,128)}, f32[24,64,64]{2,1,0:T(8,128)}, f32[6,64,64]{2,1,0:T(8,128)}, f32[64,64]{1,0:T(8,128)}, bf16[4,2,2,64,64]{4,3,2,1,0:T(8,128)(2,1)}) custom-call(s32[2]{0:T(128)} %get-tuple-element.22.sizes, s32[736]{0:T(1024)} %get-tuple-element.23.slots, s32[16,24]{1,0:T(8,128)} %bitcast.6, s32[16,24]{1,0:T(8,128)} %bitcast.7, ...), custom_call_target="tpu_custom_call" | custom-call | flops 8589934592 | bytes 4194304 | tf_op jit(solution)/shard_map/near_and_coupled_fields/pallas_call | solution.py:429
  66.0 0.0 all-to-all-done.1.nodes_in
  66.0 0.0 copy-start
  66.0 0.7 copy-done
  66.8 4.6 %group_to_points.1 = f32[64,3072]{1,0:T(8,128)} custom-call(s32[1]{0:T(128)} %bitcast.place, bf16[16,64,128]{2,1,0:T(8,128)(2,1)} %copy-done, bf16[8,2,64,64]{3,2,1,0:T(8,128)(2,1)} %up_in.3, f32[64,64]{1,0:T(8,128)} %get-tuple-element.28.base_in, bf16[4,2,2,64,64]{4,3,2,1,0:T(8,128)(2,1)} %get-tuple-element.29.tip_in, s32[24]{0:T(128)} %bitcast.5, ...), custom_call_target="tpu_custom_call" | custom-call | tf_op jit(solution)/shard_map/group_to_points/pallas_call | solution.py:498
  (1 shorter events, 0.0 us)
Async XLA Ops:
  4.0 14.8 %all-to-all-start = ((bf16[32,32,128]{2,1,0:T(8,128)(2,1)}), bf16[32,32,128]{2,1,0:T(8,128)(2,1)S(1)}, u32[]{:S(2)}, u32[]{:S(2)}) async-start(bf16[32,32,128]{2,1,0:T(8,128)(2,1)} %get-tuple-element.19), calls=%async_computation | async-start | bytes 524288 | tf_op jit(solution)/shard_map/all_to_all | solution.py:531
  11.3 0.7 copy-start.2
  11.4 0.7 copy-start.3
  18.8 0.7 copy-start.1
  23.9 28.2 %collective-permute-start.1 = (bf16[36,80,128]{2,1,0:T(8,128)(2,1)}, bf16[36,80,128]{2,1,0:T(8,128)(2,1)}, u32[]{:S(2)}, u32[]{:S(2)}) collective-permute-start(bf16[36,80,128]{2,1,0:T(8,128)(2,1)} %get-tuple-element.27.sent.mine), channel_id=1, source_target_pairs={{1,0},{2,1},{3,2},{4,3},{5,4},{6,5},{7,6},{8,7},{9,8},{10,9},{11,1... | collective-permute-start | bytes 2211848 | tf_op jit(solution)/shard_map/ppermute | solution.py:526
  26.2 25.9 %collective-permute-start = (bf16[36,80,128]{2,1,0:T(8,128)(2,1)}, bf16[36,80,128]{2,1,0:T(8,128)(2,1)}, u32[]{:S(2)}, u32[]{:S(2)}) collective-permute-start(bf16[36,80,128]{2,1,0:T(8,128)(2,1)} %get-tuple-element.27.sent.mine), channel_id=1, source_target_pairs={{0,1},{1,2},{2,3},{3,4},{4,5},{5,6},{6,7},{7,8},{8,9},{9,10},{10,1... | collective-permute-start | bytes 2211848 | tf_op jit(solution)/shard_map/ppermute | solution.py:525
  30.7 35.3 %all-to-all-start.1 = ((bf16[16,64,128]{2,1,0:T(8,128)(2,1)}), bf16[16,64,128]{2,1,0:T(8,128)(2,1)S(1)}, u32[]{:S(2)}, u32[]{:S(2)}) async-start(bf16[16,64,128]{2,1,0:T(8,128)(2,1)} %get-tuple-element.21), calls=%async_computation.1 | async-start | bytes 524288 | tf_op jit(solution)/shard_map/all_to_all | solution.py:531
  66.0 0.7 %copy-start = (bf16[16,64,128]{2,1,0:T(8,128)(2,1)}, bf16[16,64,128]{2,1,0:T(8,128)(2,1)S(1)}, u32[]{:S(2)}) copy-start(bf16[16,64,128]{2,1,0:T(8,128)(2,1)S(1)} %all-to-all-done.1.nodes_in) | copy-start | bytes 786436
